TPU v7x, 256 devices: a whole 4x4x8 slice. The times are simulated.
256 devices in a mesh: table: 8 (over y, core), dp: 32 (over z, x).
Axes of the slice: x: 4, y: 4, z: 8, core: 2. Of those that a mesh axis runs over, the one named last changes fastest.
Arguments:
- hot_table: bfloat16 [512, 1024], replicated, may hold values from -6 to 6
- cold_table: bfloat16 [4096, 1024], P('table'), may hold values from -6 to 6
- w_in: bfloat16 [1024, 2048], replicated, may hold values from -0.1875 to 0.1875
- w_out: bfloat16 [512, 1024], replicated, may hold values from -0.25 to 0.25
- seq_lengths: int32 [256, 8], P(('table', 'dp')), may hold values from 1 to 256, 512 in all within a row
- event_hot: int32 [131072], P(('table', 'dp')), may hold values from 0 to 1
- event_index: int32 [131072], P(('table', 'dp')), may hold values from 0 to 511, as said below
- cold_requests: int32 [2048, 16], P(('table', 'dp')), may hold values from 0 to 511, as said below
- out_grad: bfloat16 [131072, 1024], P(('table', 'dp')), may hold values from -6 to 6
Outputs:
- layer_out: bfloat16 [131072, 1024], P(('table', 'dp'))
- hot_grad: float32 [512, 1024], P('dp')
- cold_grad: float32 [4096, 1024], P(('table', 'dp'))
Inputs may be any that keep to these rules, and one draw needn't show every extreme that they name: `event_index`: where event_hot is 1 the value is a row of hot_table, below 512; where it is 0 it is a slot of the event's device, below 128. `cold_requests`: the 16 entries of one row are distinct.
All inputs are finite; a program needn't handle non-finite values.
Results may differ from a plain program's by a relative error of at most 0.012.
Values may be sent and summed in bfloat16 or wider, within the bound.
No kernel may reach another device: no remote copies, remote signals or barrier semaphores. Data moves between devices by JAX's collectives and lax.ppermute only.
A program may use at most 128 MiB of HBM per device.

v0:
```python
import jax
import jax.numpy as jnp
from jax import lax
from jax.sharding import PartitionSpec as P

HEAD = 128


eps = 1e-06


def layer_norm(values):
    average = jnp.mean(values, axis=-1, keepdims=True)
    centered = values - average
    variance = jnp.mean(centered * centered, axis=-1, keepdims=True)
    return centered * lax.rsqrt(variance + eps)


def causal_scale(lengths, tokens):
    seq_ends = jnp.cumsum(lengths)
    position = lax.iota(jnp.int32, tokens)
    seq_of = jnp.sum((position[:, None] >= seq_ends[None, :]).astype(jnp.int32), axis=1)
    picks = seq_of[:, None] == lax.iota(jnp.int32, lengths.shape[0])[None, :]
    length_of = jnp.sum(jnp.where(picks, lengths[None, :], 0), axis=1).astype(jnp.float32)
    allowed = (seq_of[:, None] == seq_of[None, :]) & (position[:, None] >= position[None, :])
    return jnp.where(allowed, 1.0 / length_of[:, None], 0.0)


def layer_forward(row_vals, w_in, w_out, scale_rows):
    tokens = row_vals.shape[0]
    inner_width = w_out.shape[0]
    head_count = inner_width // HEAD
    normed = layer_norm(row_vals).astype(jnp.bfloat16)
    mixed = jax.nn.silu(jnp.dot(normed, w_in, preferred_element_type=jnp.float32)).astype(
        jnp.bfloat16
    )
    gate_vals = mixed[:, :inner_width].astype(jnp.float32)
    value_vals = mixed[:, inner_width : 2 * inner_width].reshape(tokens, head_count, HEAD)
    query_vals = mixed[:, 2 * inner_width : 3 * inner_width].reshape(tokens, head_count, HEAD)
    key_vals = mixed[:, 3 * inner_width :].reshape(tokens, head_count, HEAD)
    scores = jnp.einsum(
        "qhd,khd->hqk", query_vals, key_vals, preferred_element_type=jnp.float32
    ) * HEAD ** (-0.5)
    weights = (jax.nn.silu(scores) * scale_rows[None]).astype(jnp.bfloat16)
    attended = jnp.einsum("hqk,khd->qhd", weights, value_vals, preferred_element_type=jnp.float32)
    attended = attended.reshape(tokens, inner_width)
    merged = (layer_norm(attended) * gate_vals).astype(jnp.bfloat16)
    return jnp.dot(merged, w_out, preferred_element_type=jnp.float32) + row_vals


def on_device(
    hot_table, cold_table, w_in, w_out, seq_lengths, event_hot, event_index, cold_requests, out_grad
):
    table_count = lax.axis_size("table")
    cap_size = cold_requests.shape[1]
    slot_count = table_count * cap_size
    shard_rows = cold_table.shape[0]
    model_width = cold_table.shape[1]
    hot_rows = hot_table.shape[0]
    wanted = lax.all_to_all(cold_requests, "table", split_axis=0, concat_axis=0, tiled=True)
    all_rows = lax.all_gather(cold_table, "table", axis=0, tiled=True)
    owners = lax.iota(jnp.int32, table_count)[:, None] * shard_rows
    fetched = all_rows[(owners + cold_requests).reshape(slot_count)]
    is_hot = event_hot == 1
    hot_index = jnp.where(is_hot, event_index, 0)
    cold_index = jnp.where(is_hot, 0, event_index)
    row_vals = jnp.where(is_hot[:, None], hot_table[hot_index], fetched[cold_index]).astype(
        jnp.float32
    )
    scale_rows = causal_scale(seq_lengths[0], row_vals.shape[0])
    pre_out, pullback = jax.vjp(
        lambda inputs: layer_forward(inputs, w_in, w_out, scale_rows), row_vals
    )
    row_grads = pullback(out_grad.astype(jnp.float32))[0]
    hot_local = jax.ops.segment_sum(
        jnp.where(is_hot[:, None], row_grads, 0.0), hot_index, num_segments=hot_rows
    )
    slot_part = jax.ops.segment_sum(
        jnp.where(is_hot[:, None], 0.0, row_grads), cold_index, num_segments=slot_count
    )
    returned = lax.all_to_all(
        slot_part.reshape(table_count, cap_size, model_width),
        "table",
        split_axis=0,
        concat_axis=0,
        tiled=True,
    )
    returned = returned.reshape(slot_count, model_width)
    wanted_rows = wanted.reshape(slot_count)
    shard_grad = jax.ops.segment_sum(returned, wanted_rows, num_segments=shard_rows)
    cold_part = lax.psum_scatter(shard_grad, "dp", scatter_dimension=0, tiled=True)
    hot_part = lax.psum_scatter(hot_local, "dp", scatter_dimension=0, tiled=True)
    hot_part = lax.psum(hot_part, "table")
    return (pre_out.astype(jnp.bfloat16), hot_part, cold_part)


def solution(mesh):
    placed = (
        P(),
        P("table", None),
        P(),
        P(),
        P(("table", "dp"), None),
        P(("table", "dp")),
        P(("table", "dp")),
        P(("table", "dp"), None),
        P(("table", "dp"), None),
    )
    return jax.shard_map(
        on_device,
        mesh=mesh,
        in_specs=placed,
        out_specs=(P(("table", "dp"), None), P("dp", None), P(("table", "dp"), None)),
        check_vma=False,
    )
```

profile of v0, /device:TPU:2, one launch (start us, length us, event | category | flops | bytes accessed | tf_op | source)
XLA Modules:
  0.0 643.2 jit_solution(9478687762722239330)
XLA Ops:
  10.2 2.1 gather_fusion
  14.0 51.1 %all-gather.2.cloned.1.call-done = bf16[4096,1024]{1,0:T(8,128)(2,1)} async-done(((bf16[512,1024]{1,0:T(8,128)(2,1)}), bf16[4096,1024]{1,0:T(8,128)(2,1)}) %all-gather.2.cloned.1.call-update) | async-done | bytes 8388624 | tf_op jit(solution)/shard_map/all_gather | solution.py:61
  65.2 5.5 gather_fusion.1
  70.7 2.8 gather_fusion.2
  75.9 4.8 multiply_convert_fusion.1
  84.9 4.9 multiply_convert_fusion
  93.5 2.6 multiply_reduce_fusion
  96.1 2.4 fusion.62
  101.5 3.2 fusion.64
  104.7 4.2 fusion.7
  111.9 2.0 copy.59
  113.9 2.1 copy.58
  116.0 2.1 copy.57
  118.0 7.3 %fusion.14 = (f32[512]{0:T(512)S(1)}, bf16[512,1024]{1,0:T(8,128)(2,1)S(1)}) fusion(bf16[512,1024]{1,0:T(8,128)(2,1)S(1)} %get-tuple-element.6, f32[512]{0:T(512)S(1)} %broadcast_multiply_fusion.1, bf16[1024,2048]{1,0:T(8,128)(2,1)} %param.11, f32[512,2048]{1,0:T(8,128)} %get-tuple-element.19, bf16[512,512]{1,0:T(8,128)(2,1)} %get-tuple-element.15, ...), kind=kOutput, calls=%fused_computation.31 | convolution fusion | flops 2168454656 | bytes 12587008 | tf_op jit(solution)/shard_map/transpose(jvp())/dot_general | solution.py:34
  126.6 2.1 add_add_fusion.1
  128.6 7.3 %scatter_custom_fusion = f32[512,1024]{1,0:T(8,128)} fusion(s32[512]{0:T(512)S(1)} %get-tuple-element.11, f32[]{:T(128)} %constant.18.clone.1, f32[512,1024]{1,0:T(8,128)} %add_add_fusion.1, pred[512]{0:T(512)(128)(4,1)S(1)} %get-tuple-element.9), kind=kCustom, calls=%fused_computation.64 | custom fusion | flops 1048576 | bytes 4195840 | tf_op jit(solution)/shard_map/scatter-add | solution.py:75
  136.0 3.5 all-to-all-start
  139.5 6.7 %scatter_custom_fusion.1 = f32[128,1024]{1,0:T(8,128)} fusion(s32[512]{0:T(512)S(1)} %get-tuple-element.8, f32[512,1024]{1,0:T(8,128)} %add_add_fusion.1, f32[]{:T(128)} %constant.18.clone.1, pred[512]{0:T(512)(128)(4,1)S(1)} %get-tuple-element.9), kind=kCustom, calls=%fused_computation.33 | custom fusion | flops 1048576 | bytes 2622976 | tf_op jit(solution)/shard_map/scatter-add | solution.py:78
  146.2 4.5 all-to-all-start.1
  150.7 200.5 %reduce-scatter.3.cloned.1.call-done = f32[16,1024]{1,0:T(8,128)} async-done(((f32[512,1024]{1,0:T(8,128)}), f32[16,1024]{1,0:T(8,128)}) %reduce-scatter.3.cloned.1.call-update) | async-done | bytes 65552 | tf_op jit(solution)/shard_map/reduce_scatter | solution.py:92
  352.6 3.5 scatter_custom_fusion.2
  356.2 2.8 fusion.15
  359.0 57.8 %all-reduce.6.cloned.1.call-done = f32[16,1024]{1,0:T(8,128)} async-done(((f32[16,1024]{1,0:T(8,128)}), f32[16,1024]{1,0:T(8,128)}) %all-reduce.6.cloned.1.call-update) | async-done | bytes 65552 | tf_op jit(solution)/shard_map/psum | solution.py:93
  416.7 218.5 %reduce-scatter.5.cloned.1.call-done = f32[16,1024]{1,0:T(8,128)} async-done(((f32[512,1024]{1,0:T(8,128)}), f32[16,1024]{1,0:T(8,128)}) %reduce-scatter.5.cloned.1.call-update) | async-done | bytes 65552 | tf_op jit(solution)/shard_map/reduce_scatter | solution.py:91
  (80 shorter events, 25.0 us)
Async XLA Ops:
  7.2 86.3 %copy-start = (bf16[512,1024]{1,0:T(8,128)(2,1)S(1)}, bf16[512,1024]{1,0:T(8,128)(2,1)}, u32[]{:S(2)}) copy-start(bf16[512,1024]{1,0:T(8,128)(2,1)} %param.12) | copy-start | bytes 3145732
  7.2 3.0 copy-start.1
  7.2 58.0 %all-gather.2.cloned.1.call-start = ((), (), s32[]{:S(2)}) async-start(), calls=%async_computation.4 | async-start | bytes 9437184 | tf_op jit(solution)/shard_map/all_gather | solution.py:61
  7.9 343.3 %reduce-scatter.3.cloned.1.call-start = ((), (), s32[]{:S(2)}) async-start(), calls=%async_computation.5 | async-start | bytes 2162688 | tf_op jit(solution)/shard_map/reduce_scatter | solution.py:92
  10.2 2.1 copy-start.14
  73.4 2.5 copy-start.15
  80.7 1.4 copy-start.4
  83.5 6.4 copy-start.7
  84.9 4.9 copy-start.9
  84.9 6.2 copy-start.5
  89.8 1.3 copy-start.3
  93.5 2.7 copy-start.2
  101.5 3.2 copy-start.6
  101.5 3.2 copy-start.11
  101.5 3.2 copy-start.13
  104.7 4.2 copy-start.10
  109.0 1.6 copy-start.8
  125.3 1.2 copy-start.12
  136.0 10.2 %all-to-all-start = ((s32[8,1,16]{2,1,0:T(1,128)}), s32[8,1,16]{2,1,0:T(1,128)S(1)}, u32[]{:S(2)}, u32[]{:S(2)}) async-start(s32[8,1,16]{2,1,0:T(1,128)} %bitcast.16), calls=%async_computation.1 | async-start | bytes 8192 | tf_op jit(solution)/shard_map/all_to_all | solution.py:60
  146.2 206.4 %all-to-all-start.1 = ((f32[8,16,1024]{2,1,0:T(8,128)}), f32[8,16,1024]{2,1,0:T(8,128)}, u32[]{:S(2)}, u32[]{:S(2)}) async-start(f32[8,16,1024]{2,1,0:T(8,128)} %bitcast.61), calls=%async_computation.2 | async-start | bytes 1048576 | tf_op jit(solution)/shard_map/all_to_all | solution.py:81
  150.7 266.0 %all-reduce.6.cloned.1.call-start = ((), (), s32[]{:S(2)}) async-start(), calls=%async_computation.6 | async-start | bytes 131072 | tf_op jit(solution)/shard_map/psum | solution.py:93
  351.3 283.9 %reduce-scatter.5.cloned.1.call-start = ((), (), s32[]{:S(2)}) async-start(), calls=%async_computation.7 | async-start | bytes 2162688 | tf_op jit(solution)/shard_map/reduce_scatter | solution.py:91
Sparse Core Ops, SparseCore 0:
  9.9 55.2 all-gather.1
  136.1 215.1 reduce-scatter.2
  353.7 63.0 all-reduce.5
  421.0 214.1 reduce-scatter.4
where the time goes:
time: 645 us; the launch traced here: 643 us
  waiting for transfers between devices  529 us (82%)
  matrix products  33.5 us (5%)
  other arithmetic  30.7 us (5%)
  local copies, waits for them, and re-layouts  28.2 us (4%)
  between operations  14 us (2%)
  starting transfers between devices  8.19 us (1%)
    reduce_scatter x1, waiting for transfers between devices, on_device(): lax.psum_scatter(shard_grad, 'dp', scatter_dimension=0, tiled=True)  218 us
    reduce_scatter x1, waiting for transfers between devices, on_device(): lax.psum_scatter(hot_local, 'dp', scatter_dimension=0, tiled=True)  201 us
    psum x1, waiting for transfers between devices, on_device(): hot_part = lax.psum(hot_part, 'table')  57.8 us
    all_gather x1, waiting for transfers between devices, on_device(): all_rows = lax.all_gather(cold_table, 'table', axis=0, tiled=True)  51.1 us
  transfers between devices with their start and end apart: 6, of which 4 were waited for; matrix products, arithmetic and copies ran while one was open for 3% of the time, Pallas kernels for 0%

commit v1 on v0

--- a/solution.py
+++ b/solution.py
@@ -48,6 +48,30 @@
     return jnp.dot(merged, w_out, preferred_element_type=jnp.float32) + row_vals
 
 
+def shift(groups, step):
+    return [(g[i], g[(i + step) % len(g)]) for g in groups for i in range(len(g))]
+
+
+CORE_GROUPS = [[2 * y, 2 * y + 1] for y in range(4)]
+Y_GROUPS = [[2 * y + core for y in range(4)] for core in range(2)]
+X_GROUPS = [[4 * z + x for x in range(4)] for z in range(8)]
+Z_GROUPS = [[4 * z + x for z in range(8)] for x in range(4)]
+
+
+def reduce_stage(chunks, axis, groups):
+    total = chunks[0].astype(jnp.float32)
+    arrived = [
+        lax.ppermute(chunk, axis, shift(groups, k)) for k, chunk in enumerate(chunks) if k > 0
+    ]
+    for piece in arrived:
+        total = total + piece.astype(jnp.float32)
+    return total.astype(jnp.bfloat16)
+
+
+def one_hot_rows(ids, rows):
+    return (lax.iota(jnp.int32, rows)[:, None] == ids[None, :]).astype(jnp.bfloat16)
+
+
 def on_device(
     hot_table, cold_table, w_in, w_out, seq_lengths, event_hot, event_index, cold_requests, out_grad
 ):
@@ -57,10 +81,18 @@
     shard_rows = cold_table.shape[0]
     model_width = cold_table.shape[1]
     hot_rows = hot_table.shape[0]
+    table_at, dp_at = lax.axis_index("table"), lax.axis_index("dp")
+    y_at, core_at, x_at = table_at // 2, table_at % 2, dp_at % 4
+
     wanted = lax.all_to_all(cold_requests, "table", split_axis=0, concat_axis=0, tiled=True)
-    all_rows = lax.all_gather(cold_table, "table", axis=0, tiled=True)
-    owners = lax.iota(jnp.int32, table_count)[:, None] * shard_rows
-    fetched = all_rows[(owners + cold_requests).reshape(slot_count)]
+    wanted = wanted.reshape(slot_count)
+    fetched = lax.all_to_all(
+        cold_table[wanted].reshape(table_count, cap_size, model_width),
+        "table",
+        split_axis=0,
+        concat_axis=0,
+        tiled=True,
+    ).reshape(slot_count, model_width)
     is_hot = event_hot == 1
     hot_index = jnp.where(is_hot, event_index, 0)
     cold_index = jnp.where(is_hot, 0, event_index)
@@ -71,27 +103,50 @@
     pre_out, pullback = jax.vjp(
         lambda inputs: layer_forward(inputs, w_in, w_out, scale_rows), row_vals
     )
-    row_grads = pullback(out_grad.astype(jnp.float32))[0]
-    hot_local = jax.ops.segment_sum(
-        jnp.where(is_hot[:, None], row_grads, 0.0), hot_index, num_segments=hot_rows
+    row_grads = pullback(out_grad.astype(jnp.float32))[0].astype(jnp.bfloat16)
+
+    hot_dp, hot_t = event_index // 16, (event_index % 16) // 2
+    hot_place = (
+        (hot_t % 2 - core_at) % 2 * 256
+        + (hot_t // 2 - y_at) % 4 * 64
+        + (hot_dp % 4 - x_at) % 4 * 16
+        + hot_dp // 4 * 2
+        + event_index % 2
     )
-    slot_part = jax.ops.segment_sum(
-        jnp.where(is_hot[:, None], 0.0, row_grads), cold_index, num_segments=slot_count
+    hot_pick = one_hot_rows(jnp.where(is_hot, hot_place, -1), hot_rows)
+    slot_pick = one_hot_rows(jnp.where(is_hot, -1, event_index), slot_count)
+    slot_part = jnp.dot(slot_pick, row_grads, preferred_element_type=jnp.float32).astype(
+        jnp.bfloat16
     )
+    hot_part = jnp.dot(hot_pick, row_grads, preferred_element_type=jnp.float32).astype(jnp.bfloat16)
+    hot_part = reduce_stage([hot_part[:256], hot_part[256:]], "table", CORE_GROUPS)
     returned = lax.all_to_all(
         slot_part.reshape(table_count, cap_size, model_width),
         "table",
         split_axis=0,
         concat_axis=0,
         tiled=True,
+    ).reshape(slot_count, model_width)
+    hot_part = reduce_stage([hot_part[64 * k : 64 * k + 64] for k in range(4)], "table", Y_GROUPS)
+    shard_place = (wanted // 16 % 4 - x_at) % 4 * 128 + wanted // 64 * 16 + wanted % 16
+    shard_pick = one_hot_rows(shard_place, shard_rows)
+    shard_grad = jnp.dot(shard_pick, returned, preferred_element_type=jnp.float32).astype(
+        jnp.bfloat16
     )
-    returned = returned.reshape(slot_count, model_width)
-    wanted_rows = wanted.reshape(slot_count)
-    shard_grad = jax.ops.segment_sum(returned, wanted_rows, num_segments=shard_rows)
-    cold_part = lax.psum_scatter(shard_grad, "dp", scatter_dimension=0, tiled=True)
-    hot_part = lax.psum_scatter(hot_local, "dp", scatter_dimension=0, tiled=True)
-    hot_part = lax.psum(hot_part, "table")
-    return (pre_out.astype(jnp.bfloat16), hot_part, cold_part)
+    both = [
+        jnp.concatenate([shard_grad[128 * k : 128 * k + 128], hot_part[16 * k : 16 * k + 16]])
+        for k in range(4)
+    ]
+    both = reduce_stage(both, "dp", X_GROUPS)
+    by_z = jnp.concatenate(
+        [both[:128].reshape(8, 16, model_width), both[128:].reshape(8, 2, model_width)], axis=1
+    )
+    by_z = lax.all_to_all(
+        by_z, "dp", split_axis=0, concat_axis=0, tiled=True, axis_index_groups=Z_GROUPS
+    )
+    summed = jnp.sum(by_z.astype(jnp.float32), axis=0)
+    hot_sum = lax.all_gather(summed[16:], "table", axis=0, tiled=True)
+    return (pre_out.astype(jnp.bfloat16), hot_sum, summed[:16])
 
 
 def solution(mesh):

time: 645 us -> 164 us (0.25)
  waiting for transfers between devices: 529 us -> 42.2 us
  starting transfers between devices: 8.19 us -> 29.1 us
  other arithmetic: 30.7 us -> 15 us
  between operations: 14 us -> 0.98 us
  blocking collectives: 0 us -> 13 us
    reduce_scatter x2 -> x0, waiting for transfers between devices: 419 us -> none  [the longest x1 218 us: on_device(): lax.psum_scatter(shard_grad, 'dp', scatter_dimension=0, tiled=True)]
    psum x1 -> x0, waiting for transfers between devices: 57.8 us -> none  [on_device(): hot_part = lax.psum(hot_part, 'table')]
    all_gather x1 -> x0, waiting for transfers between devices: 51.1 us -> none  [on_device(): all_rows = lax.all_gather(cold_table, 'table', axis=0, tiled=True)]
    all_to_all x0 -> x2, waiting for transfers between devices: none -> 17.7 us  [the longest x1 11.4 us: on_device(): lax.all_to_all(by_z, 'dp', split_axis=0, concat_axis=0, tiled=True, axis_...]
    scatter-add x3 -> x0, other arithmetic: 17.5 us -> none  [the longest x1 7.33 us: on_device(): jax.ops.segment_sum(jnp.where(is_hot[:, None], row_grads, 0.0), hot_index...]
    ppermute x0 -> x7, waiting for transfers between devices: none -> 17.2 us  [reduce_stage(): lax.ppermute(chunk, axis, shift(groups, k))]
    all_gather x0 -> x1, blocking collectives: none -> 13 us  [on_device(): hot_sum = lax.all_gather(summed[16:], 'table', axis=0, tiled=True)]
    all_to_all x0 -> x2, starting transfers between devices: none -> 12.8 us  [the longest x1 7.97 us: on_device(): lax.all_to_all(by_z, 'dp', split_axis=0, concat_axis=0, tiled=True, axis_...]
  transfers between devices with their start and end apart: 6 -> 11, of which waited for: 4 -> 9; matrix products, arithmetic and copies ran while one was open for 3% -> 8% of each run, Pallas kernels for 0% -> 0%
where the time goes in v1:
time: 164 us; the launch traced here: 162 us
  waiting for transfers between devices  42.2 us (26%)
  matrix products  35.7 us (22%)
  starting transfers between devices  29.1 us (18%)
  local copies, waits for them, and re-layouts  26.2 us (16%)
  other arithmetic  15 us (9%)
  blocking collectives  13 us (8%)
    ppermute x7, waiting for transfers between devices, reduce_stage(): lax.ppermute(chunk, axis, shift(groups, k))  17.2 us
    all_gather x1, blocking collectives, on_device(): hot_sum = lax.all_gather(summed[16:], 'table', axis=0, tiled=True)  13 us
    dot_general x2, matrix products, layer_forward(): jnp.dot(normed, w_in, preferred_element_type=jnp.float32)  12.1 us
    all_to_all x1, waiting for transfers between devices, on_device(): lax.all_to_all(by_z, 'dp', split_axis=0, concat_axis=0, tiled=True, axis_...  11.4 us
    ppermute x7, starting transfers between devices, reduce_stage(): lax.ppermute(chunk, axis, shift(groups, k))  8.33 us
    dot_general x3, matrix products, layer_forward(): jnp.einsum('hqk,khd->qhd', weights, value_vals, preferred_element_type=jn...  8.27 us
    all_to_all x1, starting transfers between devices, on_device(): lax.all_to_all(by_z, 'dp', split_axis=0, concat_axis=0, tiled=True, axis_...  7.97 us
    dot_general x3, matrix products, layer_forward(): jnp.einsum('qhd,khd->hqk', query_vals, key_vals, preferred_element_type=j...  7.73 us
  transfers between devices with their start and end apart: 11, of which 9 were waited for; matrix products, arithmetic and copies ran while one was open for 8% of the time, Pallas kernels for 0%

profile of v1, /device:TPU:2, one launch (start us, length us, event | category | flops | bytes accessed | tf_op | source)
XLA Modules:
  0.0 162.2 jit_solution(280852370758316368)
XLA Ops:
  0.6 4.6 %all-to-all-start = ((s32[8,1,16]{2,1,0:T(1,128)}), s32[8,1,16]{2,1,0:T(1,128)S(1)}, u32[]{:S(2)}, u32[]{:S(2)}) async-start(s32[8,1,16]{2,1,0:T(1,128)} %bitcast.80), calls=%async_computation | async-start | bytes 8192 | tf_op jit(solution)/shard_map/all_to_all | solution.py:87
  8.4 4.2 %gather_fusion = bf16[512,1024]{1,0:T(8,128)(2,1)S(1)} fusion(bf16[512,1024]{1,0:T(8,128)(2,1)} %param.9, s32[1024]{0:T(1024)S(1)} %get-tuple-element.40), kind=kCustom, calls=%fused_computation | custom fusion | bytes 2099200 | tf_op jit(solution)/shard_map/gather | solution.py:99
  15.4 4.8 %all-to-all-start.1 = ((bf16[8,16,1024]{2,1,0:T(8,128)(2,1)}), bf16[8,16,1024]{2,1,0:T(8,128)(2,1)S(1)}, u32[]{:S(2)}, u32[]{:S(2)}) async-start(bf16[8,16,1024]{2,1,0:T(8,128)(2,1)} %bitcast.3), calls=%async_computation.1 | async-start | bytes 524288 | tf_op jit(solution)/shard_map/all_to_all | solution.py:89
  21.5 6.3 %all-to-all-done.1 = bf16[8,16,1024]{2,1,0:T(8,128)(2,1)S(1)} async-done(((bf16[8,16,1024]{2,1,0:T(8,128)(2,1)}), bf16[8,16,1024]{2,1,0:T(8,128)(2,1)S(1)}, u32[]{:S(2)}, u32[]{:S(2)}) %all-to-all-start.1) | async-done | bytes 262176 | tf_op jit(solution)/shard_map/all_to_all | solution.py:89
  27.8 2.8 %gather_fusion.2 = bf16[512,1024]{1,0:T(8,128)(2,1)} fusion(bf16[128,1024]{1,0:T(8,128)(2,1)S(1)} %bitcast.65, s32[1024]{0:T(1024)S(1)} %get-tuple-element.39), kind=kCustom, calls=%fused_computation.2 | custom fusion | bytes 2099200 | tf_op jit(solution)/shard_map/gather | solution.py:99
  33.1 4.8 %multiply_convert_fusion.1 = (bf16[512,2048]{1,0:T(8,128)(2,1)S(1)}, f32[512,2048]{1,0:T(8,128)}) fusion(bf16[1024,2048]{1,0:T(8,128)(2,1)S(1)} %copy-done.15, bf16[512,1024]{1,0:T(8,128)(2,1)S(1)} %get-tuple-element.8, f32[512]{0:T(512)S(1)} %fusion.72, f32[512]{0:T(512)S(1)} %broadcast_multiply_fusion.1), kind=kOutput, calls=%fused_computation.15 | convolution fusion | flops 2154823680 | bytes 11538432 | tf_op jit(solution)/shard_map/jvp()/dot_general | solution.py:34
  42.0 4.9 %multiply_convert_fusion = (bf16[4,512,512]{2,1,0:T(8,128)(2,1)S(1)}, f32[4,512,512]{2,1,0:T(8,128)}) fusion(f32[512,512]{1,0:T(8,128)} %fusion.37, bf16[512,4,128]{0,2,1:T(8,128)(2,1)S(1)} %bitcast.69, bf16[512,4,128]{0,2,1:T(8,128)(2,1)S(1)} %bitcast.67), kind=kOutput, calls=%fused_computation.13 | convolution fusion | flops 275775488 | bytes 8388608 | tf_op jit(solution)/shard_map/jvp(qhd,khd->hqk)/dot_general | solution.py:41
  49.6 2.6 %multiply_reduce_fusion = (f32[512]{0:T(512)S(1)}, bf16[512,512]{1,0:T(8,128)(2,1)S(1)}) fusion(f32[512,512]{1,0:T(8,128)} %copy.55, f32[512]{0:T(512)S(1)} %broadcast_multiply_fusion, bf16[512,2048]{1,0:T(8,128)(2,1)} %copy-done.4, bf16[512,1024]{1,0:T(8,128)(2,1)} %param.17, bf16[512,1024]{1,0:T(8,128)(2,1)S(1)} %copy-done), kind=kOutput, calls=%fused_computation.60 | convolution fusion | flops 538705408 | bytes 4198400 | tf_op jit(solution)/shard_map/transpose(jvp())/dot_general | solution.py:48
  52.2 2.4 %fusion.83 = (f32[512]{0:T(512)S(1)}, f32[512,512]{1,0:T(8,128)S(1)}, bf16[512,512]{1,0:T(8,128)(2,1)}) fusion(f32[512]{0:T(512)S(1)} %get-tuple-element.27, f32[512,512]{1,0:T(8,128)S(1)} %copy-done.1, f32[512]{0:T(512)S(1)} %broadcast_multiply_fusion, f32[512]{0:T(512)S(1)} %get-tuple-element.28, bf16[512,2048]{1,0:T(8,128)(2,1)} %copy-done.4, ...), kind=kLoop, calls=%fused_computation.192 | loop fusion | flops 3145216 | bytes 3678208 | tf_op jit(solution)/shard_map/transpose(jvp())/reduce_sum | solution.py:14
  57.6 3.1 %fusion.88 = bf16[4,128,512]{2,1,0:T(8,128)(2,1)} fusion(bf16[4,128,512]{2,1,0:T(8,128)(2,1)} %bitcast.73, bf16[4,512,512]{2,1,0:T(8,128)(2,1)} %copy-done.2), kind=kOutput, calls=%fused_computation.197 | convolution fusion | flops 268435456 | bytes 3145728 | tf_op jit(solution)/shard_map/transpose(jvp(hqk,khd->qhd))/dot_general | solution.py:45
  60.8 4.3 %fusion.7 = bf16[4,512,512]{2,1,0:T(8,128)(2,1)S(1)} fusion(f32[4,512,512]{2,1,0:T(8,128)} %get-tuple-element.32, f32[512,512]{1,0:T(8,128)S(1)} %copy-done.13, bf16[4,128,512]{2,1,0:T(8,128)(2,1)S(1)} %bitcast.74, bf16[64,4,8,128]{3,2,1,0:T(8,128)(2,1)S(1)} %copy-done.6), kind=kOutput, calls=%fused_computation.12 | convolution fusion | flops 283115520 | bytes 8388608 | tf_op jit(solution)/shard_map/transpose(jvp(hqk,khd->qhd))/dot_general | solution.py:45
  67.9 2.1 %copy.59 = bf16[512,512]{1,0:T(8,128)(2,1)} copy(bf16[512,512]{0,1:T(8,128)(2,1)} %bitcast.71) | data formatting | bytes 1048576 | tf_op jit(solution)/shard_map/transpose(jvp())/reshape | solution.py:38
  74.1 7.3 %fusion.14 = (f32[512]{0:T(512)S(1)}, bf16[512,1024]{1,0:T(8,128)(2,1)S(1)}) fusion(bf16[512,1024]{1,0:T(8,128)(2,1)S(1)} %get-tuple-element.8, f32[512]{0:T(512)S(1)} %broadcast_multiply_fusion.1, bf16[1024,2048]{1,0:T(8,128)(2,1)} %param.11, f32[512,2048]{1,0:T(8,128)} %get-tuple-element.30, bf16[512,512]{1,0:T(8,128)(2,1)} %get-tuple-element.12, ...), kind=kOutput, calls=%fused_computation.28 | convolution fusion | flops 2168454656 | bytes 12587008 | tf_op jit(solution)/shard_map/transpose(jvp())/dot_general | solution.py:34
  86.1 3.4 %all-to-all-start.2 = ((bf16[8,16,1024]{2,1,0:T(8,128)(2,1)}), bf16[8,16,1024]{2,1,0:T(8,128)(2,1)S(1)}, u32[]{:S(2)}, u32[]{:S(2)}) async-start(bf16[8,16,1024]{2,1,0:T(8,128)(2,1)} %bitcast.77), calls=%async_computation.2 | async-start | bytes 524288 | tf_op jit(solution)/shard_map/all_to_all | solution.py:123
  89.6 7.3 %all-to-all-done.2 = bf16[8,16,1024]{2,1,0:T(8,128)(2,1)S(1)} async-done(((bf16[8,16,1024]{2,1,0:T(8,128)(2,1)}), bf16[8,16,1024]{2,1,0:T(8,128)(2,1)S(1)}, u32[]{:S(2)}, u32[]{:S(2)}) %all-to-all-start.2) | async-done | bytes 262176 | tf_op jit(solution)/shard_map/all_to_all | solution.py:123
  99.5 2.7 %collective-permute-start.3 = (bf16[64,1024]{1,0:T(8,128)(2,1)S(1)}, bf16[64,1024]{1,0:T(8,128)(2,1)S(1)}, u32[]{:S(2)}, u32[]{:S(2)}) collective-permute-start(bf16[64,1024]{1,0:T(8,128)(2,1)S(1)} %get-tuple-element.18), channel_id=1, source_target_pairs={{0,192},{64,0},{128,64},{192,128},{32,224},{96,32},{160,96},{224,1... | collective-permute-start | bytes 393224 | tf_op jit(solution)/shard_map/ppermute | solution.py:64
  102.2 2.9 %collective-permute-done.1 = bf16[64,1024]{1,0:T(8,128)(2,1)S(1)} collective-permute-done((bf16[64,1024]{1,0:T(8,128)(2,1)S(1)}, bf16[64,1024]{1,0:T(8,128)(2,1)S(1)}, u32[]{:S(2)}, u32[]{:S(2)}) %collective-permute-start.1) | collective-permute-done | bytes 131104 | tf_op jit(solution)/shard_map/ppermute | solution.py:64
  113.8 4.9 %collective-permute-done.4 = bf16[144,1024]{1,0:T(8,128)(2,1)S(1)} collective-permute-done((bf16[144,1024]{1,0:T(8,128)(2,1)S(1)}, bf16[144,1024]{1,0:T(8,128)(2,1)S(1)}, u32[]{:S(2)}, u32[]{:S(2)}) %collective-permute-start.4) | collective-permute-done | bytes 294944 | tf_op jit(solution)/shard_map/ppermute | solution.py:64
  118.6 2.9 %collective-permute-done.5 = bf16[144,1024]{1,0:T(8,128)(2,1)S(1)} collective-permute-done((bf16[144,1024]{1,0:T(8,128)(2,1)S(1)}, bf16[144,1024]{1,0:T(8,128)(2,1)S(1)}, u32[]{:S(2)}, u32[]{:S(2)}) %collective-permute-start.5) | collective-permute-done | bytes 294944 | tf_op jit(solution)/shard_map/ppermute | solution.py:64
  121.6 3.0 %collective-permute-done.6 = bf16[144,1024]{1,0:T(8,128)(2,1)S(1)} collective-permute-done((bf16[144,1024]{1,0:T(8,128)(2,1)S(1)}, bf16[144,1024]{1,0:T(8,128)(2,1)S(1)}, u32[]{:S(2)}, u32[]{:S(2)}) %collective-permute-start.6) | collective-permute-done | bytes 294944 | tf_op jit(solution)/shard_map/ppermute | solution.py:64
  125.6 8.0 %all-to-all-start.3 = ((bf16[8,18,1024]{2,1,0:T(8,128)(2,1)}), bf16[8,18,1024]{2,1,0:T(8,128)(2,1)S(1)}, u32[]{:S(2)}, u32[]{:S(2)}) async-start(bf16[8,18,1024]{2,1,0:T(8,128)(2,1)} %pad_maximum_fusion), calls=%async_computation.3 | async-start | bytes 786432 | tf_op jit(solution)/shard_map/all_to_all | solution.py:144
  133.6 2.8 %fusion.15 = bf16[512,1024]{1,0:T(8,128)(2,1)} fusion(bf16[512,1024]{1,0:T(8,128)(2,1)S(1)} %get-tuple-element.8, bf16[512,1024]{1,0:T(8,128)(2,1)S(1)} %copy-done, f32[512,512]{1,0:T(8,128)S(1)} %copy-done.1, f32[512]{0:T(512)S(1)} %get-tuple-element.28, f32[512]{0:T(512)S(1)} %broadcast_multiply_fusion, bf16[512,2048]{1,0:T(8,128)(2,1)} %copy-done.4), kind=kOutput, calls=%fused_computation.29 | convolution fusion | flops 539754496 | bytes 4722688 | tf_op jit(solution)/shard_map/jvp()/dot_general | solution.py:48
  136.4 11.4 %all-to-all-done.3 = bf16[8,18,1024]{2,1,0:T(8,128)(2,1)S(1)} async-done(((bf16[8,18,1024]{2,1,0:T(8,128)(2,1)}), bf16[8,18,1024]{2,1,0:T(8,128)(2,1)S(1)}, u32[]{:S(2)}, u32[]{:S(2)}) %all-to-all-start.3) | async-done | bytes 294944 | tf_op jit(solution)/shard_map/all_to_all | solution.py:144
  148.5 13.0 %all-gather = f32[8,2,1024]{2,1,0:T(2,128)S(1)} all-gather(f32[1,2,1024]{2,1,0:T(2,128)S(1)} %slice_bitcast_fusion.1), channel_id=1, replica_groups=mesh['table'=8,'dp'=32] {'table'}, dimensions={0}, use_global_device_ids=true | all-gather | bytes 73728 | tf_op jit(solution)/shard_map/all_gather | solution.py:148
  (102 shorter events, 44.8 us)
Async XLA Ops:
  0.6 48.9 %copy-start = (bf16[512,1024]{1,0:T(8,128)(2,1)S(1)}, bf16[512,1024]{1,0:T(8,128)(2,1)}, u32[]{:S(2)}) copy-start(bf16[512,1024]{1,0:T(8,128)(2,1)} %param.12) | copy-start | bytes 3145732
  0.6 11.9 %all-to-all-start = ((s32[8,1,16]{2,1,0:T(1,128)}), s32[8,1,16]{2,1,0:T(1,128)S(1)}, u32[]{:S(2)}, u32[]{:S(2)}) async-start(s32[8,1,16]{2,1,0:T(1,128)} %bitcast.80), calls=%async_computation | async-start | bytes 8192 | tf_op jit(solution)/shard_map/all_to_all | solution.py:87
  8.4 5.5 %copy-start.3 = (bf16[512,1024]{1,0:T(8,128)(2,1)S(1)}, bf16[512,1024]{1,0:T(8,128)(2,1)}, u32[]{:S(2)}) copy-start(bf16[512,1024]{1,0:T(8,128)(2,1)} %param.10) | copy-start | bytes 3145732
  15.4 12.3 %all-to-all-start.1 = ((bf16[8,16,1024]{2,1,0:T(8,128)(2,1)}), bf16[8,16,1024]{2,1,0:T(8,128)(2,1)S(1)}, u32[]{:S(2)}, u32[]{:S(2)}) async-start(bf16[8,16,1024]{2,1,0:T(8,128)(2,1)} %bitcast.3), calls=%async_computation.1 | async-start | bytes 524288 | tf_op jit(solution)/shard_map/all_to_all | solution.py:89
  30.5 2.5 %copy-start.15 = (bf16[1024,2048]{1,0:T(8,128)(2,1)S(1)}, bf16[1024,2048]{1,0:T(8,128)(2,1)}, u32[]{:S(2)}) copy-start(bf16[1024,2048]{1,0:T(8,128)(2,1)} %param.11) | copy-start | bytes 12582916
  40.6 6.4 %copy-start.7 = (bf16[512,512]{0,1:T(8,128)(2,1)}, bf16[512,512]{0,1:T(8,128)(2,1)S(1)}, u32[]{:S(2)}) copy-start(bf16[512,512]{0,1:T(8,128)(2,1)S(1)} %copy.61) | copy-start | bytes 1572868
  42.0 4.9 %copy-start.9 = (bf16[512,512]{0,1:T(8,128)(2,1)}, bf16[512,512]{0,1:T(8,128)(2,1)S(1)}, u32[]{:S(2)}) copy-start(bf16[512,512]{0,1:T(8,128)(2,1)S(1)} %copy.60) | copy-start | bytes 1572868
  42.0 4.9 %copy-start.5 = (bf16[64,4,8,128]{3,2,1,0:T(8,128)(2,1)S(1)}, bf16[64,4,8,128]{3,2,1,0:T(8,128)(2,1)}, u32[]{:S(2)}) copy-start(bf16[64,4,8,128]{3,2,1,0:T(8,128)(2,1)} %get-tuple-element.9) | copy-start | bytes 1572868
  49.6 2.7 %copy-start.1 = (f32[512,512]{1,0:T(8,128)S(1)}, f32[512,512]{1,0:T(8,128)}, u32[]{:S(2)}) copy-start(f32[512,512]{1,0:T(8,128)} %copy.55) | copy-start | bytes 3145732
  57.6 3.2 %copy-start.6 = (bf16[64,4,8,128]{3,2,1,0:T(8,128)(2,1)S(1)}, bf16[64,4,8,128]{3,2,1,0:T(8,128)(2,1)}, u32[]{:S(2)}) copy-start(bf16[64,4,8,128]{3,2,1,0:T(8,128)(2,1)} %get-tuple-element.9) | copy-start | bytes 1572868
  57.6 3.2 %copy-start.11 = (bf16[512,512]{0,1:T(8,128)(2,1)S(1)}, bf16[512,512]{0,1:T(8,128)(2,1)}, u32[]{:S(2)}) copy-start(bf16[512,512]{0,1:T(8,128)(2,1)} %copy.56) | copy-start | bytes 1572868
  57.6 3.2 %copy-start.13 = (f32[512,512]{1,0:T(8,128)S(1)}, f32[512,512]{1,0:T(8,128)}, u32[]{:S(2)}) copy-start(f32[512,512]{1,0:T(8,128)} %fusion.37) | copy-start | bytes 3145732
  60.8 4.3 %copy-start.8 = (bf16[512,512]{0,1:T(8,128)(2,1)S(1)}, bf16[512,512]{0,1:T(8,128)(2,1)}, u32[]{:S(2)}) copy-start(bf16[512,512]{0,1:T(8,128)(2,1)} %copy-done.7) | copy-start | bytes 1572868
  65.1 1.6 copy-start.10
  84.2 1.9 %copy-start.12 = (bf16[512,1024]{1,0:T(8,128)(2,1)}, bf16[512,1024]{1,0:T(8,128)(2,1)S(1)}, u32[]{:S(2)}) copy-start(bf16[512,1024]{1,0:T(8,128)(2,1)S(1)} %convolution_convert_fusion) | copy-start | bytes 3145732
  85.0 12.3 %collective-permute-start = (bf16[256,1024]{1,0:T(8,128)(2,1)}, bf16[256,1024]{1,0:T(8,128)(2,1)}, u32[]{:S(2)}, u32[]{:S(2)}) collective-permute-start(bf16[256,1024]{1,0:T(8,128)(2,1)} %slice.100), channel_id=1, source_target_pairs={{0,32},{32,0},{64,96},{96,64},{128,160},{160,128},{192,224},{224,1... | collective-permute-start | bytes 1572872 | tf_op jit(solution)/shard_map/ppermute | solution.py:64
  86.1 10.9 %all-to-all-start.2 = ((bf16[8,16,1024]{2,1,0:T(8,128)(2,1)}), bf16[8,16,1024]{2,1,0:T(8,128)(2,1)S(1)}, u32[]{:S(2)}, u32[]{:S(2)}) async-start(bf16[8,16,1024]{2,1,0:T(8,128)(2,1)} %bitcast.77), calls=%async_computation.2 | async-start | bytes 524288 | tf_op jit(solution)/shard_map/all_to_all | solution.py:123
  98.8 6.3 %collective-permute-start.1 = (bf16[64,1024]{1,0:T(8,128)(2,1)S(1)}, bf16[64,1024]{1,0:T(8,128)(2,1)S(1)}, u32[]{:S(2)}, u32[]{:S(2)}) collective-permute-start(bf16[64,1024]{1,0:T(8,128)(2,1)S(1)} %get-tuple-element.17), channel_id=1, source_target_pairs={{0,64},{64,128},{128,192},{192,0},{32,96},{96,160},{160,224},{224,... | collective-permute-start | bytes 393224 | tf_op jit(solution)/shard_map/ppermute | solution.py:64
  99.5 7.6 %collective-permute-start.3 = (bf16[64,1024]{1,0:T(8,128)(2,1)S(1)}, bf16[64,1024]{1,0:T(8,128)(2,1)S(1)}, u32[]{:S(2)}, u32[]{:S(2)}) collective-permute-start(bf16[64,1024]{1,0:T(8,128)(2,1)S(1)} %get-tuple-element.18), channel_id=1, source_target_pairs={{0,192},{64,0},{128,64},{192,128},{32,224},{96,32},{160,96},{224,1... | collective-permute-start | bytes 393224 | tf_op jit(solution)/shard_map/ppermute | solution.py:64
  102.1 6.5 %collective-permute-start.2 = (bf16[64,1024]{1,0:T(8,128)(2,1)S(1)}, bf16[64,1024]{1,0:T(8,128)(2,1)S(1)}, u32[]{:S(2)}, u32[]{:S(2)}) collective-permute-start(bf16[64,1024]{1,0:T(8,128)(2,1)S(1)} %get-tuple-element.19), channel_id=1, source_target_pairs={{0,128},{64,192},{128,0},{192,64},{32,160},{96,224},{160,32},{224,... | collective-permute-start | bytes 393224 | tf_op jit(solution)/shard_map/ppermute | solution.py:64
  108.7 9.9 %collective-permute-start.4 = (bf16[144,1024]{1,0:T(8,128)(2,1)S(1)}, bf16[144,1024]{1,0:T(8,128)(2,1)S(1)}, u32[]{:S(2)}, u32[]{:S(2)}) collective-permute-start(bf16[144,1024]{1,0:T(8,128)(2,1)S(1)} %pad_maximum_fusion.1), channel_id=1, source_target_pairs={{0,1},{1,2},{2,3},{3,0},{4,5},{5,6},{6,7},{7,4},{8,9},{9,10},{10,1... | collective-permute-start | bytes 884744 | tf_op jit(solution)/shard_map/ppermute | solution.py:64
  110.3 11.2 %collective-permute-start.5 = (bf16[144,1024]{1,0:T(8,128)(2,1)S(1)}, bf16[144,1024]{1,0:T(8,128)(2,1)S(1)}, u32[]{:S(2)}, u32[]{:S(2)}) collective-permute-start(bf16[144,1024]{1,0:T(8,128)(2,1)S(1)} %pad_maximum_fusion.2), channel_id=1, source_target_pairs={{0,2},{1,3},{2,0},{3,1},{4,6},{5,7},{6,4},{7,5},{8,10},{9,11},{10,... | collective-permute-start | bytes 884744 | tf_op jit(solution)/shard_map/ppermute | solution.py:64
  112.0 12.5 %collective-permute-start.6 = (bf16[144,1024]{1,0:T(8,128)(2,1)S(1)}, bf16[144,1024]{1,0:T(8,128)(2,1)S(1)}, u32[]{:S(2)}, u32[]{:S(2)}) collective-permute-start(bf16[144,1024]{1,0:T(8,128)(2,1)S(1)} %pad_maximum_fusion.3), channel_id=1, source_target_pairs={{0,3},{1,0},{2,1},{3,2},{4,7},{5,4},{6,5},{7,6},{8,11},{9,8},{10,9... | collective-permute-start | bytes 884744 | tf_op jit(solution)/shard_map/ppermute | solution.py:64
  125.6 22.2 %all-to-all-start.3 = ((bf16[8,18,1024]{2,1,0:T(8,128)(2,1)}), bf16[8,18,1024]{2,1,0:T(8,128)(2,1)S(1)}, u32[]{:S(2)}, u32[]{:S(2)}) async-start(bf16[8,18,1024]{2,1,0:T(8,128)(2,1)} %pad_maximum_fusion), calls=%async_computation.3 | async-start | bytes 786432 | tf_op jit(solution)/shard_map/all_to_all | solution.py:144
  (3 other events, 3.9 us)

commit v2 on v1

v2 whole, which is shorter than its diff:
```python
import jax
import jax.numpy as jnp
from jax import lax
from jax.experimental import pallas as pl
from jax.experimental.pallas import tpu as pltpu
from jax.sharding import PartitionSpec as P

HEAD = 128


EPS = 1e-06
BLOCK = 128
BACK = 2


def sigmoid(values):
    return 0.5 * jnp.tanh(0.5 * values) + 0.5


def mean_of(values):
    return jnp.mean(values, axis=-1, keepdims=True)


def dot_nn(a, b):
    return jnp.dot(a, b, preferred_element_type=jnp.float32)


def dot_nt(a, b):
    return lax.dot_general(a, b, (((1,), (1,)), ((), ())), preferred_element_type=jnp.float32)


def dot_tn(a, b):
    return lax.dot_general(a, b, (((0,), (0,)), ((), ())), preferred_element_type=jnp.float32)


def layer_kernel(
    lengths_ref,
    hot_ref,
    fetched_ref,
    w_in_ref,
    w_out_ref,
    out_grad_ref,
    source_ref,
    place_ref,
    layer_out_ref,
    near_ref,
    far_ref,
    slots_ref,
    rows_ref,
    normed_ref,
    rstd_ref,
    mixed_ref,
    slope_ref,
    weights_ref,
    dscore_ref,
    attended_ref,
    dvalue_ref,
    dkey_ref,
    dpre_ref,
    dnorm_ref,
):
    tokens, width = rows_ref.shape
    hot_rows, slot_count = hot_ref.shape[0], fetched_ref.shape[0]
    inner = w_out_ref.shape[0]
    heads = inner // HEAD
    bf16, f32 = jnp.bfloat16, jnp.float32

    @pl.loop(0, tokens // BLOCK)
    def _(step):
        at = pl.ds(pl.multiple_of(step * BLOCK, BLOCK), BLOCK)
        source = source_ref[at, :]
        hot_pick = (source == lax.broadcasted_iota(jnp.int32, (BLOCK, hot_rows), 1)).astype(bf16)
        slot_pick = (
            source == lax.broadcasted_iota(jnp.int32, (BLOCK, slot_count), 1) + hot_rows
        ).astype(bf16)
        rows = dot_nn(hot_pick, hot_ref[...]) + dot_nn(slot_pick, fetched_ref[...])
        centered = rows - mean_of(rows)
        rstd = lax.rsqrt(mean_of(centered * centered) + EPS)
        rows_ref[at, :] = rows.astype(bf16)
        normed_ref[at, :] = (centered * rstd).astype(bf16)
        rstd_ref[at, :] = rstd

    @pl.loop(0, 4 * inner // 256)
    def _(step):
        at = pl.ds(pl.multiple_of(step * 256, 256), 256)
        pre = dot_nn(normed_ref[...], w_in_ref[:, at])
        sig = sigmoid(pre)
        act = pre * sig
        mixed_ref[:, at] = act.astype(bf16)
        slope_ref[:, at] = (sig + act * (1.0 - sig)).astype(bf16)

    def columns(part, head):
        return pl.ds(part * inner + head * HEAD, HEAD)

    for block in range(tokens // BLOCK):
        q_at = pl.ds(block * BLOCK, BLOCK)
        first = max(0, block - BACK)
        reach = (block + 1 - first) * BLOCK
        k_at = pl.ds(first * BLOCK, reach)
        position = lax.broadcasted_iota(jnp.int32, (BLOCK, 1), 0) + block * BLOCK
        begin = jnp.zeros((BLOCK, 1), jnp.int32)
        length = jnp.zeros((BLOCK, 1), jnp.int32)
        end = jnp.int32(0)
        for history in range(lengths_ref.shape[1]):
            start = end
            end = start + lengths_ref[0, history]
            inside = position >= start
            begin = jnp.where(inside, start, begin)
            length = jnp.where(inside, end - start, length)
        key_position = lax.broadcasted_iota(jnp.int32, (BLOCK, reach), 1) + first * BLOCK
        allowed = (key_position <= position) & (key_position >= begin)
        share = jnp.where(allowed, 1.0 / length.astype(f32), 0.0)
        for head in range(heads):
            scores = dot_nt(
                mixed_ref[q_at, columns(2, head)], mixed_ref[k_at, columns(3, head)]
            ) * (HEAD ** -0.5)
            sig = sigmoid(scores)
            act = scores * sig
            weights = (act * share).astype(bf16)
            weights_ref[head, q_at, :reach] = weights
            dscore_ref[head, q_at, :reach] = (
                (sig + act * (1.0 - sig)) * (share * (HEAD ** -0.5))
            ).astype(bf16)
            attended_ref[q_at, pl.ds(head * HEAD, HEAD)] = dot_nn(
                weights, mixed_ref[k_at, columns(1, head)]
            )

    for block in range(tokens // 256):
        at = pl.ds(block * 256, 256)
        attended = attended_ref[at, :]
        centered = attended - mean_of(attended)
        rstd = lax.rsqrt(mean_of(centered * centered) + EPS)
        unit = centered * rstd
        gate = mixed_ref[at, :inner].astype(f32)
        merged = (unit * gate).astype(bf16)
        layer_out_ref[at, :] = (
            dot_nn(merged, w_out_ref[...]) + rows_ref[at, :].astype(f32)
        ).astype(bf16)
        dmerged = dot_nt(out_grad_ref[at, :], w_out_ref[...])
        dpre_ref[at, :inner] = (dmerged * unit * slope_ref[at, :inner].astype(f32)).astype(bf16)
        dunit = dmerged * gate
        attended_ref[at, :] = rstd * (dunit - mean_of(dunit) - unit * mean_of(dunit * unit))

    dvalue_ref[...] = jnp.zeros_like(dvalue_ref)
    dkey_ref[...] = jnp.zeros_like(dkey_ref)
    for block in range(tokens // BLOCK):
        q_at = pl.ds(block * BLOCK, BLOCK)
        first = max(0, block - BACK)
        reach = (block + 1 - first) * BLOCK
        k_at = pl.ds(first * BLOCK, reach)
        for head in range(heads):
            own = pl.ds(head * HEAD, HEAD)
            dattended = attended_ref[q_at, own].astype(bf16)
            dweights = dot_nt(dattended, mixed_ref[k_at, columns(1, head)])
            dscores = (dweights * dscore_ref[head, q_at, :reach].astype(f32)).astype(bf16)
            dquery = dot_nn(dscores, mixed_ref[k_at, columns(3, head)])
            dpre_ref[q_at, columns(2, head)] = (
                dquery * slope_ref[q_at, columns(2, head)].astype(f32)
            ).astype(bf16)
            dvalue_ref[k_at, own] += dot_tn(weights_ref[head, q_at, :reach], dattended)
            dkey_ref[k_at, own] += dot_tn(dscores, mixed_ref[q_at, columns(2, head)])
    values, keys = pl.ds(inner, inner), pl.ds(3 * inner, inner)
    dpre_ref[:, values] = (dvalue_ref[...] * slope_ref[:, values].astype(f32)).astype(bf16)
    dpre_ref[:, keys] = (dkey_ref[...] * slope_ref[:, keys].astype(f32)).astype(bf16)

    @pl.loop(0, width // 256)
    def _(step):
        at = pl.ds(pl.multiple_of(step * 256, 256), 256)
        dnorm_ref[:, at] = dot_nt(dpre_ref[...], w_in_ref[at, :])

    @pl.loop(0, tokens // BLOCK)
    def _(step):
        at = pl.ds(pl.multiple_of(step * BLOCK, BLOCK), BLOCK)
        rows = rows_ref[at, :].astype(f32)
        rstd = rstd_ref[at, :]
        unit = (rows - mean_of(rows)) * rstd
        dunit = dnorm_ref[at, :]
        grads = rstd * (dunit - mean_of(dunit) - unit * mean_of(dunit * unit))
        normed_ref[at, :] = (grads + out_grad_ref[at, :].astype(f32)).astype(bf16)

    base = 0
    for ref in (near_ref, far_ref, slots_ref):
        count = ref.shape[0]
        pick = (
            lax.broadcasted_iota(jnp.int32, (count, tokens), 0) + base == place_ref[...]
        ).astype(bf16)
        base += count
        for half in range(2):
            at = pl.ds(half * (width // 2), width // 2)
            ref[:, at] = dot_nn(pick, normed_ref[:, at]).astype(bf16)


def layer(lengths, hot_table, fetched, w_in, w_out, out_grad, source, place):
    tokens, width = out_grad.shape
    inner = w_out.shape[0]
    heads = inner // HEAD
    half = hot_table.shape[0] // 2
    bf16, f32 = jnp.bfloat16, jnp.float32
    vmem = pl.BlockSpec(memory_space=pltpu.VMEM)
    reach = (BACK + 1) * BLOCK
    return pl.pallas_call(
        layer_kernel,
        out_shape=(
            jax.ShapeDtypeStruct((tokens, width), bf16),
            jax.ShapeDtypeStruct((half, width), bf16),
            jax.ShapeDtypeStruct((half, width), bf16),
            jax.ShapeDtypeStruct(fetched.shape, bf16),
        ),
        in_specs=[pl.BlockSpec(memory_space=pltpu.SMEM)] + [vmem] * 7,
        out_specs=(vmem,) * 4,
        scratch_shapes=[
            pltpu.VMEM((tokens, width), bf16),
            pltpu.VMEM((tokens, width), bf16),
            pltpu.VMEM((tokens, 1), f32),
            pltpu.VMEM((tokens, 4 * inner), bf16),
            pltpu.VMEM((tokens, 4 * inner), bf16),
            pltpu.VMEM((heads, tokens, reach), bf16),
            pltpu.VMEM((heads, tokens, reach), bf16),
            pltpu.VMEM((tokens, inner), f32),
            pltpu.VMEM((tokens, inner), f32),
            pltpu.VMEM((tokens, inner), f32),
            pltpu.VMEM((tokens, 4 * inner), bf16),
            pltpu.VMEM((tokens, width), f32),
        ],
        compiler_params=pltpu.CompilerParams(vmem_limit_bytes=48 * 1024 * 1024),
        cost_estimate=pl.CostEstimate(flops=8 * 10**9, bytes_accessed=12 * 10**6, transcendentals=0),
        name="layer",
    )(lengths, hot_table, fetched, w_in, w_out, out_grad, source, place)


def shift(groups, step):
    return [(g[i], g[(i + step) % len(g)]) for g in groups for i in range(len(g))]


CORE_GROUPS = [[2 * y, 2 * y + 1] for y in range(4)]
Y_GROUPS = [[2 * y + core for y in range(4)] for core in range(2)]
X_GROUPS = [[4 * z + x for x in range(4)] for z in range(8)]
Z_GROUPS = [[4 * z + x for z in range(8)] for x in range(4)]


def reduce_stage(chunks, axis, groups):
    total = chunks[0].astype(jnp.float32)
    arrived = [
        lax.ppermute(chunk, axis, shift(groups, k)) for k, chunk in enumerate(chunks) if k > 0
    ]
    for piece in arrived:
        total = total + piece.astype(jnp.float32)
    return total.astype(jnp.bfloat16)


def one_hot_rows(ids, rows):
    return (lax.iota(jnp.int32, rows)[:, None] == ids[None, :]).astype(jnp.bfloat16)


def on_device(
    hot_table, cold_table, w_in, w_out, seq_lengths, event_hot, event_index, cold_requests, out_grad
):
    table_count = lax.axis_size("table")
    cap_size = cold_requests.shape[1]
    slot_count = table_count * cap_size
    shard_rows = cold_table.shape[0]
    model_width = cold_table.shape[1]
    hot_rows = hot_table.shape[0]
    table_at, dp_at = lax.axis_index("table"), lax.axis_index("dp")
    y_at, core_at, x_at = table_at // 2, table_at % 2, dp_at % 4

    wanted = lax.all_to_all(cold_requests, "table", split_axis=0, concat_axis=0, tiled=True)
    wanted = wanted.reshape(slot_count)
    fetched = lax.all_to_all(
        cold_table[wanted].reshape(table_count, cap_size, model_width),
        "table",
        split_axis=0,
        concat_axis=0,
        tiled=True,
    ).reshape(slot_count, model_width)
    is_hot = event_hot == 1
    hot_dp, hot_t = event_index // 16, (event_index % 16) // 2
    hot_place = (
        (hot_t % 2 - core_at) % 2 * 256
        + (hot_t // 2 - y_at) % 4 * 64
        + (hot_dp % 4 - x_at) % 4 * 16
        + hot_dp // 4 * 2
        + event_index % 2
    )
    source = jnp.where(is_hot, event_index, event_index + hot_rows)
    place = jnp.where(is_hot, hot_place, event_index + hot_rows)
    layer_out, near_part, far_part, slot_part = layer(
        seq_lengths,
        hot_table,
        fetched,
        w_in,
        w_out,
        out_grad,
        source.reshape(-1, 1),
        place.reshape(1, -1),
    )
    hot_part = reduce_stage([near_part, far_part], "table", CORE_GROUPS)
    returned = lax.all_to_all(
        slot_part.reshape(table_count, cap_size, model_width),
        "table",
        split_axis=0,
        concat_axis=0,
        tiled=True,
    ).reshape(slot_count, model_width)
    hot_part = reduce_stage([hot_part[64 * k : 64 * k + 64] for k in range(4)], "table", Y_GROUPS)
    shard_place = (wanted // 16 % 4 - x_at) % 4 * 128 + wanted // 64 * 16 + wanted % 16
    shard_pick = one_hot_rows(shard_place, shard_rows)
    shard_grad = jnp.dot(shard_pick, returned, preferred_element_type=jnp.float32).astype(
        jnp.bfloat16
    )
    both = [
        jnp.concatenate([shard_grad[128 * k : 128 * k + 128], hot_part[16 * k : 16 * k + 16]])
        for k in range(4)
    ]
    both = reduce_stage(both, "dp", X_GROUPS)
    by_z = jnp.concatenate(
        [both[:128].reshape(8, 16, model_width), both[128:].reshape(8, 2, model_width)], axis=1
    )
    by_z = lax.all_to_all(
        by_z, "dp", split_axis=0, concat_axis=0, tiled=True, axis_index_groups=Z_GROUPS
    )
    summed = jnp.sum(by_z.astype(jnp.float32), axis=0)
    hot_sum = lax.all_gather(summed[16:], "table", axis=0, tiled=True)
    return (layer_out, hot_sum, summed[:16])


def solution(mesh):
    placed = (
        P(),
        P("table", None),
        P(),
        P(),
        P(("table", "dp"), None),
        P(("table", "dp")),
        P(("table", "dp")),
        P(("table", "dp"), None),
        P(("table", "dp"), None),
    )
    return jax.shard_map(
        on_device,
        mesh=mesh,
        in_specs=placed,
        out_specs=(P(("table", "dp"), None), P("dp", None), P(("table", "dp"), None)),
        check_vma=False,
    )
```

time: 164 us -> 126 us (0.77)
  matrix products: 35.7 us -> 0.42 us
  Pallas kernels: 0 us -> 21.9 us
  blocking collectives: 13 us -> 34.9 us
  local copies, waits for them, and re-layouts: 26.2 us -> 8.18 us
  other arithmetic: 15 us -> 2.77 us
  starting transfers between devices: 29.1 us -> 19.8 us
  waiting for transfers between devices: 42.2 us -> 35.6 us
    dot_general x12 -> x0, matrix products: 35.2 us -> none  [the longest x2 12.1 us: layer_forward(): jnp.dot(normed, w_in, preferred_element_type=jnp.float32)]
    all_to_all x0 -> x1, blocking collectives: none -> 21.9 us  [on_device(): lax.all_to_all(by_z, 'dp', split_axis=0, concat_axis=0, tiled=True, axis_...]
    pallas_call x0 -> x1, Pallas kernels: none -> 21.9 us  [layer(): pl.pallas_call(layer_kernel, out_shape=(jax.ShapeDtypeStruct((tokens, wid...]
    all_to_all x1 -> x0, waiting for transfers between devices: 11.4 us -> none  [on_device(): lax.all_to_all(by_z, 'dp', split_axis=0, concat_axis=0, tiled=True, axis_...]
    reshape x7 -> x1, local copies, waits for them, and re-layouts: 11.2 us -> 0.15 us  [on_device(): source.reshape(-1, 1)]
    all_to_all x1 -> x0, starting transfers between devices: 7.97 us -> none  [on_device(): lax.all_to_all(by_z, 'dp', split_axis=0, concat_axis=0, tiled=True, axis_...]
    gather x2 -> x0, local copies, waits for them, and re-layouts: 6.94 us -> none  [the longest x1 4.18 us: on_device(): hot_table[hot_index]]
    reduce_sum x7 -> x0, other arithmetic: 6.39 us -> none  [the longest x2 3.11 us: layer_norm(): centered = values - average]
  transfers between devices with their start and end apart: 11 -> 10, of which waited for: 9 -> 9; matrix products, arithmetic and copies ran while one was open for 8% -> 2% of each run, Pallas kernels for 0% -> 0%
where the time goes in v2:
time: 126 us; the launch traced here: 124 us
  waiting for transfers between devices  35.6 us (28%)
  blocking collectives  34.9 us (28%)
  Pallas kernels  21.9 us (17%)
  starting transfers between devices  19.8 us (16%)
  local copies, waits for them, and re-layouts  8.18 us (6%)
  other arithmetic  2.77 us (2%)
    all_to_all x1, blocking collectives, on_device(): lax.all_to_all(by_z, 'dp', split_axis=0, concat_axis=0, tiled=True, axis_...  21.9 us
    pallas_call x1, Pallas kernels, layer(): pl.pallas_call(layer_kernel, out_shape=(jax.ShapeDtypeStruct((tokens, wid...  21.9 us
    ppermute x7, waiting for transfers between devices, reduce_stage(): lax.ppermute(chunk, axis, shift(groups, k))  17.2 us
    all_gather x1, blocking collectives, on_device(): hot_sum = lax.all_gather(summed[16:], 'table', axis=0, tiled=True)  13 us
    ppermute x7, starting transfers between devices, reduce_stage(): lax.ppermute(chunk, axis, shift(groups, k))  8.34 us
    all_to_all x1, waiting for transfers between devices, on_device(): lax.all_to_all(slot_part.reshape(table_count, cap_size, model_width), 'ta...  7.35 us
    all_to_all x1, waiting for transfers between devices, on_device(): lax.all_to_all(cold_table[wanted].reshape(table_count, cap_size, model_wi...  5.87 us
    all_to_all x1, waiting for transfers between devices, on_device(): lax.all_to_all(cold_requests, 'table', split_axis=0, concat_axis=0, tiled...  5.19 us
  transfers between devices with their start and end apart: 10, of which 9 were waited for; matrix products, arithmetic and copies ran while one was open for 2% of the time, Pallas kernels for 0%

profile of v2, /device:TPU:2, one launch (start us, length us, event | category | flops | bytes accessed | tf_op | source)
XLA Modules:
  0.0 124.4 jit_solution(1864903759083299558)
XLA Ops:
  0.6 4.6 %all-to-all-start = ((s32[8,1,16]{2,1,0:T(1,128)}), s32[8,1,16]{2,1,0:T(1,128)S(1)}, u32[]{:S(2)}, u32[]{:S(2)}) async-start(s32[8,1,16]{2,1,0:T(1,128)} %bitcast.22), calls=%async_computation | async-start | bytes 8192 | tf_op jit(solution)/shard_map/all_to_all | solution.py:267
  5.3 5.2 %all-to-all-done = s32[8,1,16]{2,1,0:T(1,128)S(1)} async-done(((s32[8,1,16]{2,1,0:T(1,128)}), s32[8,1,16]{2,1,0:T(1,128)S(1)}, u32[]{:S(2)}, u32[]{:S(2)}) %all-to-all-start) | async-done | bytes 544 | tf_op jit(solution)/shard_map/all_to_all | solution.py:267
  11.7 1.6 %gather_fusion = bf16[128,1024]{1,0:T(8,128)(2,1)} fusion(bf16[512,1024]{1,0:T(8,128)(2,1)S(1)} %copy-done, s32[1024]{0:T(1024)S(1)} %pad_clamp_fusion), kind=kCustom, calls=%fused_computation | custom fusion | bytes 524800 | tf_op jit(solution)/shard_map/gather | solution.py:270
  13.3 3.4 %all-to-all-start.1 = ((bf16[8,16,1024]{2,1,0:T(8,128)(2,1)}), bf16[8,16,1024]{2,1,0:T(8,128)(2,1)S(1)}, u32[]{:S(2)}, u32[]{:S(2)}) async-start(bf16[8,16,1024]{2,1,0:T(8,128)(2,1)} %bitcast.3), calls=%async_computation.1 | async-start | bytes 524288 | tf_op jit(solution)/shard_map/all_to_all | solution.py:269
  16.7 0.7 add_select_fusion.11
  18.3 5.9 %all-to-all-done.1 = bf16[8,16,1024]{2,1,0:T(8,128)(2,1)S(1)} async-done(((bf16[8,16,1024]{2,1,0:T(8,128)(2,1)}), bf16[8,16,1024]{2,1,0:T(8,128)(2,1)S(1)}, u32[]{:S(2)}, u32[]{:S(2)}) %all-to-all-start.1) | async-done | bytes 262176 | tf_op jit(solution)/shard_map/all_to_all | solution.py:269
  24.2 1.2 copy-done.1
  25.4 1.2 copy-done.2
  26.6 1.2 copy-done.3
  28.5 21.9 %layer.1 = (bf16[512,1024]{1,0:T(8,128)(2,1)}, bf16[256,1024]{1,0:T(8,128)(2,1)S(1)}, bf16[256,1024]{1,0:T(8,128)(2,1)S(1)}, bf16[128,1024]{1,0:T(8,128)(2,1)}) custom-call(s32[1,8]{1,0:T(1,128)S(1)} %copy-done.4, bf16[512,1024]{1,0:T(8,128)(2,1)S(1)} %copy-done.1, bf16[128,1024]{1,0:T(8,128)(2,1)S(1)} %bitcast.16, bf16[1024,2048]{1,0:T(8,128)(2,1)} %w_in_ref.1, ...), custom_call_target="tpu_custom_call" | custom-call | flops 8000000000 | bytes 12000000 | tf_op jit(solution)/shard_map/layer/pallas_call | solution.py:201
  50.4 3.4 %all-to-all-start.2 = ((bf16[8,16,1024]{2,1,0:T(8,128)(2,1)}), bf16[8,16,1024]{2,1,0:T(8,128)(2,1)S(1)}, u32[]{:S(2)}, u32[]{:S(2)}) async-start(bf16[8,16,1024]{2,1,0:T(8,128)(2,1)} %bitcast.7), calls=%async_computation.2 | async-start | bytes 524288 | tf_op jit(solution)/shard_map/all_to_all | solution.py:298
  53.9 7.3 %all-to-all-done.2 = bf16[8,16,1024]{2,1,0:T(8,128)(2,1)S(1)} async-done(((bf16[8,16,1024]{2,1,0:T(8,128)(2,1)}), bf16[8,16,1024]{2,1,0:T(8,128)(2,1)S(1)}, u32[]{:S(2)}, u32[]{:S(2)}) %all-to-all-start.2) | async-done | bytes 262176 | tf_op jit(solution)/shard_map/all_to_all | solution.py:298
  62.6 2.7 %collective-permute-start.3 = (bf16[64,1024]{1,0:T(8,128)(2,1)S(1)}, bf16[64,1024]{1,0:T(8,128)(2,1)S(1)}, u32[]{:S(2)}, u32[]{:S(2)}) collective-permute-start(bf16[64,1024]{1,0:T(8,128)(2,1)S(1)} %get-tuple-element.18), channel_id=1, source_target_pairs={{0,192},{64,0},{128,64},{192,128},{32,224},{96,32},{160,96},{224,1... | collective-permute-start | bytes 393224 | tf_op jit(solution)/shard_map/ppermute | solution.py:244
  65.3 2.9 %collective-permute-done.1 = bf16[64,1024]{1,0:T(8,128)(2,1)S(1)} collective-permute-done((bf16[64,1024]{1,0:T(8,128)(2,1)S(1)}, bf16[64,1024]{1,0:T(8,128)(2,1)S(1)}, u32[]{:S(2)}, u32[]{:S(2)}) %collective-permute-start.1) | collective-permute-done | bytes 131104 | tf_op jit(solution)/shard_map/ppermute | solution.py:244
  68.2 2.0 %collective-permute-done.3 = bf16[64,1024]{1,0:T(8,128)(2,1)S(1)} collective-permute-done((bf16[64,1024]{1,0:T(8,128)(2,1)S(1)}, bf16[64,1024]{1,0:T(8,128)(2,1)S(1)}, u32[]{:S(2)}, u32[]{:S(2)}) %collective-permute-start.3) | collective-permute-done | bytes 131104 | tf_op jit(solution)/shard_map/ppermute | solution.py:244
  70.2 1.5 %collective-permute-done.2 = bf16[64,1024]{1,0:T(8,128)(2,1)S(1)} collective-permute-done((bf16[64,1024]{1,0:T(8,128)(2,1)S(1)}, bf16[64,1024]{1,0:T(8,128)(2,1)S(1)}, u32[]{:S(2)}, u32[]{:S(2)}) %collective-permute-start.2) | collective-permute-done | bytes 131104 | tf_op jit(solution)/shard_map/ppermute | solution.py:244
  71.9 1.6 %collective-permute-start.4 = (bf16[144,1024]{1,0:T(8,128)(2,1)S(1)}, bf16[144,1024]{1,0:T(8,128)(2,1)S(1)}, u32[]{:S(2)}, u32[]{:S(2)}) collective-permute-start(bf16[144,1024]{1,0:T(8,128)(2,1)S(1)} %pad_maximum_fusion.1), channel_id=1, source_target_pairs={{0,1},{1,2},{2,3},{3,0},{4,5},{5,6},{6,7},{7,4},{8,9},{9,10},{10,1... | collective-permute-start | bytes 884744 | tf_op jit(solution)/shard_map/ppermute | solution.py:244
  73.5 1.7 %collective-permute-start.5 = (bf16[144,1024]{1,0:T(8,128)(2,1)S(1)}, bf16[144,1024]{1,0:T(8,128)(2,1)S(1)}, u32[]{:S(2)}, u32[]{:S(2)}) collective-permute-start(bf16[144,1024]{1,0:T(8,128)(2,1)S(1)} %pad_maximum_fusion.2), channel_id=1, source_target_pairs={{0,2},{1,3},{2,0},{3,1},{4,6},{5,7},{6,4},{7,5},{8,10},{9,11},{10,... | collective-permute-start | bytes 884744 | tf_op jit(solution)/shard_map/ppermute | solution.py:244
  75.2 1.7 %collective-permute-start.6 = (bf16[144,1024]{1,0:T(8,128)(2,1)S(1)}, bf16[144,1024]{1,0:T(8,128)(2,1)S(1)}, u32[]{:S(2)}, u32[]{:S(2)}) collective-permute-start(bf16[144,1024]{1,0:T(8,128)(2,1)S(1)} %pad_maximum_fusion.3), channel_id=1, source_target_pairs={{0,3},{1,0},{2,1},{3,2},{4,7},{5,4},{6,5},{7,6},{8,11},{9,8},{10,9... | collective-permute-start | bytes 884744 | tf_op jit(solution)/shard_map/ppermute | solution.py:244
  76.9 4.8 %collective-permute-done.4 = bf16[144,1024]{1,0:T(8,128)(2,1)S(1)} collective-permute-done((bf16[144,1024]{1,0:T(8,128)(2,1)S(1)}, bf16[144,1024]{1,0:T(8,128)(2,1)S(1)}, u32[]{:S(2)}, u32[]{:S(2)}) %collective-permute-start.4) | collective-permute-done | bytes 294944 | tf_op jit(solution)/shard_map/ppermute | solution.py:244
  81.8 2.9 %collective-permute-done.5 = bf16[144,1024]{1,0:T(8,128)(2,1)S(1)} collective-permute-done((bf16[144,1024]{1,0:T(8,128)(2,1)S(1)}, bf16[144,1024]{1,0:T(8,128)(2,1)S(1)}, u32[]{:S(2)}, u32[]{:S(2)}) %collective-permute-start.5) | collective-permute-done | bytes 294944 | tf_op jit(solution)/shard_map/ppermute | solution.py:244
  84.7 3.0 %collective-permute-done.6 = bf16[144,1024]{1,0:T(8,128)(2,1)S(1)} collective-permute-done((bf16[144,1024]{1,0:T(8,128)(2,1)S(1)}, bf16[144,1024]{1,0:T(8,128)(2,1)S(1)}, u32[]{:S(2)}, u32[]{:S(2)}) %collective-permute-start.6) | collective-permute-done | bytes 294944 | tf_op jit(solution)/shard_map/ppermute | solution.py:244
  88.0 21.9 %all_to_all.24 = bf16[8,18,1024]{2,1,0:T(8,128)(2,1)S(1)} all-to-all(bf16[8,18,1024]{2,1,0:T(8,128)(2,1)S(1)} %pad_maximum_fusion), channel_id=1, replica_groups={{0,4,8,12,16,20,24,28},{1,5,9,13,17,21,25,29},{2,6,10,14,18,22,26,30},{..., dimensions={0} | all-to-all | bytes 589824 | tf_op jit(solution)/shard_map/all_to_all | solution.py:319
  110.7 13.0 %all-gather = f32[8,2,1024]{2,1,0:T(2,128)S(1)} all-gather(f32[1,2,1024]{2,1,0:T(2,128)S(1)} %slice_bitcast_fusion), channel_id=1, replica_groups=mesh['table'=8,'dp'=32] {'table'}, dimensions={0}, use_global_device_ids=true | all-gather | bytes 73728 | tf_op jit(solution)/shard_map/all_gather | solution.py:323
  (38 shorter events, 6.1 us)
Async XLA Ops:
  0.6 11.1 %copy-start = (bf16[512,1024]{1,0:T(8,128)(2,1)S(1)}, bf16[512,1024]{1,0:T(8,128)(2,1)}, u32[]{:S(2)}) copy-start(bf16[512,1024]{1,0:T(8,128)(2,1)} %param.10) | copy-start | bytes 3145732
  0.6 9.8 %all-to-all-start = ((s32[8,1,16]{2,1,0:T(1,128)}), s32[8,1,16]{2,1,0:T(1,128)S(1)}, u32[]{:S(2)}, u32[]{:S(2)}) async-start(s32[8,1,16]{2,1,0:T(1,128)} %bitcast.22), calls=%async_computation | async-start | bytes 8192 | tf_op jit(solution)/shard_map/all_to_all | solution.py:267
  13.3 10.9 %all-to-all-start.1 = ((bf16[8,16,1024]{2,1,0:T(8,128)(2,1)}), bf16[8,16,1024]{2,1,0:T(8,128)(2,1)S(1)}, u32[]{:S(2)}, u32[]{:S(2)}) async-start(bf16[8,16,1024]{2,1,0:T(8,128)(2,1)} %bitcast.3), calls=%async_computation.1 | async-start | bytes 524288 | tf_op jit(solution)/shard_map/all_to_all | solution.py:269
  24.2 1.2 copy-start.1
  25.4 1.2 copy-start.2
  26.6 1.2 copy-start.3
  27.9 0.7 copy-start.4
  50.4 11.3 %collective-permute-start = (bf16[256,1024]{1,0:T(8,128)(2,1)S(1)}, bf16[256,1024]{1,0:T(8,128)(2,1)S(1)}, u32[]{:S(2)}, u32[]{:S(2)}) collective-permute-start(bf16[256,1024]{1,0:T(8,128)(2,1)S(1)} %get-tuple-element.10), channel_id=1, source_target_pairs={{0,32},{32,0},{64,96},{96,64},{128,160},{160,128},{192,224},{224,1... | collective-permute-start | bytes 1572872 | tf_op jit(solution)/shard_map/ppermute | solution.py:244
  50.4 10.9 %all-to-all-start.2 = ((bf16[8,16,1024]{2,1,0:T(8,128)(2,1)}), bf16[8,16,1024]{2,1,0:T(8,128)(2,1)S(1)}, u32[]{:S(2)}, u32[]{:S(2)}) async-start(bf16[8,16,1024]{2,1,0:T(8,128)(2,1)} %bitcast.7), calls=%async_computation.2 | async-start | bytes 524288 | tf_op jit(solution)/shard_map/all_to_all | solution.py:298
  62.0 6.3 %collective-permute-start.1 = (bf16[64,1024]{1,0:T(8,128)(2,1)S(1)}, bf16[64,1024]{1,0:T(8,128)(2,1)S(1)}, u32[]{:S(2)}, u32[]{:S(2)}) collective-permute-start(bf16[64,1024]{1,0:T(8,128)(2,1)S(1)} %get-tuple-element.17), channel_id=1, source_target_pairs={{0,64},{64,128},{128,192},{192,0},{32,96},{96,160},{160,224},{224,... | collective-permute-start | bytes 393224 | tf_op jit(solution)/shard_map/ppermute | solution.py:244
  62.6 7.6 %collective-permute-start.3 = (bf16[64,1024]{1,0:T(8,128)(2,1)S(1)}, bf16[64,1024]{1,0:T(8,128)(2,1)S(1)}, u32[]{:S(2)}, u32[]{:S(2)}) collective-permute-start(bf16[64,1024]{1,0:T(8,128)(2,1)S(1)} %get-tuple-element.18), channel_id=1, source_target_pairs={{0,192},{64,0},{128,64},{192,128},{32,224},{96,32},{160,96},{224,1... | collective-permute-start | bytes 393224 | tf_op jit(solution)/shard_map/ppermute | solution.py:244
  65.3 6.5 %collective-permute-start.2 = (bf16[64,1024]{1,0:T(8,128)(2,1)S(1)}, bf16[64,1024]{1,0:T(8,128)(2,1)S(1)}, u32[]{:S(2)}, u32[]{:S(2)}) collective-permute-start(bf16[64,1024]{1,0:T(8,128)(2,1)S(1)} %get-tuple-element.19), channel_id=1, source_target_pairs={{0,128},{64,192},{128,0},{192,64},{32,160},{96,224},{160,32},{224,... | collective-permute-start | bytes 393224 | tf_op jit(solution)/shard_map/ppermute | solution.py:244
  71.9 9.9 %collective-permute-start.4 = (bf16[144,1024]{1,0:T(8,128)(2,1)S(1)}, bf16[144,1024]{1,0:T(8,128)(2,1)S(1)}, u32[]{:S(2)}, u32[]{:S(2)}) collective-permute-start(bf16[144,1024]{1,0:T(8,128)(2,1)S(1)} %pad_maximum_fusion.1), channel_id=1, source_target_pairs={{0,1},{1,2},{2,3},{3,0},{4,5},{5,6},{6,7},{7,4},{8,9},{9,10},{10,1... | collective-permute-start | bytes 884744 | tf_op jit(solution)/shard_map/ppermute | solution.py:244
  73.5 11.2 %collective-permute-start.5 = (bf16[144,1024]{1,0:T(8,128)(2,1)S(1)}, bf16[144,1024]{1,0:T(8,128)(2,1)S(1)}, u32[]{:S(2)}, u32[]{:S(2)}) collective-permute-start(bf16[144,1024]{1,0:T(8,128)(2,1)S(1)} %pad_maximum_fusion.2), channel_id=1, source_target_pairs={{0,2},{1,3},{2,0},{3,1},{4,6},{5,7},{6,4},{7,5},{8,10},{9,11},{10,... | collective-permute-start | bytes 884744 | tf_op jit(solution)/shard_map/ppermute | solution.py:244
  75.2 12.5 %collective-permute-start.6 = (bf16[144,1024]{1,0:T(8,128)(2,1)S(1)}, bf16[144,1024]{1,0:T(8,128)(2,1)S(1)}, u32[]{:S(2)}, u32[]{:S(2)}) collective-permute-start(bf16[144,1024]{1,0:T(8,128)(2,1)S(1)} %pad_maximum_fusion.3), channel_id=1, source_target_pairs={{0,3},{1,0},{2,1},{3,2},{4,7},{5,4},{6,5},{7,6},{8,11},{9,8},{10,9... | collective-permute-start | bytes 884744 | tf_op jit(solution)/shard_map/ppermute | solution.py:244

commit v3 on v2

--- a/solution.py
+++ b/solution.py
@@ -33,19 +33,47 @@
     return lax.dot_general(a, b, (((0,), (0,)), ((), ())), preferred_element_type=jnp.float32)
 
 
+def pick_kernel(wanted_ref, table_ref, rows_ref):
+    takers, cap = wanted_ref.shape
+    shard_rows, count = table_ref.shape[0], takers * cap
+    wide = jnp.concatenate([wanted_ref[...]] * takers, axis=1)
+    taker = lax.broadcasted_iota(jnp.int32, (takers, count), 0)
+    lane = lax.broadcasted_iota(jnp.int32, (takers, count), 1)
+    own = (lane >= taker * cap) & (lane < taker * cap + cap)
+    flat = jnp.sum(jnp.where(own, wide, 0), axis=0, keepdims=True)
+    pick = (lax.broadcasted_iota(jnp.int32, (shard_rows, count), 0) == flat).astype(jnp.bfloat16)
+    rows_ref[...] = dot_tn(pick, table_ref[...]).astype(jnp.bfloat16)
+
+
+def pick_rows(wanted, table):
+    vmem = pl.BlockSpec(memory_space=pltpu.VMEM)
+    return pl.pallas_call(
+        pick_kernel,
+        out_shape=jax.ShapeDtypeStruct((wanted.size, table.shape[1]), jnp.bfloat16),
+        in_specs=[vmem] * 2,
+        out_specs=vmem,
+        compiler_params=pltpu.CompilerParams(vmem_limit_bytes=4 * 1024 * 1024),
+        name="pick_rows",
+    )(wanted, table)
+
+
 def layer_kernel(
     lengths_ref,
+    fetched_ref,
+    source_ref,
+    place_ref,
+    hot_hbm,
+    w_in_hbm,
+    w_out_hbm,
+    out_grad_hbm,
+    layer_out_hbm,
+    near_ref,
+    far_ref,
     hot_ref,
-    fetched_ref,
     w_in_ref,
     w_out_ref,
     out_grad_ref,
-    source_ref,
-    place_ref,
     layer_out_ref,
-    near_ref,
-    far_ref,
-    slots_ref,
     rows_ref,
     normed_ref,
     rstd_ref,
@@ -58,12 +86,22 @@
     dkey_ref,
     dpre_ref,
     dnorm_ref,
+    sems,
 ):
     tokens, width = rows_ref.shape
     hot_rows, slot_count = hot_ref.shape[0], fetched_ref.shape[0]
     inner = w_out_ref.shape[0]
     heads = inner // HEAD
     bf16, f32 = jnp.bfloat16, jnp.float32
+
+    hot_copy = pltpu.make_async_copy(hot_hbm, hot_ref, sems.at[0])
+    w_in_copy = pltpu.make_async_copy(w_in_hbm, w_in_ref, sems.at[1])
+    w_out_copy = pltpu.make_async_copy(w_out_hbm, w_out_ref, sems.at[2])
+    out_grad_copy = pltpu.make_async_copy(out_grad_hbm, out_grad_ref, sems.at[3])
+    layer_out_copy = pltpu.make_async_copy(layer_out_ref, layer_out_hbm, sems.at[4])
+    for copy in (hot_copy, w_in_copy, w_out_copy, out_grad_copy):
+        copy.start()
+    hot_copy.wait()
 
     @pl.loop(0, tokens // BLOCK)
     def _(step):
@@ -79,6 +117,8 @@
         rows_ref[at, :] = rows.astype(bf16)
         normed_ref[at, :] = (centered * rstd).astype(bf16)
         rstd_ref[at, :] = rstd
+
+    w_in_copy.wait()
 
     @pl.loop(0, 4 * inner // 256)
     def _(step):
@@ -125,6 +165,9 @@
                 weights, mixed_ref[k_at, columns(1, head)]
             )
 
+    w_out_copy.wait()
+    out_grad_copy.wait()
+
     for block in range(tokens // 256):
         at = pl.ds(block * 256, 256)
         attended = attended_ref[at, :]
@@ -140,6 +183,8 @@
         dpre_ref[at, :inner] = (dmerged * unit * slope_ref[at, :inner].astype(f32)).astype(bf16)
         dunit = dmerged * gate
         attended_ref[at, :] = rstd * (dunit - mean_of(dunit) - unit * mean_of(dunit * unit))
+
+    layer_out_copy.start()
 
     dvalue_ref[...] = jnp.zeros_like(dvalue_ref)
     dkey_ref[...] = jnp.zeros_like(dkey_ref)
@@ -171,32 +216,31 @@
     @pl.loop(0, tokens // BLOCK)
     def _(step):
         at = pl.ds(pl.multiple_of(step * BLOCK, BLOCK), BLOCK)
-        rows = rows_ref[at, :].astype(f32)
         rstd = rstd_ref[at, :]
-        unit = (rows - mean_of(rows)) * rstd
+        unit = normed_ref[at, :].astype(f32)
         dunit = dnorm_ref[at, :]
         grads = rstd * (dunit - mean_of(dunit) - unit * mean_of(dunit * unit))
         normed_ref[at, :] = (grads + out_grad_ref[at, :].astype(f32)).astype(bf16)
 
-    base = 0
-    for ref in (near_ref, far_ref, slots_ref):
-        count = ref.shape[0]
+    half = near_ref.shape[0]
+    for base, ref in ((half, far_ref), (0, near_ref)):
         pick = (
-            lax.broadcasted_iota(jnp.int32, (count, tokens), 0) + base == place_ref[...]
+            lax.broadcasted_iota(jnp.int32, (half, tokens), 0) + base == place_ref[...]
         ).astype(bf16)
-        base += count
-        for half in range(2):
-            at = pl.ds(half * (width // 2), width // 2)
+        for part in range(2):
+            at = pl.ds(part * (width // 2), width // 2)
             ref[:, at] = dot_nn(pick, normed_ref[:, at]).astype(bf16)
+    layer_out_copy.wait()
 
 
 def layer(lengths, hot_table, fetched, w_in, w_out, out_grad, source, place):
     tokens, width = out_grad.shape
     inner = w_out.shape[0]
     heads = inner // HEAD
-    half = hot_table.shape[0] // 2
+    half = (hot_table.shape[0] + fetched.shape[0]) // 2
     bf16, f32 = jnp.bfloat16, jnp.float32
     vmem = pl.BlockSpec(memory_space=pltpu.VMEM)
+    hbm = pl.BlockSpec(memory_space=pl.ANY)
     reach = (BACK + 1) * BLOCK
     return pl.pallas_call(
         layer_kernel,
@@ -204,11 +248,15 @@
             jax.ShapeDtypeStruct((tokens, width), bf16),
             jax.ShapeDtypeStruct((half, width), bf16),
             jax.ShapeDtypeStruct((half, width), bf16),
-            jax.ShapeDtypeStruct(fetched.shape, bf16),
         ),
-        in_specs=[pl.BlockSpec(memory_space=pltpu.SMEM)] + [vmem] * 7,
-        out_specs=(vmem,) * 4,
+        in_specs=[pl.BlockSpec(memory_space=pltpu.SMEM)] + [vmem] * 3 + [hbm] * 4,
+        out_specs=(hbm, vmem, vmem),
         scratch_shapes=[
+            pltpu.VMEM(hot_table.shape, bf16),
+            pltpu.VMEM(w_in.shape, bf16),
+            pltpu.VMEM(w_out.shape, bf16),
+            pltpu.VMEM((tokens, width), bf16),
+            pltpu.VMEM((tokens, width), bf16),
             pltpu.VMEM((tokens, width), bf16),
             pltpu.VMEM((tokens, width), bf16),
             pltpu.VMEM((tokens, 1), f32),
@@ -221,11 +269,65 @@
             pltpu.VMEM((tokens, inner), f32),
             pltpu.VMEM((tokens, 4 * inner), bf16),
             pltpu.VMEM((tokens, width), f32),
+            pltpu.SemaphoreType.DMA((5,)),
         ],
-        compiler_params=pltpu.CompilerParams(vmem_limit_bytes=48 * 1024 * 1024),
+        compiler_params=pltpu.CompilerParams(vmem_limit_bytes=58 * 1024 * 1024),
         cost_estimate=pl.CostEstimate(flops=8 * 10**9, bytes_accessed=12 * 10**6, transcendentals=0),
         name="layer",
-    )(lengths, hot_table, fetched, w_in, w_out, out_grad, source, place)
+    )(lengths, fetched, source, place, hot_table, w_in, w_out, out_grad)
+
+
+def core_sums_kernel(near_ref, got_ref, *out_refs):
+    slots = near_ref.shape[0] // 5
+    hot = near_ref.shape[0] - slots
+    for k in range(4):
+        piece = pl.ds(k * slots // 4 + hot, slots // 4)
+        out_refs[k][: slots // 4, :] = near_ref[piece, :]
+        out_refs[k][slots // 4 :, :] = got_ref[piece, :]
+    for k in range(4):
+        piece = pl.ds(k * hot // 4, hot // 4)
+        total = near_ref[piece, :].astype(jnp.float32) + got_ref[piece, :].astype(jnp.float32)
+        out_refs[4 + k][...] = total.astype(jnp.bfloat16)
+
+
+def core_sums(near, got):
+    size, width = near.shape[0] // 5, near.shape[1]
+    vmem = pl.BlockSpec(memory_space=pltpu.VMEM)
+    out = pl.pallas_call(
+        core_sums_kernel,
+        out_shape=[jax.ShapeDtypeStruct((size // 2, width), jnp.bfloat16)] * 4
+        + [jax.ShapeDtypeStruct((size, width), jnp.bfloat16)] * 4,
+        in_specs=[vmem] * 2,
+        out_specs=[vmem] * 8,
+        compiler_params=pltpu.CompilerParams(vmem_limit_bytes=8 * 1024 * 1024),
+        name="core_sums",
+    )(near, got)
+    return out[:4], out[4:]
+
+
+def shard_sums_kernel(place_ref, own_ref, first_ref, second_ref, third_ref, *out_refs):
+    rows = out_refs[0].shape[0]
+    slots = jnp.concatenate(
+        [own_ref[...], first_ref[...], second_ref[...], third_ref[...]], axis=0
+    )
+    for k, ref in enumerate(out_refs):
+        pick = (
+            lax.broadcasted_iota(jnp.int32, (rows, slots.shape[0]), 0) + k * rows == place_ref[...]
+        ).astype(jnp.bfloat16)
+        ref[...] = dot_nn(pick, slots).astype(jnp.bfloat16)
+
+
+def shard_sums(place, pieces, shard_rows):
+    width = pieces[0].shape[1]
+    vmem = pl.BlockSpec(memory_space=pltpu.VMEM)
+    return pl.pallas_call(
+        shard_sums_kernel,
+        out_shape=[jax.ShapeDtypeStruct((shard_rows // 4, width), jnp.bfloat16)] * 4,
+        in_specs=[vmem] * 5,
+        out_specs=[vmem] * 4,
+        compiler_params=pltpu.CompilerParams(vmem_limit_bytes=4 * 1024 * 1024),
+        name="shard_sums",
+    )(place, *pieces)
 
 
 def shift(groups, step):
@@ -238,18 +340,16 @@
 Z_GROUPS = [[4 * z + x for z in range(8)] for x in range(4)]
 
 
-def reduce_stage(chunks, axis, groups):
-    total = chunks[0].astype(jnp.float32)
-    arrived = [
-        lax.ppermute(chunk, axis, shift(groups, k)) for k, chunk in enumerate(chunks) if k > 0
+def exchange(chunks, axis, groups):
+    return [
+        chunk if k == 0 else lax.ppermute(chunk, axis, shift(groups, k))
+        for k, chunk in enumerate(chunks)
     ]
-    for piece in arrived:
-        total = total + piece.astype(jnp.float32)
-    return total.astype(jnp.bfloat16)
-
-
-def one_hot_rows(ids, rows):
-    return (lax.iota(jnp.int32, rows)[:, None] == ids[None, :]).astype(jnp.bfloat16)
+
+
+def add_up(pieces):
+    here, back_1, back_2, back_3 = [piece.astype(jnp.float32) for piece in pieces]
+    return (here + back_2) + (back_1 + back_3)
 
 
 def on_device(
@@ -265,26 +365,34 @@
     y_at, core_at, x_at = table_at // 2, table_at % 2, dp_at % 4
 
     wanted = lax.all_to_all(cold_requests, "table", split_axis=0, concat_axis=0, tiled=True)
-    wanted = wanted.reshape(slot_count)
     fetched = lax.all_to_all(
-        cold_table[wanted].reshape(table_count, cap_size, model_width),
+        pick_rows(wanted, cold_table).reshape(table_count, cap_size, model_width),
         "table",
         split_axis=0,
         concat_axis=0,
         tiled=True,
     ).reshape(slot_count, model_width)
+    wanted = wanted.reshape(slot_count)
     is_hot = event_hot == 1
+
     hot_dp, hot_t = event_index // 16, (event_index % 16) // 2
     hot_place = (
-        (hot_t % 2 - core_at) % 2 * 256
-        + (hot_t // 2 - y_at) % 4 * 64
-        + (hot_dp % 4 - x_at) % 4 * 16
-        + hot_dp // 4 * 2
+        (hot_t % 2 - core_at) % 2 * 320
+        + (hot_dp % 4 - x_at) % 4 * 64
+        + hot_dp // 4 * 8
+        + hot_t // 2 * 2
         + event_index % 2
     )
+    slot_t = event_index // 16
+    slot_place = (
+        (slot_t % 2 - core_at) % 2 * 320
+        + 256
+        + (slot_t // 2 - y_at) % 4 * 16
+        + event_index % 16
+    )
     source = jnp.where(is_hot, event_index, event_index + hot_rows)
-    place = jnp.where(is_hot, hot_place, event_index + hot_rows)
-    layer_out, near_part, far_part, slot_part = layer(
+    place = jnp.where(is_hot, hot_place, slot_place)
+    layer_out, near, far = layer(
         seq_lengths,
         hot_table,
         fetched,
@@ -294,34 +402,35 @@
         source.reshape(-1, 1),
         place.reshape(1, -1),
     )
-    hot_part = reduce_stage([near_part, far_part], "table", CORE_GROUPS)
-    returned = lax.all_to_all(
-        slot_part.reshape(table_count, cap_size, model_width),
-        "table",
-        split_axis=0,
-        concat_axis=0,
-        tiled=True,
-    ).reshape(slot_count, model_width)
-    hot_part = reduce_stage([hot_part[64 * k : 64 * k + 64] for k in range(4)], "table", Y_GROUPS)
+    got = lax.ppermute(far, "table", shift(CORE_GROUPS, 1))
+    slot_chunks, hot_chunks = core_sums(near, got)
+    pieces = exchange(slot_chunks, "table", Y_GROUPS)
+    hot_part = add_up(exchange(hot_chunks, "dp", X_GROUPS))
     shard_place = (wanted // 16 % 4 - x_at) % 4 * 128 + wanted // 64 * 16 + wanted % 16
-    shard_pick = one_hot_rows(shard_place, shard_rows)
-    shard_grad = jnp.dot(shard_pick, returned, preferred_element_type=jnp.float32).astype(
-        jnp.bfloat16
-    )
-    both = [
-        jnp.concatenate([shard_grad[128 * k : 128 * k + 128], hot_part[16 * k : 16 * k + 16]])
-        for k in range(4)
-    ]
-    both = reduce_stage(both, "dp", X_GROUPS)
-    by_z = jnp.concatenate(
-        [both[:128].reshape(8, 16, model_width), both[128:].reshape(8, 2, model_width)], axis=1
-    )
-    by_z = lax.all_to_all(
-        by_z, "dp", split_axis=0, concat_axis=0, tiled=True, axis_index_groups=Z_GROUPS
-    )
-    summed = jnp.sum(by_z.astype(jnp.float32), axis=0)
-    hot_sum = lax.all_gather(summed[16:], "table", axis=0, tiled=True)
-    return (layer_out, hot_sum, summed[:16])
+    back = (y_at - lax.iota(jnp.int32, 4)) % 4
+    cores = (core_at + lax.iota(jnp.int32, 2)) % 2
+    arriving = (back[:, None] * 2 + cores[None, :]).reshape(table_count)
+    shard_place = shard_place.reshape(table_count, cap_size)[arriving].reshape(1, slot_count)
+    cold_chunks = shard_sums(shard_place, pieces, shard_rows)
+    cold_pieces = exchange(cold_chunks, "dp", X_GROUPS)
+
+    def over_z(rows):
+        by_z = rows.astype(jnp.bfloat16).reshape(8, -1, model_width)
+        by_z = lax.all_to_all(
+            by_z, "dp", split_axis=0, concat_axis=0, tiled=True, axis_index_groups=Z_GROUPS
+        )
+        return jnp.sum(by_z.astype(jnp.float32), axis=0)
+
+    hot_sum = over_z(hot_part)
+    cold_sum = over_z(add_up(cold_pieces))
+    hot_sum = add_up(exchange([hot_sum] * 4, "table", Y_GROUPS)).reshape(4, 1, 2, model_width)
+    other = lax.ppermute(hot_sum, "table", shift(CORE_GROUPS, 1))
+    ordered = jnp.where(
+        core_at == 0,
+        jnp.concatenate([hot_sum, other], axis=1),
+        jnp.concatenate([other, hot_sum], axis=1),
+    )
+    return (layer_out, ordered.reshape(16, model_width), cold_sum)
 
 
 def solution(mesh):

time: 126 us -> 104 us (0.83)
  the two profiles are of different devices: /device:TPU:2 before, /device:TPU:6 now
where the time goes in v3:
time: 104 us; the launch traced here: 103 us
  starting transfers between devices  36.3 us (35%)
  waiting for transfers between devices  31.9 us (31%)
  Pallas kernels  24.3 us (23%)
  local copies, waits for them, and re-layouts  5.27 us (5%)
  other arithmetic  4.44 us (4%)
    pallas_call x1, Pallas kernels, layer(): pl.pallas_call(layer_kernel, out_shape=(jax.ShapeDtypeStruct((tokens, wid...  22.6 us
    ppermute x12, starting transfers between devices, exchange(): lax.ppermute(chunk, axis, shift(groups, k))  16.3 us
    all_to_all x2, starting transfers between devices, over_z(): lax.all_to_all(by_z, 'dp', split_axis=0, concat_axis=0, tiled=True, axis_...  11.9 us
    ppermute x12, waiting for transfers between devices, exchange(): lax.ppermute(chunk, axis, shift(groups, k))  9.77 us
    all_to_all x2, waiting for transfers between devices, over_z(): lax.all_to_all(by_z, 'dp', split_axis=0, concat_axis=0, tiled=True, axis_...  9.08 us
    all_to_all x1, waiting for transfers between devices, on_device(): lax.all_to_all(cold_requests, 'table', split_axis=0, concat_axis=0, tiled...  5.19 us
    all_to_all x1, waiting for transfers between devices, on_device(): lax.all_to_all(pick_rows(wanted, cold_table).reshape(table_count, cap_siz...  4.59 us
    all_to_all x1, starting transfers between devices, on_device(): lax.all_to_all(cold_requests, 'table', split_axis=0, concat_axis=0, tiled...  4.48 us
  transfers between devices with their start and end apart: 18, of which 9 were waited for; matrix products, arithmetic and copies ran while one was open for 6% of the time, Pallas kernels for 0%

profile of v3, /device:TPU:6, one launch (start us, length us, event | category | flops | bytes accessed | tf_op | source)
XLA Modules:
  0.0 103.0 jit_solution(3310809819187451398)
XLA Ops:
  0.6 4.5 %all-to-all-start = ((s32[8,1,16]{2,1,0:T(1,128)}), s32[8,1,16]{2,1,0:T(1,128)S(1)}, u32[]{:S(2)}, u32[]{:S(2)}) async-start(s32[8,1,16]{2,1,0:T(1,128)} %bitcast.17), calls=%async_computation | async-start | bytes 8192 | tf_op jit(solution)/shard_map/all_to_all | solution.py:367
  5.1 5.2 %all-to-all-done = s32[8,1,16]{2,1,0:T(1,128)S(1)} async-done(((s32[8,1,16]{2,1,0:T(1,128)}), s32[8,1,16]{2,1,0:T(1,128)S(1)}, u32[]{:S(2)}, u32[]{:S(2)}) %all-to-all-start) | async-done | bytes 544 | tf_op jit(solution)/shard_map/all_to_all | solution.py:367
  10.3 1.2 %copy-done = bf16[512,1024]{1,0:T(8,128)(2,1)S(1)} copy-done((bf16[512,1024]{1,0:T(8,128)(2,1)S(1)}, bf16[512,1024]{1,0:T(8,128)(2,1)}, u32[]{:S(2)}) %copy-start) | copy-done | bytes 1048600
  11.5 1.1 %pick_rows.1 = bf16[128,1024]{1,0:T(8,128)(2,1)} custom-call(s32[8,16]{1,0:T(8,128)S(1)} %bitcast.13, bf16[512,1024]{1,0:T(8,128)(2,1)S(1)} %copy-done), custom_call_target="tpu_custom_call" | custom-call | tf_op jit(solution)/shard_map/pick_rows/pallas_call | solution.py:50
  12.6 3.4 %all-to-all-start.1 = ((bf16[8,16,1024]{2,1,0:T(8,128)(2,1)}), bf16[8,16,1024]{2,1,0:T(8,128)(2,1)S(1)}, u32[]{:S(2)}, u32[]{:S(2)}) async-start(bf16[8,16,1024]{2,1,0:T(8,128)(2,1)} %bitcast.3), calls=%async_computation.1 | async-start | bytes 524288 | tf_op jit(solution)/shard_map/all_to_all | solution.py:368
  16.1 1.3 %fusion.21 = (s32[512]{0:T(512)}, pred[512]{0:T(512)(128)(4,1)S(1)}) fusion(s32[512]{0:T(512)} %param.15, s32[]{:T(128)S(6)} %select_n.164, s32[]{:T(128)S(6)} %select_n.156, s32[]{:T(128)S(6)} %select_n.152, s32[512]{0:T(512)} %param.14), kind=kLoop, calls=%fused_computation.87 | loop fusion | flops 80384 | bytes 6668 | tf_op jit(solution)/shard_map/jit(_where)/select_n | solution.py:394
  18.9 4.6 %all-to-all-done.1 = bf16[8,16,1024]{2,1,0:T(8,128)(2,1)S(1)} async-done(((bf16[8,16,1024]{2,1,0:T(8,128)(2,1)}), bf16[8,16,1024]{2,1,0:T(8,128)(2,1)S(1)}, u32[]{:S(2)}, u32[]{:S(2)}) %all-to-all-start.1) | async-done | bytes 262176 | tf_op jit(solution)/shard_map/all_to_all | solution.py:368
  24.2 22.6 %layer.1 = (bf16[512,1024]{1,0:T(8,128)(2,1)}, bf16[320,1024]{1,0:T(8,128)(2,1)}, bf16[320,1024]{1,0:T(8,128)(2,1)}) custom-call(s32[1,8]{1,0:T(1,128)} %lengths_ref.1, bf16[128,1024]{1,0:T(8,128)(2,1)} %bitcast.15, s32[512,1]{1,0:T(8,128)} %copy.14.source_ref, s32[1,512]{1,0:T(1,128)} %bitcast.18, bf16[512,1024]{1,0:T(8,128)(2,1)} %hot_hbm.1, ...), custom_call_target="tpu_custom_call" | custom-call | flops 8000000000 | bytes 12000000 | tf_op jit(solution)/shard_map/layer/pallas_call | solution.py:245
  47.1 2.1 %collective-permute-done.got_ref = bf16[320,1024]{1,0:T(8,128)(2,1)S(1)} collective-permute-done((bf16[320,1024]{1,0:T(8,128)(2,1)}, bf16[320,1024]{1,0:T(8,128)(2,1)S(1)}, u32[]{:S(2)}, u32[]{:S(2)}) %collective-permute-start) | collective-permute-done | bytes 655392 | tf_op jit(solution)/shard_map/ppermute | solution.py:405
  49.2 1.1 %copy-done.1 = bf16[320,1024]{1,0:T(8,128)(2,1)S(1)} copy-done((bf16[320,1024]{1,0:T(8,128)(2,1)S(1)}, bf16[320,1024]{1,0:T(8,128)(2,1)}, u32[]{:S(2)}) %copy-start.1) | copy-done | bytes 655384
  51.2 2.0 %collective-permute-start.9 = (bf16[32,1024]{1,0:T(8,128)(2,1)S(1)}, bf16[32,1024]{1,0:T(8,128)(2,1)S(1)}, u32[]{:S(2)}, u32[]{:S(2)}) collective-permute-start(bf16[32,1024]{1,0:T(8,128)(2,1)S(1)} %get-tuple-element.27), channel_id=1, source_target_pairs={{0,128},{64,192},{128,0},{192,64},{32,160},{96,224},{160,32},{224,... | collective-permute-start | bytes 196616 | tf_op jit(solution)/shard_map/ppermute | solution.py:345
  53.2 0.9 collective-permute-start.10
  54.1 1.4 %collective-permute-start.1 = (bf16[64,1024]{1,0:T(8,128)(2,1)S(1)}, bf16[64,1024]{1,0:T(8,128)(2,1)S(1)}, u32[]{:S(2)}, u32[]{:S(2)}) collective-permute-start(bf16[64,1024]{1,0:T(8,128)(2,1)S(1)} %get-tuple-element.22), channel_id=1, source_target_pairs={{0,2},{1,3},{2,0},{3,1},{4,6},{5,7},{6,4},{7,5},{8,10},{9,11},{10,... | collective-permute-start | bytes 393224 | tf_op jit(solution)/shard_map/ppermute | solution.py:345
  55.5 2.1 %collective-permute-start.2 = (bf16[64,1024]{1,0:T(8,128)(2,1)S(1)}, bf16[64,1024]{1,0:T(8,128)(2,1)S(1)}, u32[]{:S(2)}, u32[]{:S(2)}) collective-permute-start(bf16[64,1024]{1,0:T(8,128)(2,1)S(1)} %get-tuple-element.23), channel_id=1, source_target_pairs={{0,1},{1,2},{2,3},{3,0},{4,5},{5,6},{6,7},{7,4},{8,9},{9,10},{10,1... | collective-permute-start | bytes 393224 | tf_op jit(solution)/shard_map/ppermute | solution.py:345
  59.2 1.7 %collective-permute-start.11 = (bf16[128,1024]{1,0:T(8,128)(2,1)S(1)}, bf16[128,1024]{1,0:T(8,128)(2,1)S(1)}, u32[]{:S(2)}, u32[]{:S(2)}) collective-permute-start(bf16[128,1024]{1,0:T(8,128)(2,1)S(1)} %get-tuple-element.30), channel_id=1, source_target_pairs={{0,2},{1,3},{2,0},{3,1},{4,6},{5,7},{6,4},{7,5},{8,10},{9,11},{10,... | collective-permute-start | bytes 786440 | tf_op jit(solution)/shard_map/ppermute | solution.py:345
  60.9 1.6 %collective-permute-start.12 = (bf16[128,1024]{1,0:T(8,128)(2,1)S(1)}, bf16[128,1024]{1,0:T(8,128)(2,1)S(1)}, u32[]{:S(2)}, u32[]{:S(2)}) collective-permute-start(bf16[128,1024]{1,0:T(8,128)(2,1)S(1)} %get-tuple-element.31), channel_id=1, source_target_pairs={{0,1},{1,2},{2,3},{3,0},{4,5},{5,6},{6,7},{7,4},{8,9},{9,10},{10,1... | collective-permute-start | bytes 786440 | tf_op jit(solution)/shard_map/ppermute | solution.py:345
  63.0 7.2 %collective-permute-done.3 = bf16[64,1024]{1,0:T(8,128)(2,1)S(1)} collective-permute-done((bf16[64,1024]{1,0:T(8,128)(2,1)S(1)}, bf16[64,1024]{1,0:T(8,128)(2,1)S(1)}, u32[]{:S(2)}, u32[]{:S(2)}) %collective-permute-start.3) | collective-permute-done | bytes 131104 | tf_op jit(solution)/shard_map/ppermute | solution.py:345
  70.9 8.5 %all-to-all-start.2 = ((bf16[8,8,1024]{2,1,0:T(8,128)(2,1)}), bf16[8,8,1024]{2,1,0:T(8,128)(2,1)S(1)}, u32[]{:S(2)}, u32[]{:S(2)}) async-start(bf16[8,8,1024]{2,1,0:T(8,128)(2,1)} %fusion), calls=%async_computation.2 | async-start | bytes 262144 | tf_op jit(solution)/shard_map/all_to_all | solution.py:419
  80.2 8.3 %all-to-all-done.2 = bf16[8,8,1024]{2,1,0:T(8,128)(2,1)S(1)} async-done(((bf16[8,8,1024]{2,1,0:T(8,128)(2,1)}), bf16[8,8,1024]{2,1,0:T(8,128)(2,1)S(1)}, u32[]{:S(2)}, u32[]{:S(2)}) %all-to-all-start.2) | async-done | bytes 131104 | tf_op jit(solution)/shard_map/all_to_all | solution.py:419
  88.5 3.4 %all-to-all-start.3 = ((bf16[8,16,1024]{2,1,0:T(8,128)(2,1)}), bf16[8,16,1024]{2,1,0:T(8,128)(2,1)S(1)}, u32[]{:S(2)}, u32[]{:S(2)}) async-start(bf16[8,16,1024]{2,1,0:T(8,128)(2,1)} %bitcast.9), calls=%async_computation.3 | async-start | bytes 524288 | tf_op jit(solution)/shard_map/all_to_all | solution.py:419
  92.1 2.0 %collective-permute-start.5 = (f32[8,1024]{1,0:T(8,128)S(1)}, f32[8,1024]{1,0:T(8,128)S(1)}, u32[]{:S(2)}, u32[]{:S(2)}) collective-permute-start(f32[8,1024]{1,0:T(8,128)S(1)} %convert_reduce_fusion.1), channel_id=1, source_target_pairs={{0,64},{64,128},{128,192},{192,0},{32,96},{96,160},{160,224},{224,... | collective-permute-start | bytes 98312 | tf_op jit(solution)/shard_map/ppermute | solution.py:345
  94.1 2.9 %collective-permute-start.4 = (f32[8,1024]{1,0:T(8,128)S(1)}, f32[8,1024]{1,0:T(8,128)S(1)}, u32[]{:S(2)}, u32[]{:S(2)}) collective-permute-start(f32[8,1024]{1,0:T(8,128)S(1)} %convert_reduce_fusion.1), channel_id=1, source_target_pairs={{0,128},{64,192},{128,0},{192,64},{32,160},{96,224},{160,32},{224,... | collective-permute-start | bytes 98312 | tf_op jit(solution)/shard_map/ppermute | solution.py:345
  97.4 2.1 %collective-permute-done.4 = f32[8,1024]{1,0:T(8,128)S(1)} collective-permute-done((f32[8,1024]{1,0:T(8,128)S(1)}, f32[8,1024]{1,0:T(8,128)S(1)}, u32[]{:S(2)}, u32[]{:S(2)}) %collective-permute-start.4) | collective-permute-done | bytes 32800 | tf_op jit(solution)/shard_map/ppermute | solution.py:345
  99.6 1.2 %collective-permute-done.7 = f32[4,1,2,1024]{3,2,1,0:T(2,128)S(1)} collective-permute-done((f32[4,1,2,1024]{3,2,1,0:T(2,128)S(1)}, f32[4,1,2,1024]{3,2,1,0:T(2,128)S(1)}, u32[]{:S(2)}, u32[]{:S(2)}) %collective-permute-start.7) | collective-permute-done | bytes 32800 | tf_op jit(solution)/shard_map/ppermute | solution.py:427
  (42 shorter events, 9.8 us)
Async XLA Ops:
  0.6 9.7 %all-to-all-start = ((s32[8,1,16]{2,1,0:T(1,128)}), s32[8,1,16]{2,1,0:T(1,128)S(1)}, u32[]{:S(2)}, u32[]{:S(2)}) async-start(s32[8,1,16]{2,1,0:T(1,128)} %bitcast.17), calls=%async_computation | async-start | bytes 8192 | tf_op jit(solution)/shard_map/all_to_all | solution.py:367
  10.3 1.2 %copy-start = (bf16[512,1024]{1,0:T(8,128)(2,1)S(1)}, bf16[512,1024]{1,0:T(8,128)(2,1)}, u32[]{:S(2)}) copy-start(bf16[512,1024]{1,0:T(8,128)(2,1)} %table_ref.1) | copy-start | bytes 3145732
  12.6 10.9 %all-to-all-start.1 = ((bf16[8,16,1024]{2,1,0:T(8,128)(2,1)}), bf16[8,16,1024]{2,1,0:T(8,128)(2,1)S(1)}, u32[]{:S(2)}, u32[]{:S(2)}) async-start(bf16[8,16,1024]{2,1,0:T(8,128)(2,1)} %bitcast.3), calls=%async_computation.1 | async-start | bytes 524288 | tf_op jit(solution)/shard_map/all_to_all | solution.py:368
  23.5 0.7 copy-start.2
  46.8 2.4 %collective-permute-start = (bf16[320,1024]{1,0:T(8,128)(2,1)}, bf16[320,1024]{1,0:T(8,128)(2,1)S(1)}, u32[]{:S(2)}, u32[]{:S(2)}) collective-permute-start(bf16[320,1024]{1,0:T(8,128)(2,1)} %get-tuple-element.20), channel_id=1, source_target_pairs={{0,32},{32,0},{64,96},{96,64},{128,160},{160,128},{192,224},{224,1... | collective-permute-start | bytes 1966088 | tf_op jit(solution)/shard_map/ppermute | solution.py:405
  49.2 1.1 %copy-start.1 = (bf16[320,1024]{1,0:T(8,128)(2,1)S(1)}, bf16[320,1024]{1,0:T(8,128)(2,1)}, u32[]{:S(2)}) copy-start(bf16[320,1024]{1,0:T(8,128)(2,1)} %get-tuple-element.19.near_ref) | copy-start | bytes 1966084
  50.5 7.1 %collective-permute-start.8 = (bf16[32,1024]{1,0:T(8,128)(2,1)S(1)}, bf16[32,1024]{1,0:T(8,128)(2,1)S(1)}, u32[]{:S(2)}, u32[]{:S(2)}) collective-permute-start(bf16[32,1024]{1,0:T(8,128)(2,1)S(1)} %get-tuple-element.26), channel_id=1, source_target_pairs={{0,64},{64,128},{128,192},{192,0},{32,96},{96,160},{160,224},{224,... | collective-permute-start | bytes 196616 | tf_op jit(solution)/shard_map/ppermute | solution.py:345
  51.2 7.7 %collective-permute-start.9 = (bf16[32,1024]{1,0:T(8,128)(2,1)S(1)}, bf16[32,1024]{1,0:T(8,128)(2,1)S(1)}, u32[]{:S(2)}, u32[]{:S(2)}) collective-permute-start(bf16[32,1024]{1,0:T(8,128)(2,1)S(1)} %get-tuple-element.27), channel_id=1, source_target_pairs={{0,128},{64,192},{128,0},{192,64},{32,160},{96,224},{160,32},{224,... | collective-permute-start | bytes 196616 | tf_op jit(solution)/shard_map/ppermute | solution.py:345
  53.2 5.6 %collective-permute-start.10 = (bf16[32,1024]{1,0:T(8,128)(2,1)S(1)}, bf16[32,1024]{1,0:T(8,128)(2,1)S(1)}, u32[]{:S(2)}, u32[]{:S(2)}) collective-permute-start(bf16[32,1024]{1,0:T(8,128)(2,1)S(1)} %get-tuple-element.28), channel_id=1, source_target_pairs={{0,192},{64,0},{128,64},{192,128},{32,224},{96,32},{160,96},{224,1... | collective-permute-start | bytes 196616 | tf_op jit(solution)/shard_map/ppermute | solution.py:345
  54.1 8.5 %collective-permute-start.1 = (bf16[64,1024]{1,0:T(8,128)(2,1)S(1)}, bf16[64,1024]{1,0:T(8,128)(2,1)S(1)}, u32[]{:S(2)}, u32[]{:S(2)}) collective-permute-start(bf16[64,1024]{1,0:T(8,128)(2,1)S(1)} %get-tuple-element.22), channel_id=1, source_target_pairs={{0,2},{1,3},{2,0},{3,1},{4,6},{5,7},{6,4},{7,5},{8,10},{9,11},{10,... | collective-permute-start | bytes 393224 | tf_op jit(solution)/shard_map/ppermute | solution.py:345
  55.5 7.5 %collective-permute-start.2 = (bf16[64,1024]{1,0:T(8,128)(2,1)S(1)}, bf16[64,1024]{1,0:T(8,128)(2,1)S(1)}, u32[]{:S(2)}, u32[]{:S(2)}) collective-permute-start(bf16[64,1024]{1,0:T(8,128)(2,1)S(1)} %get-tuple-element.23), channel_id=1, source_target_pairs={{0,1},{1,2},{2,3},{3,0},{4,5},{5,6},{6,7},{7,4},{8,9},{9,10},{10,1... | collective-permute-start | bytes 393224 | tf_op jit(solution)/shard_map/ppermute | solution.py:345
  57.6 12.6 %collective-permute-start.3 = (bf16[64,1024]{1,0:T(8,128)(2,1)S(1)}, bf16[64,1024]{1,0:T(8,128)(2,1)S(1)}, u32[]{:S(2)}, u32[]{:S(2)}) collective-permute-start(bf16[64,1024]{1,0:T(8,128)(2,1)S(1)} %get-tuple-element.24), channel_id=1, source_target_pairs={{0,3},{1,0},{2,1},{3,2},{4,7},{5,4},{6,5},{7,6},{8,11},{9,8},{10,9... | collective-permute-start | bytes 393224 | tf_op jit(solution)/shard_map/ppermute | solution.py:345
  59.2 20.1 %collective-permute-start.11 = (bf16[128,1024]{1,0:T(8,128)(2,1)S(1)}, bf16[128,1024]{1,0:T(8,128)(2,1)S(1)}, u32[]{:S(2)}, u32[]{:S(2)}) collective-permute-start(bf16[128,1024]{1,0:T(8,128)(2,1)S(1)} %get-tuple-element.30), channel_id=1, source_target_pairs={{0,2},{1,3},{2,0},{3,1},{4,6},{5,7},{6,4},{7,5},{8,10},{9,11},{10,... | collective-permute-start | bytes 786440 | tf_op jit(solution)/shard_map/ppermute | solution.py:345
  60.9 18.4 %collective-permute-start.12 = (bf16[128,1024]{1,0:T(8,128)(2,1)S(1)}, bf16[128,1024]{1,0:T(8,128)(2,1)S(1)}, u32[]{:S(2)}, u32[]{:S(2)}) collective-permute-start(bf16[128,1024]{1,0:T(8,128)(2,1)S(1)} %get-tuple-element.31), channel_id=1, source_target_pairs={{0,1},{1,2},{2,3},{3,0},{4,5},{5,6},{6,7},{7,4},{8,9},{9,10},{10,1... | collective-permute-start | bytes 786440 | tf_op jit(solution)/shard_map/ppermute | solution.py:345
  62.6 16.8 %collective-permute-start.13 = (bf16[128,1024]{1,0:T(8,128)(2,1)S(1)}, bf16[128,1024]{1,0:T(8,128)(2,1)S(1)}, u32[]{:S(2)}, u32[]{:S(2)}) collective-permute-start(bf16[128,1024]{1,0:T(8,128)(2,1)S(1)} %get-tuple-element.32), channel_id=1, source_target_pairs={{0,3},{1,0},{2,1},{3,2},{4,7},{5,4},{6,5},{7,6},{8,11},{9,8},{10,9... | collective-permute-start | bytes 786440 | tf_op jit(solution)/shard_map/ppermute | solution.py:345
  70.9 17.6 %all-to-all-start.2 = ((bf16[8,8,1024]{2,1,0:T(8,128)(2,1)}), bf16[8,8,1024]{2,1,0:T(8,128)(2,1)S(1)}, u32[]{:S(2)}, u32[]{:S(2)}) async-start(bf16[8,8,1024]{2,1,0:T(8,128)(2,1)} %fusion), calls=%async_computation.2 | async-start | bytes 262144 | tf_op jit(solution)/shard_map/all_to_all | solution.py:419
  88.5 13.8 %all-to-all-start.3 = ((bf16[8,16,1024]{2,1,0:T(8,128)(2,1)}), bf16[8,16,1024]{2,1,0:T(8,128)(2,1)S(1)}, u32[]{:S(2)}, u32[]{:S(2)}) async-start(bf16[8,16,1024]{2,1,0:T(8,128)(2,1)} %bitcast.9), calls=%async_computation.3 | async-start | bytes 524288 | tf_op jit(solution)/shard_map/all_to_all | solution.py:419
  92.0 5.0 %collective-permute-start.6 = (f32[8,1024]{1,0:T(8,128)S(1)}, f32[8,1024]{1,0:T(8,128)S(1)}, u32[]{:S(2)}, u32[]{:S(2)}) collective-permute-start(f32[8,1024]{1,0:T(8,128)S(1)} %convert_reduce_fusion.1), channel_id=1, source_target_pairs={{0,192},{64,0},{128,64},{192,128},{32,224},{96,32},{160,96},{224,1... | collective-permute-start | bytes 98312 | tf_op jit(solution)/shard_map/ppermute | solution.py:345
  92.1 5.3 %collective-permute-start.5 = (f32[8,1024]{1,0:T(8,128)S(1)}, f32[8,1024]{1,0:T(8,128)S(1)}, u32[]{:S(2)}, u32[]{:S(2)}) collective-permute-start(f32[8,1024]{1,0:T(8,128)S(1)} %convert_reduce_fusion.1), channel_id=1, source_target_pairs={{0,64},{64,128},{128,192},{192,0},{32,96},{96,160},{160,224},{224,... | collective-permute-start | bytes 98312 | tf_op jit(solution)/shard_map/ppermute | solution.py:345
  94.1 5.4 %collective-permute-start.4 = (f32[8,1024]{1,0:T(8,128)S(1)}, f32[8,1024]{1,0:T(8,128)S(1)}, u32[]{:S(2)}, u32[]{:S(2)}) collective-permute-start(f32[8,1024]{1,0:T(8,128)S(1)} %convert_reduce_fusion.1), channel_id=1, source_target_pairs={{0,128},{64,192},{128,0},{192,64},{32,160},{96,224},{160,32},{224,... | collective-permute-start | bytes 98312 | tf_op jit(solution)/shard_map/ppermute | solution.py:345
  99.5 1.3 %collective-permute-start.7 = (f32[4,1,2,1024]{3,2,1,0:T(2,128)S(1)}, f32[4,1,2,1024]{3,2,1,0:T(2,128)S(1)}, u32[]{:S(2)}, u32[]{:S(2)}) collective-permute-start(f32[4,1,2,1024]{3,2,1,0:T(2,128)S(1)} %reshape.106), channel_id=1, source_target_pairs={{0,32},{32,0},{64,96},{96,64},{128,160},{160,128},{192,224},{224,1... | collective-permute-start | bytes 98312 | tf_op jit(solution)/shard_map/ppermute | solution.py:427

commit v4 on v3

--- a/solution.py
+++ b/solution.py
@@ -59,9 +59,9 @@
 
 def layer_kernel(
     lengths_ref,
-    fetched_ref,
     source_ref,
     place_ref,
+    fetched_hbm,
     hot_hbm,
     w_in_hbm,
     w_out_hbm,
@@ -69,6 +69,7 @@
     layer_out_hbm,
     near_ref,
     far_ref,
+    fetched_ref,
     hot_ref,
     w_in_ref,
     w_out_ref,
@@ -99,17 +100,18 @@
     w_out_copy = pltpu.make_async_copy(w_out_hbm, w_out_ref, sems.at[2])
     out_grad_copy = pltpu.make_async_copy(out_grad_hbm, out_grad_ref, sems.at[3])
     layer_out_copy = pltpu.make_async_copy(layer_out_ref, layer_out_hbm, sems.at[4])
-    for copy in (hot_copy, w_in_copy, w_out_copy, out_grad_copy):
+    fetched_copy = pltpu.make_async_copy(fetched_hbm, fetched_ref, sems.at[5])
+    for copy in (hot_copy, fetched_copy, w_in_copy, w_out_copy, out_grad_copy):
         copy.start()
     hot_copy.wait()
-
-    @pl.loop(0, tokens // BLOCK)
-    def _(step):
-        at = pl.ds(pl.multiple_of(step * BLOCK, BLOCK), BLOCK)
+    fetched_copy.wait()
+
+    for block in range(tokens // 256):
+        at = pl.ds(block * 256, 256)
         source = source_ref[at, :]
-        hot_pick = (source == lax.broadcasted_iota(jnp.int32, (BLOCK, hot_rows), 1)).astype(bf16)
+        hot_pick = (source == lax.broadcasted_iota(jnp.int32, (256, hot_rows), 1)).astype(bf16)
         slot_pick = (
-            source == lax.broadcasted_iota(jnp.int32, (BLOCK, slot_count), 1) + hot_rows
+            source == lax.broadcasted_iota(jnp.int32, (256, slot_count), 1) + hot_rows
         ).astype(bf16)
         rows = dot_nn(hot_pick, hot_ref[...]) + dot_nn(slot_pick, fetched_ref[...])
         centered = rows - mean_of(rows)
@@ -120,9 +122,8 @@
 
     w_in_copy.wait()
 
-    @pl.loop(0, 4 * inner // 256)
-    def _(step):
-        at = pl.ds(pl.multiple_of(step * 256, 256), 256)
+    for step in range(4 * inner // 256):
+        at = pl.ds(step * 256, 256)
         pre = dot_nn(normed_ref[...], w_in_ref[:, at])
         sig = sigmoid(pre)
         act = pre * sig
@@ -208,14 +209,12 @@
     dpre_ref[:, values] = (dvalue_ref[...] * slope_ref[:, values].astype(f32)).astype(bf16)
     dpre_ref[:, keys] = (dkey_ref[...] * slope_ref[:, keys].astype(f32)).astype(bf16)
 
-    @pl.loop(0, width // 256)
-    def _(step):
-        at = pl.ds(pl.multiple_of(step * 256, 256), 256)
+    for step in range(width // 256):
+        at = pl.ds(step * 256, 256)
         dnorm_ref[:, at] = dot_nt(dpre_ref[...], w_in_ref[at, :])
 
-    @pl.loop(0, tokens // BLOCK)
-    def _(step):
-        at = pl.ds(pl.multiple_of(step * BLOCK, BLOCK), BLOCK)
+    for block in range(tokens // 64):
+        at = pl.ds(block * 64, 64)
         rstd = rstd_ref[at, :]
         unit = normed_ref[at, :].astype(f32)
         dunit = dnorm_ref[at, :]
@@ -249,9 +248,10 @@
             jax.ShapeDtypeStruct((half, width), bf16),
             jax.ShapeDtypeStruct((half, width), bf16),
         ),
-        in_specs=[pl.BlockSpec(memory_space=pltpu.SMEM)] + [vmem] * 3 + [hbm] * 4,
+        in_specs=[pl.BlockSpec(memory_space=pltpu.SMEM)] + [vmem] * 2 + [hbm] * 5,
         out_specs=(hbm, vmem, vmem),
         scratch_shapes=[
+            pltpu.VMEM(fetched.shape, bf16),
             pltpu.VMEM(hot_table.shape, bf16),
             pltpu.VMEM(w_in.shape, bf16),
             pltpu.VMEM(w_out.shape, bf16),
@@ -269,12 +269,12 @@
             pltpu.VMEM((tokens, inner), f32),
             pltpu.VMEM((tokens, 4 * inner), bf16),
             pltpu.VMEM((tokens, width), f32),
-            pltpu.SemaphoreType.DMA((5,)),
+            pltpu.SemaphoreType.DMA((6,)),
         ],
         compiler_params=pltpu.CompilerParams(vmem_limit_bytes=58 * 1024 * 1024),
         cost_estimate=pl.CostEstimate(flops=8 * 10**9, bytes_accessed=12 * 10**6, transcendentals=0),
         name="layer",
-    )(lengths, fetched, source, place, hot_table, w_in, w_out, out_grad)
+    )(lengths, source, place, fetched, hot_table, w_in, w_out, out_grad)
 
 
 def core_sums_kernel(near_ref, got_ref, *out_refs):
@@ -362,7 +362,7 @@
     model_width = cold_table.shape[1]
     hot_rows = hot_table.shape[0]
     table_at, dp_at = lax.axis_index("table"), lax.axis_index("dp")
-    y_at, core_at, x_at = table_at // 2, table_at % 2, dp_at % 4
+    y_at, core_at, x_at, z_at = table_at // 2, table_at % 2, dp_at % 4, dp_at // 4
 
     wanted = lax.all_to_all(cold_requests, "table", split_axis=0, concat_axis=0, tiled=True)
     fetched = lax.all_to_all(
@@ -376,10 +376,11 @@
     is_hot = event_hot == 1
 
     hot_dp, hot_t = event_index // 16, (event_index % 16) // 2
+    z_step = (hot_dp // 4) ^ z_at
     hot_place = (
         (hot_t % 2 - core_at) % 2 * 320
         + (hot_dp % 4 - x_at) % 4 * 64
-        + hot_dp // 4 * 8
+        + (z_step % 2 * 4 + z_step // 2 % 2 * 2 + z_step // 4) * 8
         + hot_t // 2 * 2
         + event_index % 2
     )
@@ -414,16 +415,17 @@
     cold_chunks = shard_sums(shard_place, pieces, shard_rows)
     cold_pieces = exchange(cold_chunks, "dp", X_GROUPS)
 
-    def over_z(rows):
-        by_z = rows.astype(jnp.bfloat16).reshape(8, -1, model_width)
-        by_z = lax.all_to_all(
-            by_z, "dp", split_axis=0, concat_axis=0, tiled=True, axis_index_groups=Z_GROUPS
-        )
-        return jnp.sum(by_z.astype(jnp.float32), axis=0)
-
-    hot_sum = over_z(hot_part)
-    cold_sum = over_z(add_up(cold_pieces))
-    hot_sum = add_up(exchange([hot_sum] * 4, "table", Y_GROUPS)).reshape(4, 1, 2, model_width)
+    for step in (1, 2, 4):
+        half = hot_part.shape[0] // 2
+        pairs = [(group[i], group[i ^ step]) for group in Z_GROUPS for i in range(8)]
+        sent = lax.ppermute(hot_part[half:].astype(jnp.bfloat16), "dp", pairs)
+        hot_part = hot_part[:half] + sent.astype(jnp.float32)
+    by_z = add_up(cold_pieces).astype(jnp.bfloat16).reshape(8, -1, model_width)
+    by_z = lax.all_to_all(
+        by_z, "dp", split_axis=0, concat_axis=0, tiled=True, axis_index_groups=Z_GROUPS
+    )
+    cold_sum = jnp.sum(by_z.astype(jnp.float32), axis=0)
+    hot_sum = add_up(exchange([hot_part] * 4, "table", Y_GROUPS)).reshape(4, 1, 2, model_width)
     other = lax.ppermute(hot_sum, "table", shift(CORE_GROUPS, 1))
     ordered = jnp.where(
         core_at == 0,

time: 104 us -> 96.8 us (0.931)
  the two profiles are of different devices: /device:TPU:6 before, /device:TPU:2 now
where the time goes in v4:
time: 96.8 us; the launch traced here: 96.3 us
  starting transfers between devices  41.6 us (43%)
  waiting for transfers between devices  24.1 us (25%)
  Pallas kernels  20.6 us (21%)
  local copies, waits for them, and re-layouts  5.33 us (6%)
  other arithmetic  3.81 us (4%)
    pallas_call x1, Pallas kernels, layer(): pl.pallas_call(layer_kernel, out_shape=(jax.ShapeDtypeStruct((tokens, wid...  19 us
    ppermute x12, starting transfers between devices, exchange(): lax.ppermute(chunk, axis, shift(groups, k))  15.3 us
    ppermute x3, starting transfers between devices, on_device(): sent = lax.ppermute(hot_part[half:].astype(jnp.bfloat16), 'dp', pairs)  11.5 us
    all_to_all x1, starting transfers between devices, on_device(): lax.all_to_all(by_z, 'dp', split_axis=0, concat_axis=0, tiled=True, axis_...  6.76 us
    ppermute x12, waiting for transfers between devices, exchange(): lax.ppermute(chunk, axis, shift(groups, k))  6.66 us
    all_to_all x1, waiting for transfers between devices, on_device(): lax.all_to_all(cold_requests, 'table', split_axis=0, concat_axis=0, tiled...  5.19 us
    all_to_all x1, waiting for transfers between devices, on_device(): lax.all_to_all(pick_rows(wanted, cold_table).reshape(table_count, cap_siz...  4.59 us
    all_to_all x1, starting transfers between devices, on_device(): lax.all_to_all(cold_requests, 'table', split_axis=0, concat_axis=0, tiled...  4.48 us
  transfers between devices with their start and end apart: 20, of which 11 were waited for; matrix products, arithmetic and copies ran while one was open for 6% of the time, Pallas kernels for 0%

profile of v4, /device:TPU:2, one launch (start us, length us, event | category | flops | bytes accessed | tf_op | source)
XLA Modules:
  0.0 96.3 jit_solution(7775690450344714885)
XLA Ops:
  0.6 4.5 %all-to-all-start = ((s32[8,1,16]{2,1,0:T(1,128)}), s32[8,1,16]{2,1,0:T(1,128)S(1)}, u32[]{:S(2)}, u32[]{:S(2)}) async-start(s32[8,1,16]{2,1,0:T(1,128)} %bitcast.15), calls=%async_computation | async-start | bytes 8192 | tf_op jit(solution)/shard_map/all_to_all | solution.py:367
  5.1 5.2 %all-to-all-done = s32[8,1,16]{2,1,0:T(1,128)S(1)} async-done(((s32[8,1,16]{2,1,0:T(1,128)}), s32[8,1,16]{2,1,0:T(1,128)S(1)}, u32[]{:S(2)}, u32[]{:S(2)}) %all-to-all-start) | async-done | bytes 544 | tf_op jit(solution)/shard_map/all_to_all | solution.py:367
  10.3 1.2 %copy-done = bf16[512,1024]{1,0:T(8,128)(2,1)S(1)} copy-done((bf16[512,1024]{1,0:T(8,128)(2,1)S(1)}, bf16[512,1024]{1,0:T(8,128)(2,1)}, u32[]{:S(2)}) %copy-start) | copy-done | bytes 1048600
  12.6 3.4 %all-to-all-start.1 = ((bf16[8,16,1024]{2,1,0:T(8,128)(2,1)}), bf16[8,16,1024]{2,1,0:T(8,128)(2,1)S(1)}, u32[]{:S(2)}, u32[]{:S(2)}) async-start(bf16[8,16,1024]{2,1,0:T(8,128)(2,1)} %bitcast.5), calls=%async_computation.1 | async-start | bytes 524288 | tf_op jit(solution)/shard_map/all_to_all | solution.py:368
  16.1 1.3 %fusion.20 = (s32[512]{0:T(512)}, pred[512]{0:T(512)(128)(4,1)S(1)}) fusion(s32[512]{0:T(512)} %param.15, s32[]{:T(128)S(6)} %select_n.186, s32[]{:T(128)S(6)} %select_n.176, s32[]{:T(128)S(6)} %select_n.173, s32[]{:T(128)S(6)} %select_n.169, s32[512]{0:T(512)} %param.14), kind=kLoop, calls=%fused_computation.102 | loop fusion | flops 103424 | bytes 6672 | tf_op jit(solution)/shard_map/jit(_where)/select_n | solution.py:395
  18.9 4.6 %all-to-all-done.1 = bf16[8,16,1024]{2,1,0:T(8,128)(2,1)S(1)} async-done(((bf16[8,16,1024]{2,1,0:T(8,128)(2,1)}), bf16[8,16,1024]{2,1,0:T(8,128)(2,1)S(1)}, u32[]{:S(2)}, u32[]{:S(2)}) %all-to-all-start.1) | async-done | bytes 262176 | tf_op jit(solution)/shard_map/all_to_all | solution.py:368
  24.2 19.0 %layer.1 = (bf16[512,1024]{1,0:T(8,128)(2,1)}, bf16[320,1024]{1,0:T(8,128)(2,1)}, bf16[320,1024]{1,0:T(8,128)(2,1)}) custom-call(s32[1,8]{1,0:T(1,128)} %lengths_ref.1, s32[512,1]{1,0:T(8,128)} %copy.16.source_ref, s32[1,512]{1,0:T(1,128)} %bitcast.16, bf16[128,1024]{1,0:T(8,128)(2,1)} %bitcast.13, bf16[512,1024]{1,0:T(8,128)(2,1)} %hot_hbm.1, ...), custom_call_target="tpu_custom_call" | custom-call | flops 8000000000 | bytes 12000000 | tf_op jit(solution)/shard_map/layer/pallas_call | solution.py:244
  43.5 2.1 %collective-permute-done.got_ref = bf16[320,1024]{1,0:T(8,128)(2,1)S(1)} collective-permute-done((bf16[320,1024]{1,0:T(8,128)(2,1)}, bf16[320,1024]{1,0:T(8,128)(2,1)S(1)}, u32[]{:S(2)}, u32[]{:S(2)}) %collective-permute-start) | collective-permute-done | bytes 655392 | tf_op jit(solution)/shard_map/ppermute | solution.py:406
  46.8 2.2 %collective-permute-start.1 = (bf16[64,1024]{1,0:T(8,128)(2,1)S(1)}, bf16[64,1024]{1,0:T(8,128)(2,1)S(1)}, u32[]{:S(2)}, u32[]{:S(2)}) collective-permute-start(bf16[64,1024]{1,0:T(8,128)(2,1)S(1)} %get-tuple-element.22), channel_id=1, source_target_pairs={{0,2},{1,3},{2,0},{3,1},{4,6},{5,7},{6,4},{7,5},{8,10},{9,11},{10,... | collective-permute-start | bytes 393224 | tf_op jit(solution)/shard_map/ppermute | solution.py:345
  49.4 1.7 %collective-permute-start.3 = (bf16[64,1024]{1,0:T(8,128)(2,1)S(1)}, bf16[64,1024]{1,0:T(8,128)(2,1)S(1)}, u32[]{:S(2)}, u32[]{:S(2)}) collective-permute-start(bf16[64,1024]{1,0:T(8,128)(2,1)S(1)} %get-tuple-element.24), channel_id=1, source_target_pairs={{0,3},{1,0},{2,1},{3,2},{4,7},{5,4},{6,5},{7,6},{8,11},{9,8},{10,9... | collective-permute-start | bytes 393224 | tf_op jit(solution)/shard_map/ppermute | solution.py:345
  51.7 2.0 %collective-permute-start.12 = (bf16[32,1024]{1,0:T(8,128)(2,1)S(1)}, bf16[32,1024]{1,0:T(8,128)(2,1)S(1)}, u32[]{:S(2)}, u32[]{:S(2)}) collective-permute-start(bf16[32,1024]{1,0:T(8,128)(2,1)S(1)} %get-tuple-element.27), channel_id=1, source_target_pairs={{0,128},{64,192},{128,0},{192,64},{32,160},{96,224},{160,32},{224,... | collective-permute-start | bytes 196616 | tf_op jit(solution)/shard_map/ppermute | solution.py:345
  56.9 2.0 %collective-permute-start.4 = (bf16[32,1024]{1,0:T(8,128)(2,1)S(1)}, bf16[32,1024]{1,0:T(8,128)(2,1)S(1)}, u32[]{:S(2)}, u32[]{:S(2)}) collective-permute-start(bf16[32,1024]{1,0:T(8,128)(2,1)S(1)} %slice.41), channel_id=1, source_target_pairs={{0,4},{4,0},{8,12},{12,8},{16,20},{20,16},{24,28},{28,24},{1,5},{5... | collective-permute-start | bytes 196616 | tf_op jit(solution)/shard_map/ppermute | solution.py:421
  60.1 2.5 %collective-permute-start.14 = (bf16[128,1024]{1,0:T(8,128)(2,1)S(1)}, bf16[128,1024]{1,0:T(8,128)(2,1)S(1)}, u32[]{:S(2)}, u32[]{:S(2)}) collective-permute-start(bf16[128,1024]{1,0:T(8,128)(2,1)S(1)} %get-tuple-element.30), channel_id=1, source_target_pairs={{0,2},{1,3},{2,0},{3,1},{4,6},{5,7},{6,4},{7,5},{8,10},{9,11},{10,... | collective-permute-start | bytes 786440 | tf_op jit(solution)/shard_map/ppermute | solution.py:345
  62.8 1.7 %collective-permute-start.16 = (bf16[128,1024]{1,0:T(8,128)(2,1)S(1)}, bf16[128,1024]{1,0:T(8,128)(2,1)S(1)}, u32[]{:S(2)}, u32[]{:S(2)}) collective-permute-start(bf16[128,1024]{1,0:T(8,128)(2,1)S(1)} %get-tuple-element.32), channel_id=1, source_target_pairs={{0,3},{1,0},{2,1},{3,2},{4,7},{5,4},{6,5},{7,6},{8,11},{9,8},{10,9... | collective-permute-start | bytes 786440 | tf_op jit(solution)/shard_map/ppermute | solution.py:345
  64.6 3.3 %collective-permute-start.5 = (bf16[16,1024]{1,0:T(8,128)(2,1)S(1)}, bf16[16,1024]{1,0:T(8,128)(2,1)S(1)}, u32[]{:S(2)}, u32[]{:S(2)}) collective-permute-start(bf16[16,1024]{1,0:T(8,128)(2,1)S(1)} %slice.42), channel_id=1, source_target_pairs={{0,8},{4,12},{8,0},{12,4},{16,24},{20,28},{24,16},{28,20},{1,9},{5... | collective-permute-start | bytes 98312 | tf_op jit(solution)/shard_map/ppermute | solution.py:421
  67.9 1.9 %collective-permute-done.5 = bf16[16,1024]{1,0:T(8,128)(2,1)S(1)} collective-permute-done((bf16[16,1024]{1,0:T(8,128)(2,1)S(1)}, bf16[16,1024]{1,0:T(8,128)(2,1)S(1)}, u32[]{:S(2)}, u32[]{:S(2)}) %collective-permute-start.5) | collective-permute-done | bytes 32800 | tf_op jit(solution)/shard_map/ppermute | solution.py:421
  69.8 6.1 %collective-permute-start.6 = (bf16[8,1024]{1,0:T(8,128)(2,1)S(1)}, bf16[8,1024]{1,0:T(8,128)(2,1)S(1)}, u32[]{:S(2)}, u32[]{:S(2)}) collective-permute-start(bf16[8,1024]{1,0:T(8,128)(2,1)S(1)} %slice.43), channel_id=1, source_target_pairs={{0,16},{4,20},{8,24},{12,28},{16,0},{20,4},{24,8},{28,12},{1,17},{... | collective-permute-start | bytes 49160 | tf_op jit(solution)/shard_map/ppermute | solution.py:421
  76.8 6.8 %all-to-all-start.2 = ((bf16[8,16,1024]{2,1,0:T(8,128)(2,1)}), bf16[8,16,1024]{2,1,0:T(8,128)(2,1)S(1)}, u32[]{:S(2)}, u32[]{:S(2)}) async-start(bf16[8,16,1024]{2,1,0:T(8,128)(2,1)} %bitcast.8), calls=%async_computation.2 | async-start | bytes 524288 | tf_op jit(solution)/shard_map/all_to_all | solution.py:424
  83.6 1.2 %collective-permute-start.9 = (f32[8,1024]{1,0:T(8,128)S(1)}, f32[8,1024]{1,0:T(8,128)S(1)}, u32[]{:S(2)}, u32[]{:S(2)}) collective-permute-start(f32[8,1024]{1,0:T(8,128)S(1)} %slice_add_fusion.2), channel_id=1, source_target_pairs={{0,192},{64,0},{128,64},{192,128},{32,224},{96,32},{160,96},{224,1... | collective-permute-start | bytes 98312 | tf_op jit(solution)/shard_map/ppermute | solution.py:345
  86.4 1.2 %collective-permute-done.9 = f32[8,1024]{1,0:T(8,128)S(1)} collective-permute-done((f32[8,1024]{1,0:T(8,128)S(1)}, f32[8,1024]{1,0:T(8,128)S(1)}, u32[]{:S(2)}, u32[]{:S(2)}) %collective-permute-start.9) | collective-permute-done | bytes 32800 | tf_op jit(solution)/shard_map/ppermute | solution.py:345
  87.6 2.4 %collective-permute-done.8 = f32[8,1024]{1,0:T(8,128)S(1)} collective-permute-done((f32[8,1024]{1,0:T(8,128)S(1)}, f32[8,1024]{1,0:T(8,128)S(1)}, u32[]{:S(2)}, u32[]{:S(2)}) %collective-permute-start.8) | collective-permute-done | bytes 32800 | tf_op jit(solution)/shard_map/ppermute | solution.py:345
  89.9 1.2 %collective-permute-done.7 = f32[8,1024]{1,0:T(8,128)S(1)} collective-permute-done((f32[8,1024]{1,0:T(8,128)S(1)}, f32[8,1024]{1,0:T(8,128)S(1)}, u32[]{:S(2)}, u32[]{:S(2)}) %collective-permute-start.7) | collective-permute-done | bytes 32800 | tf_op jit(solution)/shard_map/ppermute | solution.py:345
  91.3 1.2 %collective-permute-done.10 = f32[4,1,2,1024]{3,2,0,1:T(2,128)S(1)} collective-permute-done((f32[4,1,2,1024]{3,2,0,1:T(2,128)S(1)}, f32[4,1,2,1024]{3,2,0,1:T(2,128)S(1)}, u32[]{:S(2)}, u32[]{:S(2)}) %collective-permute-start.10) | collective-permute-done | bytes 32800 | tf_op jit(solution)/shard_map/ppermute | solution.py:429
  93.2 2.5 %all-to-all-done.2 = bf16[8,16,1024]{2,1,0:T(8,128)(2,1)S(1)} async-done(((bf16[8,16,1024]{2,1,0:T(8,128)(2,1)}), bf16[8,16,1024]{2,1,0:T(8,128)(2,1)S(1)}, u32[]{:S(2)}, u32[]{:S(2)}) %all-to-all-start.2) | async-done | bytes 262176 | tf_op jit(solution)/shard_map/all_to_all | solution.py:424
  (52 shorter events, 14.4 us)
Async XLA Ops:
  0.6 9.7 %all-to-all-start = ((s32[8,1,16]{2,1,0:T(1,128)}), s32[8,1,16]{2,1,0:T(1,128)S(1)}, u32[]{:S(2)}, u32[]{:S(2)}) async-start(s32[8,1,16]{2,1,0:T(1,128)} %bitcast.15), calls=%async_computation | async-start | bytes 8192 | tf_op jit(solution)/shard_map/all_to_all | solution.py:367
  10.3 1.2 %copy-start = (bf16[512,1024]{1,0:T(8,128)(2,1)S(1)}, bf16[512,1024]{1,0:T(8,128)(2,1)}, u32[]{:S(2)}) copy-start(bf16[512,1024]{1,0:T(8,128)(2,1)} %table_ref.1) | copy-start | bytes 3145732
  12.6 10.9 %all-to-all-start.1 = ((bf16[8,16,1024]{2,1,0:T(8,128)(2,1)}), bf16[8,16,1024]{2,1,0:T(8,128)(2,1)S(1)}, u32[]{:S(2)}, u32[]{:S(2)}) async-start(bf16[8,16,1024]{2,1,0:T(8,128)(2,1)} %bitcast.5), calls=%async_computation.1 | async-start | bytes 524288 | tf_op jit(solution)/shard_map/all_to_all | solution.py:368
  23.5 0.7 copy-start.2
  43.2 2.4 %collective-permute-start = (bf16[320,1024]{1,0:T(8,128)(2,1)}, bf16[320,1024]{1,0:T(8,128)(2,1)S(1)}, u32[]{:S(2)}, u32[]{:S(2)}) collective-permute-start(bf16[320,1024]{1,0:T(8,128)(2,1)} %get-tuple-element.20), channel_id=1, source_target_pairs={{0,32},{32,0},{64,96},{96,64},{128,160},{160,128},{192,224},{224,1... | collective-permute-start | bytes 1966088 | tf_op jit(solution)/shard_map/ppermute | solution.py:406
  45.6 1.1 %copy-start.1 = (bf16[320,1024]{1,0:T(8,128)(2,1)S(1)}, bf16[320,1024]{1,0:T(8,128)(2,1)}, u32[]{:S(2)}) copy-start(bf16[320,1024]{1,0:T(8,128)(2,1)} %get-tuple-element.19.near_ref) | copy-start | bytes 1966084
  46.8 7.9 %collective-permute-start.1 = (bf16[64,1024]{1,0:T(8,128)(2,1)S(1)}, bf16[64,1024]{1,0:T(8,128)(2,1)S(1)}, u32[]{:S(2)}, u32[]{:S(2)}) collective-permute-start(bf16[64,1024]{1,0:T(8,128)(2,1)S(1)} %get-tuple-element.22), channel_id=1, source_target_pairs={{0,2},{1,3},{2,0},{3,1},{4,6},{5,7},{6,4},{7,5},{8,10},{9,11},{10,... | collective-permute-start | bytes 393224 | tf_op jit(solution)/shard_map/ppermute | solution.py:345
  49.1 7.8 %collective-permute-start.2 = (bf16[64,1024]{1,0:T(8,128)(2,1)S(1)}, bf16[64,1024]{1,0:T(8,128)(2,1)S(1)}, u32[]{:S(2)}, u32[]{:S(2)}) collective-permute-start(bf16[64,1024]{1,0:T(8,128)(2,1)S(1)} %get-tuple-element.23), channel_id=1, source_target_pairs={{0,1},{1,2},{2,3},{3,0},{4,5},{5,6},{6,7},{7,4},{8,9},{9,10},{10,1... | collective-permute-start | bytes 393224 | tf_op jit(solution)/shard_map/ppermute | solution.py:345
  49.4 7.4 %collective-permute-start.3 = (bf16[64,1024]{1,0:T(8,128)(2,1)S(1)}, bf16[64,1024]{1,0:T(8,128)(2,1)S(1)}, u32[]{:S(2)}, u32[]{:S(2)}) collective-permute-start(bf16[64,1024]{1,0:T(8,128)(2,1)S(1)} %get-tuple-element.24), channel_id=1, source_target_pairs={{0,3},{1,0},{2,1},{3,2},{4,7},{5,4},{6,5},{7,6},{8,11},{9,8},{10,9... | collective-permute-start | bytes 393224 | tf_op jit(solution)/shard_map/ppermute | solution.py:345
  51.1 8.5 %collective-permute-start.11 = (bf16[32,1024]{1,0:T(8,128)(2,1)S(1)}, bf16[32,1024]{1,0:T(8,128)(2,1)S(1)}, u32[]{:S(2)}, u32[]{:S(2)}) collective-permute-start(bf16[32,1024]{1,0:T(8,128)(2,1)S(1)} %get-tuple-element.26), channel_id=1, source_target_pairs={{0,64},{64,128},{128,192},{192,0},{32,96},{96,160},{160,224},{224,... | collective-permute-start | bytes 196616 | tf_op jit(solution)/shard_map/ppermute | solution.py:345
  51.7 7.9 %collective-permute-start.12 = (bf16[32,1024]{1,0:T(8,128)(2,1)S(1)}, bf16[32,1024]{1,0:T(8,128)(2,1)S(1)}, u32[]{:S(2)}, u32[]{:S(2)}) collective-permute-start(bf16[32,1024]{1,0:T(8,128)(2,1)S(1)} %get-tuple-element.27), channel_id=1, source_target_pairs={{0,128},{64,192},{128,0},{192,64},{32,160},{96,224},{160,32},{224,... | collective-permute-start | bytes 196616 | tf_op jit(solution)/shard_map/ppermute | solution.py:345
  54.8 4.9 %collective-permute-start.13 = (bf16[32,1024]{1,0:T(8,128)(2,1)S(1)}, bf16[32,1024]{1,0:T(8,128)(2,1)S(1)}, u32[]{:S(2)}, u32[]{:S(2)}) collective-permute-start(bf16[32,1024]{1,0:T(8,128)(2,1)S(1)} %get-tuple-element.28), channel_id=1, source_target_pairs={{0,192},{64,0},{128,64},{192,128},{32,224},{96,32},{160,96},{224,1... | collective-permute-start | bytes 196616 | tf_op jit(solution)/shard_map/ppermute | solution.py:345
  56.9 7.6 %collective-permute-start.4 = (bf16[32,1024]{1,0:T(8,128)(2,1)S(1)}, bf16[32,1024]{1,0:T(8,128)(2,1)S(1)}, u32[]{:S(2)}, u32[]{:S(2)}) collective-permute-start(bf16[32,1024]{1,0:T(8,128)(2,1)S(1)} %slice.41), channel_id=1, source_target_pairs={{0,4},{4,0},{8,12},{12,8},{16,20},{20,16},{24,28},{28,24},{1,5},{5... | collective-permute-start | bytes 196616 | tf_op jit(solution)/shard_map/ppermute | solution.py:421
  60.1 15.9 %collective-permute-start.14 = (bf16[128,1024]{1,0:T(8,128)(2,1)S(1)}, bf16[128,1024]{1,0:T(8,128)(2,1)S(1)}, u32[]{:S(2)}, u32[]{:S(2)}) collective-permute-start(bf16[128,1024]{1,0:T(8,128)(2,1)S(1)} %get-tuple-element.30), channel_id=1, source_target_pairs={{0,2},{1,3},{2,0},{3,1},{4,6},{5,7},{6,4},{7,5},{8,10},{9,11},{10,... | collective-permute-start | bytes 786440 | tf_op jit(solution)/shard_map/ppermute | solution.py:345
  62.5 13.4 %collective-permute-start.15 = (bf16[128,1024]{1,0:T(8,128)(2,1)S(1)}, bf16[128,1024]{1,0:T(8,128)(2,1)S(1)}, u32[]{:S(2)}, u32[]{:S(2)}) collective-permute-start(bf16[128,1024]{1,0:T(8,128)(2,1)S(1)} %get-tuple-element.31), channel_id=1, source_target_pairs={{0,1},{1,2},{2,3},{3,0},{4,5},{5,6},{6,7},{7,4},{8,9},{9,10},{10,1... | collective-permute-start | bytes 786440 | tf_op jit(solution)/shard_map/ppermute | solution.py:345
  62.8 13.1 %collective-permute-start.16 = (bf16[128,1024]{1,0:T(8,128)(2,1)S(1)}, bf16[128,1024]{1,0:T(8,128)(2,1)S(1)}, u32[]{:S(2)}, u32[]{:S(2)}) collective-permute-start(bf16[128,1024]{1,0:T(8,128)(2,1)S(1)} %get-tuple-element.32), channel_id=1, source_target_pairs={{0,3},{1,0},{2,1},{3,2},{4,7},{5,4},{6,5},{7,6},{8,11},{9,8},{10,9... | collective-permute-start | bytes 786440 | tf_op jit(solution)/shard_map/ppermute | solution.py:345
  64.6 5.2 %collective-permute-start.5 = (bf16[16,1024]{1,0:T(8,128)(2,1)S(1)}, bf16[16,1024]{1,0:T(8,128)(2,1)S(1)}, u32[]{:S(2)}, u32[]{:S(2)}) collective-permute-start(bf16[16,1024]{1,0:T(8,128)(2,1)S(1)} %slice.42), channel_id=1, source_target_pairs={{0,8},{4,12},{8,0},{12,4},{16,24},{20,28},{24,16},{28,20},{1,9},{5... | collective-permute-start | bytes 98312 | tf_op jit(solution)/shard_map/ppermute | solution.py:421
  69.8 13.7 %collective-permute-start.6 = (bf16[8,1024]{1,0:T(8,128)(2,1)S(1)}, bf16[8,1024]{1,0:T(8,128)(2,1)S(1)}, u32[]{:S(2)}, u32[]{:S(2)}) collective-permute-start(bf16[8,1024]{1,0:T(8,128)(2,1)S(1)} %slice.43), channel_id=1, source_target_pairs={{0,16},{4,20},{8,24},{12,28},{16,0},{20,4},{24,8},{28,12},{1,17},{... | collective-permute-start | bytes 49160 | tf_op jit(solution)/shard_map/ppermute | solution.py:421
  76.8 18.8 %all-to-all-start.2 = ((bf16[8,16,1024]{2,1,0:T(8,128)(2,1)}), bf16[8,16,1024]{2,1,0:T(8,128)(2,1)S(1)}, u32[]{:S(2)}, u32[]{:S(2)}) async-start(bf16[8,16,1024]{2,1,0:T(8,128)(2,1)} %bitcast.8), calls=%async_computation.2 | async-start | bytes 524288 | tf_op jit(solution)/shard_map/all_to_all | solution.py:424
  83.6 4.0 %collective-permute-start.9 = (f32[8,1024]{1,0:T(8,128)S(1)}, f32[8,1024]{1,0:T(8,128)S(1)}, u32[]{:S(2)}, u32[]{:S(2)}) collective-permute-start(f32[8,1024]{1,0:T(8,128)S(1)} %slice_add_fusion.2), channel_id=1, source_target_pairs={{0,192},{64,0},{128,64},{192,128},{32,224},{96,32},{160,96},{224,1... | collective-permute-start | bytes 98312 | tf_op jit(solution)/shard_map/ppermute | solution.py:345
  84.8 5.1 %collective-permute-start.8 = (f32[8,1024]{1,0:T(8,128)S(1)}, f32[8,1024]{1,0:T(8,128)S(1)}, u32[]{:S(2)}, u32[]{:S(2)}) collective-permute-start(f32[8,1024]{1,0:T(8,128)S(1)} %slice_add_fusion.2), channel_id=1, source_target_pairs={{0,64},{64,128},{128,192},{192,0},{32,96},{96,160},{160,224},{224,... | collective-permute-start | bytes 98312 | tf_op jit(solution)/shard_map/ppermute | solution.py:345
  85.7 5.4 %collective-permute-start.7 = (f32[8,1024]{1,0:T(8,128)S(1)}, f32[8,1024]{1,0:T(8,128)S(1)}, u32[]{:S(2)}, u32[]{:S(2)}) collective-permute-start(f32[8,1024]{1,0:T(8,128)S(1)} %slice_add_fusion.2), channel_id=1, source_target_pairs={{0,128},{64,192},{128,0},{192,64},{32,160},{96,224},{160,32},{224,... | collective-permute-start | bytes 98312 | tf_op jit(solution)/shard_map/ppermute | solution.py:345
  91.2 1.3 %collective-permute-start.10 = (f32[4,1,2,1024]{3,2,0,1:T(2,128)S(1)}, f32[4,1,2,1024]{3,2,0,1:T(2,128)S(1)}, u32[]{:S(2)}, u32[]{:S(2)}) collective-permute-start(f32[4,1,2,1024]{3,2,0,1:T(2,128)S(1)} %reshape.102), channel_id=1, source_target_pairs={{0,32},{32,0},{64,96},{96,64},{128,160},{160,128},{192,224},{224,1... | collective-permute-start | bytes 98312 | tf_op jit(solution)/shard_map/ppermute | solution.py:429

commit v5 on v4

--- a/solution.py
+++ b/solution.py
@@ -271,7 +271,7 @@
             pltpu.VMEM((tokens, width), f32),
             pltpu.SemaphoreType.DMA((6,)),
         ],
-        compiler_params=pltpu.CompilerParams(vmem_limit_bytes=58 * 1024 * 1024),
+        compiler_params=pltpu.CompilerParams(vmem_limit_bytes=52 * 1024 * 1024),
         cost_estimate=pl.CostEstimate(flops=8 * 10**9, bytes_accessed=12 * 10**6, transcendentals=0),
         name="layer",
     )(lengths, source, place, fetched, hot_table, w_in, w_out, out_grad)

time: 96.8 us -> 93.9 us (0.970)
  local copies, waits for them, and re-layouts: 5.33 us -> 3.47 us
  Pallas kernels: 20.6 us -> 19.1 us
  waiting for transfers between devices: 24.1 us -> 25.2 us
    pallas_call x1, Pallas kernels: 19 us -> 17.5 us  [layer(): pl.pallas_call(layer_kernel, out_shape=(jax.ShapeDtypeStruct((tokens, wid...]
    all_to_all x1, waiting for transfers between devices: 4.59 us -> 5.87 us  [on_device(): lax.all_to_all(pick_rows(wanted, cold_table).reshape(table_count, cap_siz...]
    unnamed x6 -> x4, local copies, waits for them, and re-layouts: 3.03 us -> 1.88 us
  transfers between devices with their start and end apart: 20 -> 20, of which waited for: 11 -> 11; matrix products, arithmetic and copies ran while one was open for 6% -> 4% of each run, Pallas kernels for 0% -> 0%
where the time goes in v5:
time: 93.9 us; the launch traced here: 93.4 us
  starting transfers between devices  41.6 us (44%)
  waiting for transfers between devices  25.2 us (27%)
  Pallas kernels  19.1 us (20%)
  local copies, waits for them, and re-layouts  3.47 us (4%)
  other arithmetic  3.24 us (3%)
    pallas_call x1, Pallas kernels, layer(): pl.pallas_call(layer_kernel, out_shape=(jax.ShapeDtypeStruct((tokens, wid...  17.5 us
    ppermute x12, starting transfers between devices, exchange(): lax.ppermute(chunk, axis, shift(groups, k))  15.4 us
    ppermute x3, starting transfers between devices, on_device(): sent = lax.ppermute(hot_part[half:].astype(jnp.bfloat16), 'dp', pairs)  11.4 us
    all_to_all x1, starting transfers between devices, on_device(): lax.all_to_all(by_z, 'dp', split_axis=0, concat_axis=0, tiled=True, axis_...  6.75 us
    ppermute x12, waiting for transfers between devices, exchange(): lax.ppermute(chunk, axis, shift(groups, k))  6.67 us
    all_to_all x1, waiting for transfers between devices, on_device(): lax.all_to_all(pick_rows(wanted, cold_table).reshape(table_count, cap_siz...  5.87 us
    all_to_all x1, waiting for transfers between devices, on_device(): lax.all_to_all(cold_requests, 'table', split_axis=0, concat_axis=0, tiled...  5.19 us
    all_to_all x1, starting transfers between devices, on_device(): lax.all_to_all(cold_requests, 'table', split_axis=0, concat_axis=0, tiled...  4.48 us
  transfers between devices with their start and end apart: 20, of which 11 were waited for; matrix products, arithmetic and copies ran while one was open for 4% of the time, Pallas kernels for 0%

profile of v5, /device:TPU:2, one launch (start us, length us, event | category | flops | bytes accessed | tf_op | source)
XLA Modules:
  0.0 93.4 jit_solution(10543957319175141116)
XLA Ops:
  0.6 4.5 %all-to-all-start = ((s32[8,1,16]{2,1,0:T(1,128)}), s32[8,1,16]{2,1,0:T(1,128)S(1)}, u32[]{:S(2)}, u32[]{:S(2)}) async-start(s32[8,1,16]{2,1,0:T(1,128)} %bitcast.16), calls=%async_computation | async-start | bytes 8192 | tf_op jit(solution)/shard_map/all_to_all | solution.py:367
  5.1 5.2 %all-to-all-done = s32[8,1,16]{2,1,0:T(1,128)S(1)} async-done(((s32[8,1,16]{2,1,0:T(1,128)}), s32[8,1,16]{2,1,0:T(1,128)S(1)}, u32[]{:S(2)}, u32[]{:S(2)}) %all-to-all-start) | async-done | bytes 544 | tf_op jit(solution)/shard_map/all_to_all | solution.py:367
  10.3 1.2 %copy-done = bf16[512,1024]{1,0:T(8,128)(2,1)S(1)} copy-done((bf16[512,1024]{1,0:T(8,128)(2,1)S(1)}, bf16[512,1024]{1,0:T(8,128)(2,1)}, u32[]{:S(2)}) %copy-start) | copy-done | bytes 1048600
  12.6 3.4 %all-to-all-start.1 = ((bf16[8,16,1024]{2,1,0:T(8,128)(2,1)}), bf16[8,16,1024]{2,1,0:T(8,128)(2,1)S(1)}, u32[]{:S(2)}, u32[]{:S(2)}) async-start(bf16[8,16,1024]{2,1,0:T(8,128)(2,1)} %bitcast.5), calls=%async_computation.1 | async-start | bytes 524288 | tf_op jit(solution)/shard_map/all_to_all | solution.py:368
  17.7 5.9 %all-to-all-done.1 = bf16[8,16,1024]{2,1,0:T(8,128)(2,1)S(1)} async-done(((bf16[8,16,1024]{2,1,0:T(8,128)(2,1)}), bf16[8,16,1024]{2,1,0:T(8,128)(2,1)S(1)}, u32[]{:S(2)}, u32[]{:S(2)}) %all-to-all-start.1) | async-done | bytes 262176 | tf_op jit(solution)/shard_map/all_to_all | solution.py:368
  24.2 17.5 %layer.1 = (bf16[512,1024]{1,0:T(8,128)(2,1)}, bf16[320,1024]{1,0:T(8,128)(2,1)S(1)}, bf16[320,1024]{1,0:T(8,128)(2,1)S(1)}) custom-call(s32[1,8]{1,0:T(1,128)S(1)} %copy-done.1, s32[512,1]{1,0:T(8,128)S(1)} %copy.16.source_ref, s32[1,512]{1,0:T(1,128)S(1)} %bitcast.14, bf16[128,1024]{1,0:T(8,128)(2,1)S(1)} %bitcast.11, bf16[512,1024]{1,0:T(8,128)(2,1)} %hot_hbm.1, ...), custom_call_target="tpu_custom_call" | custom-call | flops 8000000000 | bytes 12000000 | tf_op jit(solution)/shard_map/layer/pallas_call | solution.py:244
  41.9 1.9 %collective-permute-done.got_ref = bf16[320,1024]{1,0:T(8,128)(2,1)S(1)} collective-permute-done((bf16[320,1024]{1,0:T(8,128)(2,1)S(1)}, bf16[320,1024]{1,0:T(8,128)(2,1)S(1)}, u32[]{:S(2)}, u32[]{:S(2)}) %collective-permute-start) | collective-permute-done | bytes 655392 | tf_op jit(solution)/shard_map/ppermute | solution.py:406
  44.0 2.2 %collective-permute-start.1 = (bf16[64,1024]{1,0:T(8,128)(2,1)S(1)}, bf16[64,1024]{1,0:T(8,128)(2,1)S(1)}, u32[]{:S(2)}, u32[]{:S(2)}) collective-permute-start(bf16[64,1024]{1,0:T(8,128)(2,1)S(1)} %get-tuple-element.22), channel_id=1, source_target_pairs={{0,2},{1,3},{2,0},{3,1},{4,6},{5,7},{6,4},{7,5},{8,10},{9,11},{10,... | collective-permute-start | bytes 393224 | tf_op jit(solution)/shard_map/ppermute | solution.py:345
  46.5 1.7 %collective-permute-start.3 = (bf16[64,1024]{1,0:T(8,128)(2,1)S(1)}, bf16[64,1024]{1,0:T(8,128)(2,1)S(1)}, u32[]{:S(2)}, u32[]{:S(2)}) collective-permute-start(bf16[64,1024]{1,0:T(8,128)(2,1)S(1)} %get-tuple-element.24), channel_id=1, source_target_pairs={{0,3},{1,0},{2,1},{3,2},{4,7},{5,4},{6,5},{7,6},{8,11},{9,8},{10,9... | collective-permute-start | bytes 393224 | tf_op jit(solution)/shard_map/ppermute | solution.py:345
  48.9 2.0 %collective-permute-start.12 = (bf16[32,1024]{1,0:T(8,128)(2,1)S(1)}, bf16[32,1024]{1,0:T(8,128)(2,1)S(1)}, u32[]{:S(2)}, u32[]{:S(2)}) collective-permute-start(bf16[32,1024]{1,0:T(8,128)(2,1)S(1)} %get-tuple-element.27), channel_id=1, source_target_pairs={{0,128},{64,192},{128,0},{192,64},{32,160},{96,224},{160,32},{224,... | collective-permute-start | bytes 196616 | tf_op jit(solution)/shard_map/ppermute | solution.py:345
  51.9 1.2 %collective-permute-start.13 = (bf16[32,1024]{1,0:T(8,128)(2,1)S(1)}, bf16[32,1024]{1,0:T(8,128)(2,1)S(1)}, u32[]{:S(2)}, u32[]{:S(2)}) collective-permute-start(bf16[32,1024]{1,0:T(8,128)(2,1)S(1)} %get-tuple-element.28), channel_id=1, source_target_pairs={{0,192},{64,0},{128,64},{192,128},{32,224},{96,32},{160,96},{224,1... | collective-permute-start | bytes 196616 | tf_op jit(solution)/shard_map/ppermute | solution.py:345
  54.1 2.0 %collective-permute-start.4 = (bf16[32,1024]{1,0:T(8,128)(2,1)S(1)}, bf16[32,1024]{1,0:T(8,128)(2,1)S(1)}, u32[]{:S(2)}, u32[]{:S(2)}) collective-permute-start(bf16[32,1024]{1,0:T(8,128)(2,1)S(1)} %slice.41), channel_id=1, source_target_pairs={{0,4},{4,0},{8,12},{12,8},{16,20},{20,16},{24,28},{28,24},{1,5},{5... | collective-permute-start | bytes 196616 | tf_op jit(solution)/shard_map/ppermute | solution.py:421
  57.2 2.5 %collective-permute-start.14 = (bf16[128,1024]{1,0:T(8,128)(2,1)S(1)}, bf16[128,1024]{1,0:T(8,128)(2,1)S(1)}, u32[]{:S(2)}, u32[]{:S(2)}) collective-permute-start(bf16[128,1024]{1,0:T(8,128)(2,1)S(1)} %get-tuple-element.30), channel_id=1, source_target_pairs={{0,2},{1,3},{2,0},{3,1},{4,6},{5,7},{6,4},{7,5},{8,10},{9,11},{10,... | collective-permute-start | bytes 786440 | tf_op jit(solution)/shard_map/ppermute | solution.py:345
  60.0 1.7 %collective-permute-start.16 = (bf16[128,1024]{1,0:T(8,128)(2,1)S(1)}, bf16[128,1024]{1,0:T(8,128)(2,1)S(1)}, u32[]{:S(2)}, u32[]{:S(2)}) collective-permute-start(bf16[128,1024]{1,0:T(8,128)(2,1)S(1)} %get-tuple-element.32), channel_id=1, source_target_pairs={{0,3},{1,0},{2,1},{3,2},{4,7},{5,4},{6,5},{7,6},{8,11},{9,8},{10,9... | collective-permute-start | bytes 786440 | tf_op jit(solution)/shard_map/ppermute | solution.py:345
  61.7 3.4 %collective-permute-start.5 = (bf16[16,1024]{1,0:T(8,128)(2,1)S(1)}, bf16[16,1024]{1,0:T(8,128)(2,1)S(1)}, u32[]{:S(2)}, u32[]{:S(2)}) collective-permute-start(bf16[16,1024]{1,0:T(8,128)(2,1)S(1)} %slice.42), channel_id=1, source_target_pairs={{0,8},{4,12},{8,0},{12,4},{16,24},{20,28},{24,16},{28,20},{1,9},{5... | collective-permute-start | bytes 98312 | tf_op jit(solution)/shard_map/ppermute | solution.py:421
  65.1 1.9 %collective-permute-done.5 = bf16[16,1024]{1,0:T(8,128)(2,1)S(1)} collective-permute-done((bf16[16,1024]{1,0:T(8,128)(2,1)S(1)}, bf16[16,1024]{1,0:T(8,128)(2,1)S(1)}, u32[]{:S(2)}, u32[]{:S(2)}) %collective-permute-start.5) | collective-permute-done | bytes 32800 | tf_op jit(solution)/shard_map/ppermute | solution.py:421
  67.0 6.1 %collective-permute-start.6 = (bf16[8,1024]{1,0:T(8,128)(2,1)S(1)}, bf16[8,1024]{1,0:T(8,128)(2,1)S(1)}, u32[]{:S(2)}, u32[]{:S(2)}) collective-permute-start(bf16[8,1024]{1,0:T(8,128)(2,1)S(1)} %slice.43), channel_id=1, source_target_pairs={{0,16},{4,20},{8,24},{12,28},{16,0},{20,4},{24,8},{28,12},{1,17},{... | collective-permute-start | bytes 49160 | tf_op jit(solution)/shard_map/ppermute | solution.py:421
  74.0 6.8 %all-to-all-start.2 = ((bf16[8,16,1024]{2,1,0:T(8,128)(2,1)}), bf16[8,16,1024]{2,1,0:T(8,128)(2,1)S(1)}, u32[]{:S(2)}, u32[]{:S(2)}) async-start(bf16[8,16,1024]{2,1,0:T(8,128)(2,1)} %bitcast.8), calls=%async_computation.2 | async-start | bytes 524288 | tf_op jit(solution)/shard_map/all_to_all | solution.py:424
  80.7 1.2 %collective-permute-start.9 = (f32[8,1024]{1,0:T(8,128)S(1)}, f32[8,1024]{1,0:T(8,128)S(1)}, u32[]{:S(2)}, u32[]{:S(2)}) collective-permute-start(f32[8,1024]{1,0:T(8,128)S(1)} %slice_add_fusion.2), channel_id=1, source_target_pairs={{0,192},{64,0},{128,64},{192,128},{32,224},{96,32},{160,96},{224,1... | collective-permute-start | bytes 98312 | tf_op jit(solution)/shard_map/ppermute | solution.py:345
  83.5 1.2 %collective-permute-done.9 = f32[8,1024]{1,0:T(8,128)S(1)} collective-permute-done((f32[8,1024]{1,0:T(8,128)S(1)}, f32[8,1024]{1,0:T(8,128)S(1)}, u32[]{:S(2)}, u32[]{:S(2)}) %collective-permute-start.9) | collective-permute-done | bytes 32800 | tf_op jit(solution)/shard_map/ppermute | solution.py:345
  84.7 2.4 %collective-permute-done.8 = f32[8,1024]{1,0:T(8,128)S(1)} collective-permute-done((f32[8,1024]{1,0:T(8,128)S(1)}, f32[8,1024]{1,0:T(8,128)S(1)}, u32[]{:S(2)}, u32[]{:S(2)}) %collective-permute-start.8) | collective-permute-done | bytes 32800 | tf_op jit(solution)/shard_map/ppermute | solution.py:345
  87.1 1.2 %collective-permute-done.7 = f32[8,1024]{1,0:T(8,128)S(1)} collective-permute-done((f32[8,1024]{1,0:T(8,128)S(1)}, f32[8,1024]{1,0:T(8,128)S(1)}, u32[]{:S(2)}, u32[]{:S(2)}) %collective-permute-start.7) | collective-permute-done | bytes 32800 | tf_op jit(solution)/shard_map/ppermute | solution.py:345
  88.4 1.2 %collective-permute-done.10 = f32[4,1,2,1024]{3,2,0,1:T(2,128)S(1)} collective-permute-done((f32[4,1,2,1024]{3,2,0,1:T(2,128)S(1)}, f32[4,1,2,1024]{3,2,0,1:T(2,128)S(1)}, u32[]{:S(2)}, u32[]{:S(2)}) %collective-permute-start.10) | collective-permute-done | bytes 32800 | tf_op jit(solution)/shard_map/ppermute | solution.py:429
  90.3 2.5 %all-to-all-done.2 = bf16[8,16,1024]{2,1,0:T(8,128)(2,1)S(1)} async-done(((bf16[8,16,1024]{2,1,0:T(8,128)(2,1)}), bf16[8,16,1024]{2,1,0:T(8,128)(2,1)S(1)}, u32[]{:S(2)}, u32[]{:S(2)}) %all-to-all-start.2) | async-done | bytes 262176 | tf_op jit(solution)/shard_map/all_to_all | solution.py:424
  (50 shorter events, 12.2 us)
Async XLA Ops:
  0.6 9.7 %all-to-all-start = ((s32[8,1,16]{2,1,0:T(1,128)}), s32[8,1,16]{2,1,0:T(1,128)S(1)}, u32[]{:S(2)}, u32[]{:S(2)}) async-start(s32[8,1,16]{2,1,0:T(1,128)} %bitcast.16), calls=%async_computation | async-start | bytes 8192 | tf_op jit(solution)/shard_map/all_to_all | solution.py:367
  10.3 1.2 %copy-start = (bf16[512,1024]{1,0:T(8,128)(2,1)S(1)}, bf16[512,1024]{1,0:T(8,128)(2,1)}, u32[]{:S(2)}) copy-start(bf16[512,1024]{1,0:T(8,128)(2,1)} %table_ref.1) | copy-start | bytes 3145732
  12.6 10.9 %all-to-all-start.1 = ((bf16[8,16,1024]{2,1,0:T(8,128)(2,1)}), bf16[8,16,1024]{2,1,0:T(8,128)(2,1)S(1)}, u32[]{:S(2)}, u32[]{:S(2)}) async-start(bf16[8,16,1024]{2,1,0:T(8,128)(2,1)} %bitcast.5), calls=%async_computation.1 | async-start | bytes 524288 | tf_op jit(solution)/shard_map/all_to_all | solution.py:368
  23.5 0.7 copy-start.1
  41.6 2.2 %collective-permute-start = (bf16[320,1024]{1,0:T(8,128)(2,1)S(1)}, bf16[320,1024]{1,0:T(8,128)(2,1)S(1)}, u32[]{:S(2)}, u32[]{:S(2)}) collective-permute-start(bf16[320,1024]{1,0:T(8,128)(2,1)S(1)} %get-tuple-element.20), channel_id=1, source_target_pairs={{0,32},{32,0},{64,96},{96,64},{128,160},{160,128},{192,224},{224,1... | collective-permute-start | bytes 1966088 | tf_op jit(solution)/shard_map/ppermute | solution.py:406
  44.0 7.9 %collective-permute-start.1 = (bf16[64,1024]{1,0:T(8,128)(2,1)S(1)}, bf16[64,1024]{1,0:T(8,128)(2,1)S(1)}, u32[]{:S(2)}, u32[]{:S(2)}) collective-permute-start(bf16[64,1024]{1,0:T(8,128)(2,1)S(1)} %get-tuple-element.22), channel_id=1, source_target_pairs={{0,2},{1,3},{2,0},{3,1},{4,6},{5,7},{6,4},{7,5},{8,10},{9,11},{10,... | collective-permute-start | bytes 393224 | tf_op jit(solution)/shard_map/ppermute | solution.py:345
  46.2 7.8 %collective-permute-start.2 = (bf16[64,1024]{1,0:T(8,128)(2,1)S(1)}, bf16[64,1024]{1,0:T(8,128)(2,1)S(1)}, u32[]{:S(2)}, u32[]{:S(2)}) collective-permute-start(bf16[64,1024]{1,0:T(8,128)(2,1)S(1)} %get-tuple-element.23), channel_id=1, source_target_pairs={{0,1},{1,2},{2,3},{3,0},{4,5},{5,6},{6,7},{7,4},{8,9},{9,10},{10,1... | collective-permute-start | bytes 393224 | tf_op jit(solution)/shard_map/ppermute | solution.py:345
  46.5 7.4 %collective-permute-start.3 = (bf16[64,1024]{1,0:T(8,128)(2,1)S(1)}, bf16[64,1024]{1,0:T(8,128)(2,1)S(1)}, u32[]{:S(2)}, u32[]{:S(2)}) collective-permute-start(bf16[64,1024]{1,0:T(8,128)(2,1)S(1)} %get-tuple-element.24), channel_id=1, source_target_pairs={{0,3},{1,0},{2,1},{3,2},{4,7},{5,4},{6,5},{7,6},{8,11},{9,8},{10,9... | collective-permute-start | bytes 393224 | tf_op jit(solution)/shard_map/ppermute | solution.py:345
  48.2 8.5 %collective-permute-start.11 = (bf16[32,1024]{1,0:T(8,128)(2,1)S(1)}, bf16[32,1024]{1,0:T(8,128)(2,1)S(1)}, u32[]{:S(2)}, u32[]{:S(2)}) collective-permute-start(bf16[32,1024]{1,0:T(8,128)(2,1)S(1)} %get-tuple-element.26), channel_id=1, source_target_pairs={{0,64},{64,128},{128,192},{192,0},{32,96},{96,160},{160,224},{224,... | collective-permute-start | bytes 196616 | tf_op jit(solution)/shard_map/ppermute | solution.py:345
  48.9 7.9 %collective-permute-start.12 = (bf16[32,1024]{1,0:T(8,128)(2,1)S(1)}, bf16[32,1024]{1,0:T(8,128)(2,1)S(1)}, u32[]{:S(2)}, u32[]{:S(2)}) collective-permute-start(bf16[32,1024]{1,0:T(8,128)(2,1)S(1)} %get-tuple-element.27), channel_id=1, source_target_pairs={{0,128},{64,192},{128,0},{192,64},{32,160},{96,224},{160,32},{224,... | collective-permute-start | bytes 196616 | tf_op jit(solution)/shard_map/ppermute | solution.py:345
  51.9 4.8 %collective-permute-start.13 = (bf16[32,1024]{1,0:T(8,128)(2,1)S(1)}, bf16[32,1024]{1,0:T(8,128)(2,1)S(1)}, u32[]{:S(2)}, u32[]{:S(2)}) collective-permute-start(bf16[32,1024]{1,0:T(8,128)(2,1)S(1)} %get-tuple-element.28), channel_id=1, source_target_pairs={{0,192},{64,0},{128,64},{192,128},{32,224},{96,32},{160,96},{224,1... | collective-permute-start | bytes 196616 | tf_op jit(solution)/shard_map/ppermute | solution.py:345
  54.1 7.6 %collective-permute-start.4 = (bf16[32,1024]{1,0:T(8,128)(2,1)S(1)}, bf16[32,1024]{1,0:T(8,128)(2,1)S(1)}, u32[]{:S(2)}, u32[]{:S(2)}) collective-permute-start(bf16[32,1024]{1,0:T(8,128)(2,1)S(1)} %slice.41), channel_id=1, source_target_pairs={{0,4},{4,0},{8,12},{12,8},{16,20},{20,16},{24,28},{28,24},{1,5},{5... | collective-permute-start | bytes 196616 | tf_op jit(solution)/shard_map/ppermute | solution.py:421
  57.2 15.9 %collective-permute-start.14 = (bf16[128,1024]{1,0:T(8,128)(2,1)S(1)}, bf16[128,1024]{1,0:T(8,128)(2,1)S(1)}, u32[]{:S(2)}, u32[]{:S(2)}) collective-permute-start(bf16[128,1024]{1,0:T(8,128)(2,1)S(1)} %get-tuple-element.30), channel_id=1, source_target_pairs={{0,2},{1,3},{2,0},{3,1},{4,6},{5,7},{6,4},{7,5},{8,10},{9,11},{10,... | collective-permute-start | bytes 786440 | tf_op jit(solution)/shard_map/ppermute | solution.py:345
  59.6 13.4 %collective-permute-start.15 = (bf16[128,1024]{1,0:T(8,128)(2,1)S(1)}, bf16[128,1024]{1,0:T(8,128)(2,1)S(1)}, u32[]{:S(2)}, u32[]{:S(2)}) collective-permute-start(bf16[128,1024]{1,0:T(8,128)(2,1)S(1)} %get-tuple-element.31), channel_id=1, source_target_pairs={{0,1},{1,2},{2,3},{3,0},{4,5},{5,6},{6,7},{7,4},{8,9},{9,10},{10,1... | collective-permute-start | bytes 786440 | tf_op jit(solution)/shard_map/ppermute | solution.py:345
  60.0 13.1 %collective-permute-start.16 = (bf16[128,1024]{1,0:T(8,128)(2,1)S(1)}, bf16[128,1024]{1,0:T(8,128)(2,1)S(1)}, u32[]{:S(2)}, u32[]{:S(2)}) collective-permute-start(bf16[128,1024]{1,0:T(8,128)(2,1)S(1)} %get-tuple-element.32), channel_id=1, source_target_pairs={{0,3},{1,0},{2,1},{3,2},{4,7},{5,4},{6,5},{7,6},{8,11},{9,8},{10,9... | collective-permute-start | bytes 786440 | tf_op jit(solution)/shard_map/ppermute | solution.py:345
  61.7 5.2 %collective-permute-start.5 = (bf16[16,1024]{1,0:T(8,128)(2,1)S(1)}, bf16[16,1024]{1,0:T(8,128)(2,1)S(1)}, u32[]{:S(2)}, u32[]{:S(2)}) collective-permute-start(bf16[16,1024]{1,0:T(8,128)(2,1)S(1)} %slice.42), channel_id=1, source_target_pairs={{0,8},{4,12},{8,0},{12,4},{16,24},{20,28},{24,16},{28,20},{1,9},{5... | collective-permute-start | bytes 98312 | tf_op jit(solution)/shard_map/ppermute | solution.py:421
  67.0 13.7 %collective-permute-start.6 = (bf16[8,1024]{1,0:T(8,128)(2,1)S(1)}, bf16[8,1024]{1,0:T(8,128)(2,1)S(1)}, u32[]{:S(2)}, u32[]{:S(2)}) collective-permute-start(bf16[8,1024]{1,0:T(8,128)(2,1)S(1)} %slice.43), channel_id=1, source_target_pairs={{0,16},{4,20},{8,24},{12,28},{16,0},{20,4},{24,8},{28,12},{1,17},{... | collective-permute-start | bytes 49160 | tf_op jit(solution)/shard_map/ppermute | solution.py:421
  74.0 18.8 %all-to-all-start.2 = ((bf16[8,16,1024]{2,1,0:T(8,128)(2,1)}), bf16[8,16,1024]{2,1,0:T(8,128)(2,1)S(1)}, u32[]{:S(2)}, u32[]{:S(2)}) async-start(bf16[8,16,1024]{2,1,0:T(8,128)(2,1)} %bitcast.8), calls=%async_computation.2 | async-start | bytes 524288 | tf_op jit(solution)/shard_map/all_to_all | solution.py:424
  80.7 4.0 %collective-permute-start.9 = (f32[8,1024]{1,0:T(8,128)S(1)}, f32[8,1024]{1,0:T(8,128)S(1)}, u32[]{:S(2)}, u32[]{:S(2)}) collective-permute-start(f32[8,1024]{1,0:T(8,128)S(1)} %slice_add_fusion.2), channel_id=1, source_target_pairs={{0,192},{64,0},{128,64},{192,128},{32,224},{96,32},{160,96},{224,1... | collective-permute-start | bytes 98312 | tf_op jit(solution)/shard_map/ppermute | solution.py:345
  82.0 5.1 %collective-permute-start.8 = (f32[8,1024]{1,0:T(8,128)S(1)}, f32[8,1024]{1,0:T(8,128)S(1)}, u32[]{:S(2)}, u32[]{:S(2)}) collective-permute-start(f32[8,1024]{1,0:T(8,128)S(1)} %slice_add_fusion.2), channel_id=1, source_target_pairs={{0,64},{64,128},{128,192},{192,0},{32,96},{96,160},{160,224},{224,... | collective-permute-start | bytes 98312 | tf_op jit(solution)/shard_map/ppermute | solution.py:345
  82.8 5.4 %collective-permute-start.7 = (f32[8,1024]{1,0:T(8,128)S(1)}, f32[8,1024]{1,0:T(8,128)S(1)}, u32[]{:S(2)}, u32[]{:S(2)}) collective-permute-start(f32[8,1024]{1,0:T(8,128)S(1)} %slice_add_fusion.2), channel_id=1, source_target_pairs={{0,128},{64,192},{128,0},{192,64},{32,160},{96,224},{160,32},{224,... | collective-permute-start | bytes 98312 | tf_op jit(solution)/shard_map/ppermute | solution.py:345
  88.3 1.3 %collective-permute-start.10 = (f32[4,1,2,1024]{3,2,0,1:T(2,128)S(1)}, f32[4,1,2,1024]{3,2,0,1:T(2,128)S(1)}, u32[]{:S(2)}, u32[]{:S(2)}) collective-permute-start(f32[4,1,2,1024]{3,2,0,1:T(2,128)S(1)} %reshape.102), channel_id=1, source_target_pairs={{0,32},{32,0},{64,96},{96,64},{128,160},{160,128},{192,224},{224,1... | collective-permute-start | bytes 98312 | tf_op jit(solution)/shard_map/ppermute | solution.py:429

commit v6 on v5

--- a/solution.py
+++ b/solution.py
@@ -31,6 +31,26 @@
 
 def dot_tn(a, b):
     return lax.dot_general(a, b, (((0,), (0,)), ((), ())), preferred_element_type=jnp.float32)
+
+
+def bring_kernel(after_ref, table_hbm, table_ref, sem):
+    copy = pltpu.make_async_copy(table_hbm, table_ref, sem)
+    copy.start()
+    copy.wait()
+
+
+def bring(table, after):
+    vmem = pl.BlockSpec(memory_space=pltpu.VMEM)
+    return pl.pallas_call(
+        bring_kernel,
+        out_shape=jax.ShapeDtypeStruct(table.shape, table.dtype),
+        in_specs=[vmem, pl.BlockSpec(memory_space=pl.ANY)],
+        out_specs=vmem,
+        scratch_shapes=[pltpu.SemaphoreType.DMA],
+        compiler_params=pltpu.CompilerParams(vmem_limit_bytes=4 * 1024 * 1024),
+        cost_estimate=pl.CostEstimate(flops=0, bytes_accessed=2 * 10**6, transcendentals=0),
+        name="bring",
+    )(after, table)
 
 
 def pick_kernel(wanted_ref, table_ref, rows_ref):
@@ -58,7 +78,7 @@
 
 
 def layer_kernel(
-    lengths_ref,
+    ends_ref,
     source_ref,
     place_ref,
     fetched_hbm,
@@ -104,7 +124,6 @@
     for copy in (hot_copy, fetched_copy, w_in_copy, w_out_copy, out_grad_copy):
         copy.start()
     hot_copy.wait()
-    fetched_copy.wait()
 
     for block in range(tokens // 256):
         at = pl.ds(block * 256, 256)
@@ -113,7 +132,10 @@
         slot_pick = (
             source == lax.broadcasted_iota(jnp.int32, (256, slot_count), 1) + hot_rows
         ).astype(bf16)
-        rows = dot_nn(hot_pick, hot_ref[...]) + dot_nn(slot_pick, fetched_ref[...])
+        rows = dot_nn(hot_pick, hot_ref[...])
+        if block == 0:
+            fetched_copy.wait()
+        rows = rows + dot_nn(slot_pick, fetched_ref[...])
         centered = rows - mean_of(rows)
         rstd = lax.rsqrt(mean_of(centered * centered) + EPS)
         rows_ref[at, :] = rows.astype(bf16)
@@ -142,9 +164,9 @@
         begin = jnp.zeros((BLOCK, 1), jnp.int32)
         length = jnp.zeros((BLOCK, 1), jnp.int32)
         end = jnp.int32(0)
-        for history in range(lengths_ref.shape[1]):
+        for history in range(ends_ref.shape[1]):
             start = end
-            end = start + lengths_ref[0, history]
+            end = ends_ref[0, history]
             inside = position >= start
             begin = jnp.where(inside, start, begin)
             length = jnp.where(inside, end - start, length)
@@ -241,6 +263,12 @@
     vmem = pl.BlockSpec(memory_space=pltpu.VMEM)
     hbm = pl.BlockSpec(memory_space=pl.ANY)
     reach = (BACK + 1) * BLOCK
+    before = lax.iota(jnp.int32, lengths.shape[1])
+    ends = jnp.sum(
+        jnp.where(before[:, None] <= before[None, :], lengths.reshape(-1, 1), 0),
+        axis=0,
+        keepdims=True,
+    )
     return pl.pallas_call(
         layer_kernel,
         out_shape=(
@@ -274,7 +302,7 @@
         compiler_params=pltpu.CompilerParams(vmem_limit_bytes=52 * 1024 * 1024),
         cost_estimate=pl.CostEstimate(flops=8 * 10**9, bytes_accessed=12 * 10**6, transcendentals=0),
         name="layer",
-    )(lengths, source, place, fetched, hot_table, w_in, w_out, out_grad)
+    )(ends, source, place, fetched, hot_table, w_in, w_out, out_grad)
 
 
 def core_sums_kernel(near_ref, got_ref, *out_refs):
@@ -366,7 +394,7 @@
 
     wanted = lax.all_to_all(cold_requests, "table", split_axis=0, concat_axis=0, tiled=True)
     fetched = lax.all_to_all(
-        pick_rows(wanted, cold_table).reshape(table_count, cap_size, model_width),
+        pick_rows(wanted, bring(cold_table, cold_requests)).reshape(table_count, cap_size, model_width),
         "table",
         split_axis=0,
         concat_axis=0,

time: 93.9 us -> 92.2 us (0.982)
  waiting for transfers between devices: 25.2 us -> 23.1 us
    all_to_all x1, waiting for transfers between devices: 5.19 us -> 2.44 us  [on_device(): lax.all_to_all(cold_requests, 'table', split_axis=0, concat_axis=0, tiled...]
    unnamed x4 -> x6, local copies, waits for them, and re-layouts: 1.88 us -> 1.91 us
  transfers between devices with their start and end apart: 20 -> 20, of which waited for: 11 -> 11; matrix products, arithmetic and copies ran while one was open for 4% -> 5% of each run, Pallas kernels for 0% -> 1%
where the time goes in v6:
time: 92.2 us; the launch traced here: 91.7 us
  starting transfers between devices  41.6 us (45%)
  waiting for transfers between devices  23.1 us (25%)
  Pallas kernels  19.3 us (21%)
  local copies, waits for them, and re-layouts  3.5 us (4%)
  other arithmetic  3.33 us (4%)
    pallas_call x1, Pallas kernels, layer(): pl.pallas_call(layer_kernel, out_shape=(jax.ShapeDtypeStruct((tokens, wid...  17.6 us
    ppermute x12, starting transfers between devices, exchange(): lax.ppermute(chunk, axis, shift(groups, k))  15.4 us
    ppermute x3, starting transfers between devices, on_device(): sent = lax.ppermute(hot_part[half:].astype(jnp.bfloat16), 'dp', pairs)  11.5 us
    all_to_all x1, starting transfers between devices, on_device(): lax.all_to_all(by_z, 'dp', split_axis=0, concat_axis=0, tiled=True, axis_...  6.74 us
    ppermute x12, waiting for transfers between devices, exchange(): lax.ppermute(chunk, axis, shift(groups, k))  6.66 us
    all_to_all x1, waiting for transfers between devices, on_device(): lax.all_to_all(pick_rows(wanted, bring(cold_table, cold_requests)).reshap...  6.52 us
    all_to_all x1, starting transfers between devices, on_device(): lax.all_to_all(cold_requests, 'table', split_axis=0, concat_axis=0, tiled...  4.48 us
    all_to_all x1, starting transfers between devices, on_device(): lax.all_to_all(pick_rows(wanted, bring(cold_table, cold_requests)).reshap...  3.41 us
  transfers between devices with their start and end apart: 20, of which 11 were waited for; matrix products, arithmetic and copies ran while one was open for 5% of the time, Pallas kernels for 1%

profile of v6, /device:TPU:2, one launch (start us, length us, event | category | flops | bytes accessed | tf_op | source)
XLA Modules:
  0.0 91.7 jit_solution(13461571821989309617)
XLA Ops:
  0.6 4.5 %all-to-all-start = ((s32[8,1,16]{2,1,0:T(1,128)}), s32[8,1,16]{2,1,0:T(1,128)S(1)}, u32[]{:S(2)}, u32[]{:S(2)}) async-start(s32[8,1,16]{2,1,0:T(1,128)} %bitcast.16), calls=%async_computation | async-start | bytes 8192 | tf_op jit(solution)/shard_map/all_to_all | solution.py:395
  5.9 1.2 %copy-done = bf16[512,1024]{1,0:T(8,128)(2,1)S(1)} copy-done((bf16[512,1024]{1,0:T(8,128)(2,1)S(1)}, bf16[512,1024]{1,0:T(8,128)(2,1)}, u32[]{:S(2)}) %copy-start) | copy-done | bytes 1048600
  7.9 2.4 %all-to-all-done = s32[8,1,16]{2,1,0:T(1,128)S(1)} async-done(((s32[8,1,16]{2,1,0:T(1,128)}), s32[8,1,16]{2,1,0:T(1,128)S(1)}, u32[]{:S(2)}, u32[]{:S(2)}) %all-to-all-start) | async-done | bytes 544 | tf_op jit(solution)/shard_map/all_to_all | solution.py:395
  11.4 3.4 %all-to-all-start.1 = ((bf16[8,16,1024]{2,1,0:T(8,128)(2,1)}), bf16[8,16,1024]{2,1,0:T(8,128)(2,1)S(1)}, u32[]{:S(2)}, u32[]{:S(2)}) async-start(bf16[8,16,1024]{2,1,0:T(8,128)(2,1)} %bitcast.7), calls=%async_computation.1 | async-start | bytes 524288 | tf_op jit(solution)/shard_map/all_to_all | solution.py:396
  15.8 6.5 %all-to-all-done.1 = bf16[8,16,1024]{2,1,0:T(8,128)(2,1)S(1)} async-done(((bf16[8,16,1024]{2,1,0:T(8,128)(2,1)}), bf16[8,16,1024]{2,1,0:T(8,128)(2,1)S(1)}, u32[]{:S(2)}, u32[]{:S(2)}) %all-to-all-start.1) | async-done | bytes 262176 | tf_op jit(solution)/shard_map/all_to_all | solution.py:396
  22.3 17.6 %layer.1 = (bf16[512,1024]{1,0:T(8,128)(2,1)}, bf16[320,1024]{1,0:T(8,128)(2,1)S(1)}, bf16[320,1024]{1,0:T(8,128)(2,1)S(1)}) custom-call(s32[1,8]{1,0:T(1,128)S(1)} %bitcast.18, s32[512,1]{1,0:T(8,128)S(1)} %copy.19.source_ref, s32[1,512]{1,0:T(1,128)S(1)} %bitcast.17, bf16[128,1024]{1,0:T(8,128)(2,1)S(1)} %bitcast.13, bf16[512,1024]{1,0:T(8,128)(2,1)} %hot_hbm.1, ...), custom_call_target="tpu_custom_call" | custom-call | flops 8000000000 | bytes 12000000 | tf_op jit(solution)/shard_map/layer/pallas_call | solution.py:272
  40.2 1.9 %collective-permute-done.got_ref = bf16[320,1024]{1,0:T(8,128)(2,1)S(1)} collective-permute-done((bf16[320,1024]{1,0:T(8,128)(2,1)S(1)}, bf16[320,1024]{1,0:T(8,128)(2,1)S(1)}, u32[]{:S(2)}, u32[]{:S(2)}) %collective-permute-start) | collective-permute-done | bytes 655392 | tf_op jit(solution)/shard_map/ppermute | solution.py:434
  42.2 2.2 %collective-permute-start.1 = (bf16[64,1024]{1,0:T(8,128)(2,1)S(1)}, bf16[64,1024]{1,0:T(8,128)(2,1)S(1)}, u32[]{:S(2)}, u32[]{:S(2)}) collective-permute-start(bf16[64,1024]{1,0:T(8,128)(2,1)S(1)} %get-tuple-element.22), channel_id=1, source_target_pairs={{0,2},{1,3},{2,0},{3,1},{4,6},{5,7},{6,4},{7,5},{8,10},{9,11},{10,... | collective-permute-start | bytes 393224 | tf_op jit(solution)/shard_map/ppermute | solution.py:373
  44.8 1.7 %collective-permute-start.3 = (bf16[64,1024]{1,0:T(8,128)(2,1)S(1)}, bf16[64,1024]{1,0:T(8,128)(2,1)S(1)}, u32[]{:S(2)}, u32[]{:S(2)}) collective-permute-start(bf16[64,1024]{1,0:T(8,128)(2,1)S(1)} %get-tuple-element.24), channel_id=1, source_target_pairs={{0,3},{1,0},{2,1},{3,2},{4,7},{5,4},{6,5},{7,6},{8,11},{9,8},{10,9... | collective-permute-start | bytes 393224 | tf_op jit(solution)/shard_map/ppermute | solution.py:373
  47.1 2.0 %collective-permute-start.12 = (bf16[32,1024]{1,0:T(8,128)(2,1)S(1)}, bf16[32,1024]{1,0:T(8,128)(2,1)S(1)}, u32[]{:S(2)}, u32[]{:S(2)}) collective-permute-start(bf16[32,1024]{1,0:T(8,128)(2,1)S(1)} %get-tuple-element.27), channel_id=1, source_target_pairs={{0,128},{64,192},{128,0},{192,64},{32,160},{96,224},{160,32},{224,... | collective-permute-start | bytes 196616 | tf_op jit(solution)/shard_map/ppermute | solution.py:373
  50.2 1.2 %collective-permute-start.13 = (bf16[32,1024]{1,0:T(8,128)(2,1)S(1)}, bf16[32,1024]{1,0:T(8,128)(2,1)S(1)}, u32[]{:S(2)}, u32[]{:S(2)}) collective-permute-start(bf16[32,1024]{1,0:T(8,128)(2,1)S(1)} %get-tuple-element.28), channel_id=1, source_target_pairs={{0,192},{64,0},{128,64},{192,128},{32,224},{96,32},{160,96},{224,1... | collective-permute-start | bytes 196616 | tf_op jit(solution)/shard_map/ppermute | solution.py:373
  52.3 2.0 %collective-permute-start.4 = (bf16[32,1024]{1,0:T(8,128)(2,1)S(1)}, bf16[32,1024]{1,0:T(8,128)(2,1)S(1)}, u32[]{:S(2)}, u32[]{:S(2)}) collective-permute-start(bf16[32,1024]{1,0:T(8,128)(2,1)S(1)} %slice.41), channel_id=1, source_target_pairs={{0,4},{4,0},{8,12},{12,8},{16,20},{20,16},{24,28},{28,24},{1,5},{5... | collective-permute-start | bytes 196616 | tf_op jit(solution)/shard_map/ppermute | solution.py:449
  55.5 2.5 %collective-permute-start.14 = (bf16[128,1024]{1,0:T(8,128)(2,1)S(1)}, bf16[128,1024]{1,0:T(8,128)(2,1)S(1)}, u32[]{:S(2)}, u32[]{:S(2)}) collective-permute-start(bf16[128,1024]{1,0:T(8,128)(2,1)S(1)} %get-tuple-element.30), channel_id=1, source_target_pairs={{0,2},{1,3},{2,0},{3,1},{4,6},{5,7},{6,4},{7,5},{8,10},{9,11},{10,... | collective-permute-start | bytes 786440 | tf_op jit(solution)/shard_map/ppermute | solution.py:373
  58.2 1.7 %collective-permute-start.16 = (bf16[128,1024]{1,0:T(8,128)(2,1)S(1)}, bf16[128,1024]{1,0:T(8,128)(2,1)S(1)}, u32[]{:S(2)}, u32[]{:S(2)}) collective-permute-start(bf16[128,1024]{1,0:T(8,128)(2,1)S(1)} %get-tuple-element.32), channel_id=1, source_target_pairs={{0,3},{1,0},{2,1},{3,2},{4,7},{5,4},{6,5},{7,6},{8,11},{9,8},{10,9... | collective-permute-start | bytes 786440 | tf_op jit(solution)/shard_map/ppermute | solution.py:373
  60.0 3.4 %collective-permute-start.5 = (bf16[16,1024]{1,0:T(8,128)(2,1)S(1)}, bf16[16,1024]{1,0:T(8,128)(2,1)S(1)}, u32[]{:S(2)}, u32[]{:S(2)}) collective-permute-start(bf16[16,1024]{1,0:T(8,128)(2,1)S(1)} %slice.42), channel_id=1, source_target_pairs={{0,8},{4,12},{8,0},{12,4},{16,24},{20,28},{24,16},{28,20},{1,9},{5... | collective-permute-start | bytes 98312 | tf_op jit(solution)/shard_map/ppermute | solution.py:449
  63.3 1.9 %collective-permute-done.5 = bf16[16,1024]{1,0:T(8,128)(2,1)S(1)} collective-permute-done((bf16[16,1024]{1,0:T(8,128)(2,1)S(1)}, bf16[16,1024]{1,0:T(8,128)(2,1)S(1)}, u32[]{:S(2)}, u32[]{:S(2)}) %collective-permute-start.5) | collective-permute-done | bytes 32800 | tf_op jit(solution)/shard_map/ppermute | solution.py:449
  65.3 6.1 %collective-permute-start.6 = (bf16[8,1024]{1,0:T(8,128)(2,1)S(1)}, bf16[8,1024]{1,0:T(8,128)(2,1)S(1)}, u32[]{:S(2)}, u32[]{:S(2)}) collective-permute-start(bf16[8,1024]{1,0:T(8,128)(2,1)S(1)} %slice.43), channel_id=1, source_target_pairs={{0,16},{4,20},{8,24},{12,28},{16,0},{20,4},{24,8},{28,12},{1,17},{... | collective-permute-start | bytes 49160 | tf_op jit(solution)/shard_map/ppermute | solution.py:449
  72.2 6.7 %all-to-all-start.2 = ((bf16[8,16,1024]{2,1,0:T(8,128)(2,1)}), bf16[8,16,1024]{2,1,0:T(8,128)(2,1)S(1)}, u32[]{:S(2)}, u32[]{:S(2)}) async-start(bf16[8,16,1024]{2,1,0:T(8,128)(2,1)} %bitcast.10), calls=%async_computation.2 | async-start | bytes 524288 | tf_op jit(solution)/shard_map/all_to_all | solution.py:452
  79.0 1.2 %collective-permute-start.9 = (f32[8,1024]{1,0:T(8,128)S(1)}, f32[8,1024]{1,0:T(8,128)S(1)}, u32[]{:S(2)}, u32[]{:S(2)}) collective-permute-start(f32[8,1024]{1,0:T(8,128)S(1)} %slice_add_fusion.2), channel_id=1, source_target_pairs={{0,192},{64,0},{128,64},{192,128},{32,224},{96,32},{160,96},{224,1... | collective-permute-start | bytes 98312 | tf_op jit(solution)/shard_map/ppermute | solution.py:373
  81.8 1.2 %collective-permute-done.9 = f32[8,1024]{1,0:T(8,128)S(1)} collective-permute-done((f32[8,1024]{1,0:T(8,128)S(1)}, f32[8,1024]{1,0:T(8,128)S(1)}, u32[]{:S(2)}, u32[]{:S(2)}) %collective-permute-start.9) | collective-permute-done | bytes 32800 | tf_op jit(solution)/shard_map/ppermute | solution.py:373
  83.0 2.4 %collective-permute-done.8 = f32[8,1024]{1,0:T(8,128)S(1)} collective-permute-done((f32[8,1024]{1,0:T(8,128)S(1)}, f32[8,1024]{1,0:T(8,128)S(1)}, u32[]{:S(2)}, u32[]{:S(2)}) %collective-permute-start.8) | collective-permute-done | bytes 32800 | tf_op jit(solution)/shard_map/ppermute | solution.py:373
  85.4 1.2 %collective-permute-done.7 = f32[8,1024]{1,0:T(8,128)S(1)} collective-permute-done((f32[8,1024]{1,0:T(8,128)S(1)}, f32[8,1024]{1,0:T(8,128)S(1)}, u32[]{:S(2)}, u32[]{:S(2)}) %collective-permute-start.7) | collective-permute-done | bytes 32800 | tf_op jit(solution)/shard_map/ppermute | solution.py:373
  86.7 1.2 %collective-permute-done.10 = f32[4,1,2,1024]{3,2,0,1:T(2,128)S(1)} collective-permute-done((f32[4,1,2,1024]{3,2,0,1:T(2,128)S(1)}, f32[4,1,2,1024]{3,2,0,1:T(2,128)S(1)}, u32[]{:S(2)}, u32[]{:S(2)}) %collective-permute-start.10) | collective-permute-done | bytes 32800 | tf_op jit(solution)/shard_map/ppermute | solution.py:457
  88.6 2.5 %all-to-all-done.2 = bf16[8,16,1024]{2,1,0:T(8,128)(2,1)S(1)} async-done(((bf16[8,16,1024]{2,1,0:T(8,128)(2,1)}), bf16[8,16,1024]{2,1,0:T(8,128)(2,1)S(1)}, u32[]{:S(2)}, u32[]{:S(2)}) %all-to-all-start.2) | async-done | bytes 262176 | tf_op jit(solution)/shard_map/all_to_all | solution.py:452
  (54 shorter events, 12.4 us)
Async XLA Ops:
  0.6 15.1 %copy-start.2 = (s32[1,8]{1,0:T(1,128)S(1)}, s32[1,8]{1,0:T(1,128)}, u32[]{:S(2)}) copy-start(s32[1,8]{1,0:T(1,128)} %param.13) | copy-start | bytes 100
  0.6 9.7 %all-to-all-start = ((s32[8,1,16]{2,1,0:T(1,128)}), s32[8,1,16]{2,1,0:T(1,128)S(1)}, u32[]{:S(2)}, u32[]{:S(2)}) async-start(s32[8,1,16]{2,1,0:T(1,128)} %bitcast.16), calls=%async_computation | async-start | bytes 8192 | tf_op jit(solution)/shard_map/all_to_all | solution.py:395
  5.9 1.2 %copy-start = (bf16[512,1024]{1,0:T(8,128)(2,1)S(1)}, bf16[512,1024]{1,0:T(8,128)(2,1)}, u32[]{:S(2)}) copy-start(bf16[512,1024]{1,0:T(8,128)(2,1)} %table_hbm.1) | copy-start | bytes 3145732
  7.1 0.7 copy-start.1
  11.4 10.9 %all-to-all-start.1 = ((bf16[8,16,1024]{2,1,0:T(8,128)(2,1)}), bf16[8,16,1024]{2,1,0:T(8,128)(2,1)S(1)}, u32[]{:S(2)}, u32[]{:S(2)}) async-start(bf16[8,16,1024]{2,1,0:T(8,128)(2,1)} %bitcast.7), calls=%async_computation.1 | async-start | bytes 524288 | tf_op jit(solution)/shard_map/all_to_all | solution.py:396
  39.9 2.2 %collective-permute-start = (bf16[320,1024]{1,0:T(8,128)(2,1)S(1)}, bf16[320,1024]{1,0:T(8,128)(2,1)S(1)}, u32[]{:S(2)}, u32[]{:S(2)}) collective-permute-start(bf16[320,1024]{1,0:T(8,128)(2,1)S(1)} %get-tuple-element.20), channel_id=1, source_target_pairs={{0,32},{32,0},{64,96},{96,64},{128,160},{160,128},{192,224},{224,1... | collective-permute-start | bytes 1966088 | tf_op jit(solution)/shard_map/ppermute | solution.py:434
  42.2 7.9 %collective-permute-start.1 = (bf16[64,1024]{1,0:T(8,128)(2,1)S(1)}, bf16[64,1024]{1,0:T(8,128)(2,1)S(1)}, u32[]{:S(2)}, u32[]{:S(2)}) collective-permute-start(bf16[64,1024]{1,0:T(8,128)(2,1)S(1)} %get-tuple-element.22), channel_id=1, source_target_pairs={{0,2},{1,3},{2,0},{3,1},{4,6},{5,7},{6,4},{7,5},{8,10},{9,11},{10,... | collective-permute-start | bytes 393224 | tf_op jit(solution)/shard_map/ppermute | solution.py:373
  44.4 7.8 %collective-permute-start.2 = (bf16[64,1024]{1,0:T(8,128)(2,1)S(1)}, bf16[64,1024]{1,0:T(8,128)(2,1)S(1)}, u32[]{:S(2)}, u32[]{:S(2)}) collective-permute-start(bf16[64,1024]{1,0:T(8,128)(2,1)S(1)} %get-tuple-element.23), channel_id=1, source_target_pairs={{0,1},{1,2},{2,3},{3,0},{4,5},{5,6},{6,7},{7,4},{8,9},{9,10},{10,1... | collective-permute-start | bytes 393224 | tf_op jit(solution)/shard_map/ppermute | solution.py:373
  44.8 7.4 %collective-permute-start.3 = (bf16[64,1024]{1,0:T(8,128)(2,1)S(1)}, bf16[64,1024]{1,0:T(8,128)(2,1)S(1)}, u32[]{:S(2)}, u32[]{:S(2)}) collective-permute-start(bf16[64,1024]{1,0:T(8,128)(2,1)S(1)} %get-tuple-element.24), channel_id=1, source_target_pairs={{0,3},{1,0},{2,1},{3,2},{4,7},{5,4},{6,5},{7,6},{8,11},{9,8},{10,9... | collective-permute-start | bytes 393224 | tf_op jit(solution)/shard_map/ppermute | solution.py:373
  46.5 8.5 %collective-permute-start.11 = (bf16[32,1024]{1,0:T(8,128)(2,1)S(1)}, bf16[32,1024]{1,0:T(8,128)(2,1)S(1)}, u32[]{:S(2)}, u32[]{:S(2)}) collective-permute-start(bf16[32,1024]{1,0:T(8,128)(2,1)S(1)} %get-tuple-element.26), channel_id=1, source_target_pairs={{0,64},{64,128},{128,192},{192,0},{32,96},{96,160},{160,224},{224,... | collective-permute-start | bytes 196616 | tf_op jit(solution)/shard_map/ppermute | solution.py:373
  47.1 7.9 %collective-permute-start.12 = (bf16[32,1024]{1,0:T(8,128)(2,1)S(1)}, bf16[32,1024]{1,0:T(8,128)(2,1)S(1)}, u32[]{:S(2)}, u32[]{:S(2)}) collective-permute-start(bf16[32,1024]{1,0:T(8,128)(2,1)S(1)} %get-tuple-element.27), channel_id=1, source_target_pairs={{0,128},{64,192},{128,0},{192,64},{32,160},{96,224},{160,32},{224,... | collective-permute-start | bytes 196616 | tf_op jit(solution)/shard_map/ppermute | solution.py:373
  50.2 4.8 %collective-permute-start.13 = (bf16[32,1024]{1,0:T(8,128)(2,1)S(1)}, bf16[32,1024]{1,0:T(8,128)(2,1)S(1)}, u32[]{:S(2)}, u32[]{:S(2)}) collective-permute-start(bf16[32,1024]{1,0:T(8,128)(2,1)S(1)} %get-tuple-element.28), channel_id=1, source_target_pairs={{0,192},{64,0},{128,64},{192,128},{32,224},{96,32},{160,96},{224,1... | collective-permute-start | bytes 196616 | tf_op jit(solution)/shard_map/ppermute | solution.py:373
  52.3 7.6 %collective-permute-start.4 = (bf16[32,1024]{1,0:T(8,128)(2,1)S(1)}, bf16[32,1024]{1,0:T(8,128)(2,1)S(1)}, u32[]{:S(2)}, u32[]{:S(2)}) collective-permute-start(bf16[32,1024]{1,0:T(8,128)(2,1)S(1)} %slice.41), channel_id=1, source_target_pairs={{0,4},{4,0},{8,12},{12,8},{16,20},{20,16},{24,28},{28,24},{1,5},{5... | collective-permute-start | bytes 196616 | tf_op jit(solution)/shard_map/ppermute | solution.py:449
  55.5 15.9 %collective-permute-start.14 = (bf16[128,1024]{1,0:T(8,128)(2,1)S(1)}, bf16[128,1024]{1,0:T(8,128)(2,1)S(1)}, u32[]{:S(2)}, u32[]{:S(2)}) collective-permute-start(bf16[128,1024]{1,0:T(8,128)(2,1)S(1)} %get-tuple-element.30), channel_id=1, source_target_pairs={{0,2},{1,3},{2,0},{3,1},{4,6},{5,7},{6,4},{7,5},{8,10},{9,11},{10,... | collective-permute-start | bytes 786440 | tf_op jit(solution)/shard_map/ppermute | solution.py:373
  57.9 13.4 %collective-permute-start.15 = (bf16[128,1024]{1,0:T(8,128)(2,1)S(1)}, bf16[128,1024]{1,0:T(8,128)(2,1)S(1)}, u32[]{:S(2)}, u32[]{:S(2)}) collective-permute-start(bf16[128,1024]{1,0:T(8,128)(2,1)S(1)} %get-tuple-element.31), channel_id=1, source_target_pairs={{0,1},{1,2},{2,3},{3,0},{4,5},{5,6},{6,7},{7,4},{8,9},{9,10},{10,1... | collective-permute-start | bytes 786440 | tf_op jit(solution)/shard_map/ppermute | solution.py:373
  58.2 13.1 %collective-permute-start.16 = (bf16[128,1024]{1,0:T(8,128)(2,1)S(1)}, bf16[128,1024]{1,0:T(8,128)(2,1)S(1)}, u32[]{:S(2)}, u32[]{:S(2)}) collective-permute-start(bf16[128,1024]{1,0:T(8,128)(2,1)S(1)} %get-tuple-element.32), channel_id=1, source_target_pairs={{0,3},{1,0},{2,1},{3,2},{4,7},{5,4},{6,5},{7,6},{8,11},{9,8},{10,9... | collective-permute-start | bytes 786440 | tf_op jit(solution)/shard_map/ppermute | solution.py:373
  60.0 5.3 %collective-permute-start.5 = (bf16[16,1024]{1,0:T(8,128)(2,1)S(1)}, bf16[16,1024]{1,0:T(8,128)(2,1)S(1)}, u32[]{:S(2)}, u32[]{:S(2)}) collective-permute-start(bf16[16,1024]{1,0:T(8,128)(2,1)S(1)} %slice.42), channel_id=1, source_target_pairs={{0,8},{4,12},{8,0},{12,4},{16,24},{20,28},{24,16},{28,20},{1,9},{5... | collective-permute-start | bytes 98312 | tf_op jit(solution)/shard_map/ppermute | solution.py:449
  65.3 13.7 %collective-permute-start.6 = (bf16[8,1024]{1,0:T(8,128)(2,1)S(1)}, bf16[8,1024]{1,0:T(8,128)(2,1)S(1)}, u32[]{:S(2)}, u32[]{:S(2)}) collective-permute-start(bf16[8,1024]{1,0:T(8,128)(2,1)S(1)} %slice.43), channel_id=1, source_target_pairs={{0,16},{4,20},{8,24},{12,28},{16,0},{20,4},{24,8},{28,12},{1,17},{... | collective-permute-start | bytes 49160 | tf_op jit(solution)/shard_map/ppermute | solution.py:449
  72.2 18.8 %all-to-all-start.2 = ((bf16[8,16,1024]{2,1,0:T(8,128)(2,1)}), bf16[8,16,1024]{2,1,0:T(8,128)(2,1)S(1)}, u32[]{:S(2)}, u32[]{:S(2)}) async-start(bf16[8,16,1024]{2,1,0:T(8,128)(2,1)} %bitcast.10), calls=%async_computation.2 | async-start | bytes 524288 | tf_op jit(solution)/shard_map/all_to_all | solution.py:452
  79.0 4.0 %collective-permute-start.9 = (f32[8,1024]{1,0:T(8,128)S(1)}, f32[8,1024]{1,0:T(8,128)S(1)}, u32[]{:S(2)}, u32[]{:S(2)}) collective-permute-start(f32[8,1024]{1,0:T(8,128)S(1)} %slice_add_fusion.2), channel_id=1, source_target_pairs={{0,192},{64,0},{128,64},{192,128},{32,224},{96,32},{160,96},{224,1... | collective-permute-start | bytes 98312 | tf_op jit(solution)/shard_map/ppermute | solution.py:373
  80.2 5.1 %collective-permute-start.8 = (f32[8,1024]{1,0:T(8,128)S(1)}, f32[8,1024]{1,0:T(8,128)S(1)}, u32[]{:S(2)}, u32[]{:S(2)}) collective-permute-start(f32[8,1024]{1,0:T(8,128)S(1)} %slice_add_fusion.2), channel_id=1, source_target_pairs={{0,64},{64,128},{128,192},{192,0},{32,96},{96,160},{160,224},{224,... | collective-permute-start | bytes 98312 | tf_op jit(solution)/shard_map/ppermute | solution.py:373
  81.1 5.4 %collective-permute-start.7 = (f32[8,1024]{1,0:T(8,128)S(1)}, f32[8,1024]{1,0:T(8,128)S(1)}, u32[]{:S(2)}, u32[]{:S(2)}) collective-permute-start(f32[8,1024]{1,0:T(8,128)S(1)} %slice_add_fusion.2), channel_id=1, source_target_pairs={{0,128},{64,192},{128,0},{192,64},{32,160},{96,224},{160,32},{224,... | collective-permute-start | bytes 98312 | tf_op jit(solution)/shard_map/ppermute | solution.py:373
  86.6 1.3 %collective-permute-start.10 = (f32[4,1,2,1024]{3,2,0,1:T(2,128)S(1)}, f32[4,1,2,1024]{3,2,0,1:T(2,128)S(1)}, u32[]{:S(2)}, u32[]{:S(2)}) collective-permute-start(f32[4,1,2,1024]{3,2,0,1:T(2,128)S(1)} %reshape.104), channel_id=1, source_target_pairs={{0,32},{32,0},{64,96},{96,64},{128,160},{160,128},{192,224},{224,1... | collective-permute-start | bytes 98312 | tf_op jit(solution)/shard_map/ppermute | solution.py:457

commit v7 on v6

--- a/solution.py
+++ b/solution.py
@@ -9,8 +9,8 @@
 
 
 EPS = 1e-06
-BLOCK = 128
-BACK = 2
+BLOCK = 256
+BACK = 1
 
 
 def sigmoid(values):

time: 92.2 us -> 90.8 us (0.985)
  Pallas kernels: 19.3 us -> 18 us
    pallas_call x1, Pallas kernels: 17.6 us -> 16.2 us  [layer(): pl.pallas_call(layer_kernel, out_shape=(jax.ShapeDtypeStruct((tokens, wid...]
where the time goes in v7:
time: 90.8 us; the launch traced here: 90.3 us
  starting transfers between devices  41.6 us (46%)
  waiting for transfers between devices  23.1 us (25%)
  Pallas kernels  18 us (20%)
  local copies, waits for them, and re-layouts  3.5 us (4%)
  other arithmetic  3.33 us (4%)
    pallas_call x1, Pallas kernels, layer(): pl.pallas_call(layer_kernel, out_shape=(jax.ShapeDtypeStruct((tokens, wid...  16.2 us
    ppermute x12, starting transfers between devices, exchange(): lax.ppermute(chunk, axis, shift(groups, k))  15.4 us
    ppermute x3, starting transfers between devices, on_device(): sent = lax.ppermute(hot_part[half:].astype(jnp.bfloat16), 'dp', pairs)  11.4 us
    all_to_all x1, starting transfers between devices, on_device(): lax.all_to_all(by_z, 'dp', split_axis=0, concat_axis=0, tiled=True, axis_...  6.75 us
    ppermute x12, waiting for transfers between devices, exchange(): lax.ppermute(chunk, axis, shift(groups, k))  6.66 us
    all_to_all x1, waiting for transfers between devices, on_device(): lax.all_to_all(pick_rows(wanted, bring(cold_table, cold_requests)).reshap...  6.52 us
    all_to_all x1, starting transfers between devices, on_device(): lax.all_to_all(cold_requests, 'table', split_axis=0, concat_axis=0, tiled...  4.48 us
    all_to_all x1, starting transfers between devices, on_device(): lax.all_to_all(pick_rows(wanted, bring(cold_table, cold_requests)).reshap...  3.41 us
  transfers between devices with their start and end apart: 20, of which 11 were waited for; matrix products, arithmetic and copies ran while one was open for 5% of the time, Pallas kernels for 1%

profile of v7, /device:TPU:2, one launch (start us, length us, event | category | flops | bytes accessed | tf_op | source)
XLA Modules:
  0.0 90.3 jit_solution(1808330223543626506)
XLA Ops:
  0.6 4.5 %all-to-all-start = ((s32[8,1,16]{2,1,0:T(1,128)}), s32[8,1,16]{2,1,0:T(1,128)S(1)}, u32[]{:S(2)}, u32[]{:S(2)}) async-start(s32[8,1,16]{2,1,0:T(1,128)} %bitcast.16), calls=%async_computation | async-start | bytes 8192 | tf_op jit(solution)/shard_map/all_to_all | solution.py:395
  5.9 1.2 %copy-done = bf16[512,1024]{1,0:T(8,128)(2,1)S(1)} copy-done((bf16[512,1024]{1,0:T(8,128)(2,1)S(1)}, bf16[512,1024]{1,0:T(8,128)(2,1)}, u32[]{:S(2)}) %copy-start) | copy-done | bytes 1048600
  7.9 2.4 %all-to-all-done = s32[8,1,16]{2,1,0:T(1,128)S(1)} async-done(((s32[8,1,16]{2,1,0:T(1,128)}), s32[8,1,16]{2,1,0:T(1,128)S(1)}, u32[]{:S(2)}, u32[]{:S(2)}) %all-to-all-start) | async-done | bytes 544 | tf_op jit(solution)/shard_map/all_to_all | solution.py:395
  11.4 3.4 %all-to-all-start.1 = ((bf16[8,16,1024]{2,1,0:T(8,128)(2,1)}), bf16[8,16,1024]{2,1,0:T(8,128)(2,1)S(1)}, u32[]{:S(2)}, u32[]{:S(2)}) async-start(bf16[8,16,1024]{2,1,0:T(8,128)(2,1)} %bitcast.7), calls=%async_computation.1 | async-start | bytes 524288 | tf_op jit(solution)/shard_map/all_to_all | solution.py:396
  15.8 6.5 %all-to-all-done.1 = bf16[8,16,1024]{2,1,0:T(8,128)(2,1)S(1)} async-done(((bf16[8,16,1024]{2,1,0:T(8,128)(2,1)}), bf16[8,16,1024]{2,1,0:T(8,128)(2,1)S(1)}, u32[]{:S(2)}, u32[]{:S(2)}) %all-to-all-start.1) | async-done | bytes 262176 | tf_op jit(solution)/shard_map/all_to_all | solution.py:396
  22.3 16.2 %layer.1 = (bf16[512,1024]{1,0:T(8,128)(2,1)}, bf16[320,1024]{1,0:T(8,128)(2,1)S(1)}, bf16[320,1024]{1,0:T(8,128)(2,1)S(1)}) custom-call(s32[1,8]{1,0:T(1,128)S(1)} %bitcast.18, s32[512,1]{1,0:T(8,128)S(1)} %copy.19.source_ref, s32[1,512]{1,0:T(1,128)S(1)} %bitcast.17, bf16[128,1024]{1,0:T(8,128)(2,1)S(1)} %bitcast.13, bf16[512,1024]{1,0:T(8,128)(2,1)} %hot_hbm.1, ...), custom_call_target="tpu_custom_call" | custom-call | flops 8000000000 | bytes 12000000 | tf_op jit(solution)/shard_map/layer/pallas_call | solution.py:272
  38.8 1.9 %collective-permute-done.got_ref = bf16[320,1024]{1,0:T(8,128)(2,1)S(1)} collective-permute-done((bf16[320,1024]{1,0:T(8,128)(2,1)S(1)}, bf16[320,1024]{1,0:T(8,128)(2,1)S(1)}, u32[]{:S(2)}, u32[]{:S(2)}) %collective-permute-start) | collective-permute-done | bytes 655392 | tf_op jit(solution)/shard_map/ppermute | solution.py:434
  40.9 2.2 %collective-permute-start.1 = (bf16[64,1024]{1,0:T(8,128)(2,1)S(1)}, bf16[64,1024]{1,0:T(8,128)(2,1)S(1)}, u32[]{:S(2)}, u32[]{:S(2)}) collective-permute-start(bf16[64,1024]{1,0:T(8,128)(2,1)S(1)} %get-tuple-element.22), channel_id=1, source_target_pairs={{0,2},{1,3},{2,0},{3,1},{4,6},{5,7},{6,4},{7,5},{8,10},{9,11},{10,... | collective-permute-start | bytes 393224 | tf_op jit(solution)/shard_map/ppermute | solution.py:373
  43.4 1.7 %collective-permute-start.3 = (bf16[64,1024]{1,0:T(8,128)(2,1)S(1)}, bf16[64,1024]{1,0:T(8,128)(2,1)S(1)}, u32[]{:S(2)}, u32[]{:S(2)}) collective-permute-start(bf16[64,1024]{1,0:T(8,128)(2,1)S(1)} %get-tuple-element.24), channel_id=1, source_target_pairs={{0,3},{1,0},{2,1},{3,2},{4,7},{5,4},{6,5},{7,6},{8,11},{9,8},{10,9... | collective-permute-start | bytes 393224 | tf_op jit(solution)/shard_map/ppermute | solution.py:373
  45.8 2.0 %collective-permute-start.12 = (bf16[32,1024]{1,0:T(8,128)(2,1)S(1)}, bf16[32,1024]{1,0:T(8,128)(2,1)S(1)}, u32[]{:S(2)}, u32[]{:S(2)}) collective-permute-start(bf16[32,1024]{1,0:T(8,128)(2,1)S(1)} %get-tuple-element.27), channel_id=1, source_target_pairs={{0,128},{64,192},{128,0},{192,64},{32,160},{96,224},{160,32},{224,... | collective-permute-start | bytes 196616 | tf_op jit(solution)/shard_map/ppermute | solution.py:373
  48.8 1.2 %collective-permute-start.13 = (bf16[32,1024]{1,0:T(8,128)(2,1)S(1)}, bf16[32,1024]{1,0:T(8,128)(2,1)S(1)}, u32[]{:S(2)}, u32[]{:S(2)}) collective-permute-start(bf16[32,1024]{1,0:T(8,128)(2,1)S(1)} %get-tuple-element.28), channel_id=1, source_target_pairs={{0,192},{64,0},{128,64},{192,128},{32,224},{96,32},{160,96},{224,1... | collective-permute-start | bytes 196616 | tf_op jit(solution)/shard_map/ppermute | solution.py:373
  51.0 2.0 %collective-permute-start.4 = (bf16[32,1024]{1,0:T(8,128)(2,1)S(1)}, bf16[32,1024]{1,0:T(8,128)(2,1)S(1)}, u32[]{:S(2)}, u32[]{:S(2)}) collective-permute-start(bf16[32,1024]{1,0:T(8,128)(2,1)S(1)} %slice.41), channel_id=1, source_target_pairs={{0,4},{4,0},{8,12},{12,8},{16,20},{20,16},{24,28},{28,24},{1,5},{5... | collective-permute-start | bytes 196616 | tf_op jit(solution)/shard_map/ppermute | solution.py:449
  54.1 2.5 %collective-permute-start.14 = (bf16[128,1024]{1,0:T(8,128)(2,1)S(1)}, bf16[128,1024]{1,0:T(8,128)(2,1)S(1)}, u32[]{:S(2)}, u32[]{:S(2)}) collective-permute-start(bf16[128,1024]{1,0:T(8,128)(2,1)S(1)} %get-tuple-element.30), channel_id=1, source_target_pairs={{0,2},{1,3},{2,0},{3,1},{4,6},{5,7},{6,4},{7,5},{8,10},{9,11},{10,... | collective-permute-start | bytes 786440 | tf_op jit(solution)/shard_map/ppermute | solution.py:373
  56.8 1.7 %collective-permute-start.16 = (bf16[128,1024]{1,0:T(8,128)(2,1)S(1)}, bf16[128,1024]{1,0:T(8,128)(2,1)S(1)}, u32[]{:S(2)}, u32[]{:S(2)}) collective-permute-start(bf16[128,1024]{1,0:T(8,128)(2,1)S(1)} %get-tuple-element.32), channel_id=1, source_target_pairs={{0,3},{1,0},{2,1},{3,2},{4,7},{5,4},{6,5},{7,6},{8,11},{9,8},{10,9... | collective-permute-start | bytes 786440 | tf_op jit(solution)/shard_map/ppermute | solution.py:373
  58.6 3.4 %collective-permute-start.5 = (bf16[16,1024]{1,0:T(8,128)(2,1)S(1)}, bf16[16,1024]{1,0:T(8,128)(2,1)S(1)}, u32[]{:S(2)}, u32[]{:S(2)}) collective-permute-start(bf16[16,1024]{1,0:T(8,128)(2,1)S(1)} %slice.42), channel_id=1, source_target_pairs={{0,8},{4,12},{8,0},{12,4},{16,24},{20,28},{24,16},{28,20},{1,9},{5... | collective-permute-start | bytes 98312 | tf_op jit(solution)/shard_map/ppermute | solution.py:449
  62.0 1.9 %collective-permute-done.5 = bf16[16,1024]{1,0:T(8,128)(2,1)S(1)} collective-permute-done((bf16[16,1024]{1,0:T(8,128)(2,1)S(1)}, bf16[16,1024]{1,0:T(8,128)(2,1)S(1)}, u32[]{:S(2)}, u32[]{:S(2)}) %collective-permute-start.5) | collective-permute-done | bytes 32800 | tf_op jit(solution)/shard_map/ppermute | solution.py:449
  63.9 6.1 %collective-permute-start.6 = (bf16[8,1024]{1,0:T(8,128)(2,1)S(1)}, bf16[8,1024]{1,0:T(8,128)(2,1)S(1)}, u32[]{:S(2)}, u32[]{:S(2)}) collective-permute-start(bf16[8,1024]{1,0:T(8,128)(2,1)S(1)} %slice.43), channel_id=1, source_target_pairs={{0,16},{4,20},{8,24},{12,28},{16,0},{20,4},{24,8},{28,12},{1,17},{... | collective-permute-start | bytes 49160 | tf_op jit(solution)/shard_map/ppermute | solution.py:449
  70.9 6.8 %all-to-all-start.2 = ((bf16[8,16,1024]{2,1,0:T(8,128)(2,1)}), bf16[8,16,1024]{2,1,0:T(8,128)(2,1)S(1)}, u32[]{:S(2)}, u32[]{:S(2)}) async-start(bf16[8,16,1024]{2,1,0:T(8,128)(2,1)} %bitcast.10), calls=%async_computation.2 | async-start | bytes 524288 | tf_op jit(solution)/shard_map/all_to_all | solution.py:452
  77.6 1.2 %collective-permute-start.9 = (f32[8,1024]{1,0:T(8,128)S(1)}, f32[8,1024]{1,0:T(8,128)S(1)}, u32[]{:S(2)}, u32[]{:S(2)}) collective-permute-start(f32[8,1024]{1,0:T(8,128)S(1)} %slice_add_fusion.2), channel_id=1, source_target_pairs={{0,192},{64,0},{128,64},{192,128},{32,224},{96,32},{160,96},{224,1... | collective-permute-start | bytes 98312 | tf_op jit(solution)/shard_map/ppermute | solution.py:373
  80.4 1.2 %collective-permute-done.9 = f32[8,1024]{1,0:T(8,128)S(1)} collective-permute-done((f32[8,1024]{1,0:T(8,128)S(1)}, f32[8,1024]{1,0:T(8,128)S(1)}, u32[]{:S(2)}, u32[]{:S(2)}) %collective-permute-start.9) | collective-permute-done | bytes 32800 | tf_op jit(solution)/shard_map/ppermute | solution.py:373
  81.6 2.4 %collective-permute-done.8 = f32[8,1024]{1,0:T(8,128)S(1)} collective-permute-done((f32[8,1024]{1,0:T(8,128)S(1)}, f32[8,1024]{1,0:T(8,128)S(1)}, u32[]{:S(2)}, u32[]{:S(2)}) %collective-permute-start.8) | collective-permute-done | bytes 32800 | tf_op jit(solution)/shard_map/ppermute | solution.py:373
  84.0 1.2 %collective-permute-done.7 = f32[8,1024]{1,0:T(8,128)S(1)} collective-permute-done((f32[8,1024]{1,0:T(8,128)S(1)}, f32[8,1024]{1,0:T(8,128)S(1)}, u32[]{:S(2)}, u32[]{:S(2)}) %collective-permute-start.7) | collective-permute-done | bytes 32800 | tf_op jit(solution)/shard_map/ppermute | solution.py:373
  85.3 1.2 %collective-permute-done.10 = f32[4,1,2,1024]{3,2,0,1:T(2,128)S(1)} collective-permute-done((f32[4,1,2,1024]{3,2,0,1:T(2,128)S(1)}, f32[4,1,2,1024]{3,2,0,1:T(2,128)S(1)}, u32[]{:S(2)}, u32[]{:S(2)}) %collective-permute-start.10) | collective-permute-done | bytes 32800 | tf_op jit(solution)/shard_map/ppermute | solution.py:457
  87.2 2.5 %all-to-all-done.2 = bf16[8,16,1024]{2,1,0:T(8,128)(2,1)S(1)} async-done(((bf16[8,16,1024]{2,1,0:T(8,128)(2,1)}), bf16[8,16,1024]{2,1,0:T(8,128)(2,1)S(1)}, u32[]{:S(2)}, u32[]{:S(2)}) %all-to-all-start.2) | async-done | bytes 262176 | tf_op jit(solution)/shard_map/all_to_all | solution.py:452
  (54 shorter events, 12.4 us)
Async XLA Ops:
  0.6 15.1 %copy-start.2 = (s32[1,8]{1,0:T(1,128)S(1)}, s32[1,8]{1,0:T(1,128)}, u32[]{:S(2)}) copy-start(s32[1,8]{1,0:T(1,128)} %param.13) | copy-start | bytes 100
  0.6 9.7 %all-to-all-start = ((s32[8,1,16]{2,1,0:T(1,128)}), s32[8,1,16]{2,1,0:T(1,128)S(1)}, u32[]{:S(2)}, u32[]{:S(2)}) async-start(s32[8,1,16]{2,1,0:T(1,128)} %bitcast.16), calls=%async_computation | async-start | bytes 8192 | tf_op jit(solution)/shard_map/all_to_all | solution.py:395
  5.9 1.2 %copy-start = (bf16[512,1024]{1,0:T(8,128)(2,1)S(1)}, bf16[512,1024]{1,0:T(8,128)(2,1)}, u32[]{:S(2)}) copy-start(bf16[512,1024]{1,0:T(8,128)(2,1)} %table_hbm.1) | copy-start | bytes 3145732
  7.1 0.7 copy-start.1
  11.4 10.9 %all-to-all-start.1 = ((bf16[8,16,1024]{2,1,0:T(8,128)(2,1)}), bf16[8,16,1024]{2,1,0:T(8,128)(2,1)S(1)}, u32[]{:S(2)}, u32[]{:S(2)}) async-start(bf16[8,16,1024]{2,1,0:T(8,128)(2,1)} %bitcast.7), calls=%async_computation.1 | async-start | bytes 524288 | tf_op jit(solution)/shard_map/all_to_all | solution.py:396
  38.5 2.2 %collective-permute-start = (bf16[320,1024]{1,0:T(8,128)(2,1)S(1)}, bf16[320,1024]{1,0:T(8,128)(2,1)S(1)}, u32[]{:S(2)}, u32[]{:S(2)}) collective-permute-start(bf16[320,1024]{1,0:T(8,128)(2,1)S(1)} %get-tuple-element.20), channel_id=1, source_target_pairs={{0,32},{32,0},{64,96},{96,64},{128,160},{160,128},{192,224},{224,1... | collective-permute-start | bytes 1966088 | tf_op jit(solution)/shard_map/ppermute | solution.py:434
  40.9 7.9 %collective-permute-start.1 = (bf16[64,1024]{1,0:T(8,128)(2,1)S(1)}, bf16[64,1024]{1,0:T(8,128)(2,1)S(1)}, u32[]{:S(2)}, u32[]{:S(2)}) collective-permute-start(bf16[64,1024]{1,0:T(8,128)(2,1)S(1)} %get-tuple-element.22), channel_id=1, source_target_pairs={{0,2},{1,3},{2,0},{3,1},{4,6},{5,7},{6,4},{7,5},{8,10},{9,11},{10,... | collective-permute-start | bytes 393224 | tf_op jit(solution)/shard_map/ppermute | solution.py:373
  43.1 7.8 %collective-permute-start.2 = (bf16[64,1024]{1,0:T(8,128)(2,1)S(1)}, bf16[64,1024]{1,0:T(8,128)(2,1)S(1)}, u32[]{:S(2)}, u32[]{:S(2)}) collective-permute-start(bf16[64,1024]{1,0:T(8,128)(2,1)S(1)} %get-tuple-element.23), channel_id=1, source_target_pairs={{0,1},{1,2},{2,3},{3,0},{4,5},{5,6},{6,7},{7,4},{8,9},{9,10},{10,1... | collective-permute-start | bytes 393224 | tf_op jit(solution)/shard_map/ppermute | solution.py:373
  43.4 7.4 %collective-permute-start.3 = (bf16[64,1024]{1,0:T(8,128)(2,1)S(1)}, bf16[64,1024]{1,0:T(8,128)(2,1)S(1)}, u32[]{:S(2)}, u32[]{:S(2)}) collective-permute-start(bf16[64,1024]{1,0:T(8,128)(2,1)S(1)} %get-tuple-element.24), channel_id=1, source_target_pairs={{0,3},{1,0},{2,1},{3,2},{4,7},{5,4},{6,5},{7,6},{8,11},{9,8},{10,9... | collective-permute-start | bytes 393224 | tf_op jit(solution)/shard_map/ppermute | solution.py:373
  45.1 8.5 %collective-permute-start.11 = (bf16[32,1024]{1,0:T(8,128)(2,1)S(1)}, bf16[32,1024]{1,0:T(8,128)(2,1)S(1)}, u32[]{:S(2)}, u32[]{:S(2)}) collective-permute-start(bf16[32,1024]{1,0:T(8,128)(2,1)S(1)} %get-tuple-element.26), channel_id=1, source_target_pairs={{0,64},{64,128},{128,192},{192,0},{32,96},{96,160},{160,224},{224,... | collective-permute-start | bytes 196616 | tf_op jit(solution)/shard_map/ppermute | solution.py:373
  45.8 7.9 %collective-permute-start.12 = (bf16[32,1024]{1,0:T(8,128)(2,1)S(1)}, bf16[32,1024]{1,0:T(8,128)(2,1)S(1)}, u32[]{:S(2)}, u32[]{:S(2)}) collective-permute-start(bf16[32,1024]{1,0:T(8,128)(2,1)S(1)} %get-tuple-element.27), channel_id=1, source_target_pairs={{0,128},{64,192},{128,0},{192,64},{32,160},{96,224},{160,32},{224,... | collective-permute-start | bytes 196616 | tf_op jit(solution)/shard_map/ppermute | solution.py:373
  48.8 4.8 %collective-permute-start.13 = (bf16[32,1024]{1,0:T(8,128)(2,1)S(1)}, bf16[32,1024]{1,0:T(8,128)(2,1)S(1)}, u32[]{:S(2)}, u32[]{:S(2)}) collective-permute-start(bf16[32,1024]{1,0:T(8,128)(2,1)S(1)} %get-tuple-element.28), channel_id=1, source_target_pairs={{0,192},{64,0},{128,64},{192,128},{32,224},{96,32},{160,96},{224,1... | collective-permute-start | bytes 196616 | tf_op jit(solution)/shard_map/ppermute | solution.py:373
  51.0 7.6 %collective-permute-start.4 = (bf16[32,1024]{1,0:T(8,128)(2,1)S(1)}, bf16[32,1024]{1,0:T(8,128)(2,1)S(1)}, u32[]{:S(2)}, u32[]{:S(2)}) collective-permute-start(bf16[32,1024]{1,0:T(8,128)(2,1)S(1)} %slice.41), channel_id=1, source_target_pairs={{0,4},{4,0},{8,12},{12,8},{16,20},{20,16},{24,28},{28,24},{1,5},{5... | collective-permute-start | bytes 196616 | tf_op jit(solution)/shard_map/ppermute | solution.py:449
  54.1 15.9 %collective-permute-start.14 = (bf16[128,1024]{1,0:T(8,128)(2,1)S(1)}, bf16[128,1024]{1,0:T(8,128)(2,1)S(1)}, u32[]{:S(2)}, u32[]{:S(2)}) collective-permute-start(bf16[128,1024]{1,0:T(8,128)(2,1)S(1)} %get-tuple-element.30), channel_id=1, source_target_pairs={{0,2},{1,3},{2,0},{3,1},{4,6},{5,7},{6,4},{7,5},{8,10},{9,11},{10,... | collective-permute-start | bytes 786440 | tf_op jit(solution)/shard_map/ppermute | solution.py:373
  56.5 13.4 %collective-permute-start.15 = (bf16[128,1024]{1,0:T(8,128)(2,1)S(1)}, bf16[128,1024]{1,0:T(8,128)(2,1)S(1)}, u32[]{:S(2)}, u32[]{:S(2)}) collective-permute-start(bf16[128,1024]{1,0:T(8,128)(2,1)S(1)} %get-tuple-element.31), channel_id=1, source_target_pairs={{0,1},{1,2},{2,3},{3,0},{4,5},{5,6},{6,7},{7,4},{8,9},{9,10},{10,1... | collective-permute-start | bytes 786440 | tf_op jit(solution)/shard_map/ppermute | solution.py:373
  56.8 13.1 %collective-permute-start.16 = (bf16[128,1024]{1,0:T(8,128)(2,1)S(1)}, bf16[128,1024]{1,0:T(8,128)(2,1)S(1)}, u32[]{:S(2)}, u32[]{:S(2)}) collective-permute-start(bf16[128,1024]{1,0:T(8,128)(2,1)S(1)} %get-tuple-element.32), channel_id=1, source_target_pairs={{0,3},{1,0},{2,1},{3,2},{4,7},{5,4},{6,5},{7,6},{8,11},{9,8},{10,9... | collective-permute-start | bytes 786440 | tf_op jit(solution)/shard_map/ppermute | solution.py:373
  58.6 5.3 %collective-permute-start.5 = (bf16[16,1024]{1,0:T(8,128)(2,1)S(1)}, bf16[16,1024]{1,0:T(8,128)(2,1)S(1)}, u32[]{:S(2)}, u32[]{:S(2)}) collective-permute-start(bf16[16,1024]{1,0:T(8,128)(2,1)S(1)} %slice.42), channel_id=1, source_target_pairs={{0,8},{4,12},{8,0},{12,4},{16,24},{20,28},{24,16},{28,20},{1,9},{5... | collective-permute-start | bytes 98312 | tf_op jit(solution)/shard_map/ppermute | solution.py:449
  63.9 13.7 %collective-permute-start.6 = (bf16[8,1024]{1,0:T(8,128)(2,1)S(1)}, bf16[8,1024]{1,0:T(8,128)(2,1)S(1)}, u32[]{:S(2)}, u32[]{:S(2)}) collective-permute-start(bf16[8,1024]{1,0:T(8,128)(2,1)S(1)} %slice.43), channel_id=1, source_target_pairs={{0,16},{4,20},{8,24},{12,28},{16,0},{20,4},{24,8},{28,12},{1,17},{... | collective-permute-start | bytes 49160 | tf_op jit(solution)/shard_map/ppermute | solution.py:449
  70.9 18.8 %all-to-all-start.2 = ((bf16[8,16,1024]{2,1,0:T(8,128)(2,1)}), bf16[8,16,1024]{2,1,0:T(8,128)(2,1)S(1)}, u32[]{:S(2)}, u32[]{:S(2)}) async-start(bf16[8,16,1024]{2,1,0:T(8,128)(2,1)} %bitcast.10), calls=%async_computation.2 | async-start | bytes 524288 | tf_op jit(solution)/shard_map/all_to_all | solution.py:452
  77.6 4.0 %collective-permute-start.9 = (f32[8,1024]{1,0:T(8,128)S(1)}, f32[8,1024]{1,0:T(8,128)S(1)}, u32[]{:S(2)}, u32[]{:S(2)}) collective-permute-start(f32[8,1024]{1,0:T(8,128)S(1)} %slice_add_fusion.2), channel_id=1, source_target_pairs={{0,192},{64,0},{128,64},{192,128},{32,224},{96,32},{160,96},{224,1... | collective-permute-start | bytes 98312 | tf_op jit(solution)/shard_map/ppermute | solution.py:373
  78.9 5.1 %collective-permute-start.8 = (f32[8,1024]{1,0:T(8,128)S(1)}, f32[8,1024]{1,0:T(8,128)S(1)}, u32[]{:S(2)}, u32[]{:S(2)}) collective-permute-start(f32[8,1024]{1,0:T(8,128)S(1)} %slice_add_fusion.2), channel_id=1, source_target_pairs={{0,64},{64,128},{128,192},{192,0},{32,96},{96,160},{160,224},{224,... | collective-permute-start | bytes 98312 | tf_op jit(solution)/shard_map/ppermute | solution.py:373
  79.7 5.4 %collective-permute-start.7 = (f32[8,1024]{1,0:T(8,128)S(1)}, f32[8,1024]{1,0:T(8,128)S(1)}, u32[]{:S(2)}, u32[]{:S(2)}) collective-permute-start(f32[8,1024]{1,0:T(8,128)S(1)} %slice_add_fusion.2), channel_id=1, source_target_pairs={{0,128},{64,192},{128,0},{192,64},{32,160},{96,224},{160,32},{224,... | collective-permute-start | bytes 98312 | tf_op jit(solution)/shard_map/ppermute | solution.py:373
  85.2 1.3 %collective-permute-start.10 = (f32[4,1,2,1024]{3,2,0,1:T(2,128)S(1)}, f32[4,1,2,1024]{3,2,0,1:T(2,128)S(1)}, u32[]{:S(2)}, u32[]{:S(2)}) collective-permute-start(f32[4,1,2,1024]{3,2,0,1:T(2,128)S(1)} %reshape.104), channel_id=1, source_target_pairs={{0,32},{32,0},{64,96},{96,64},{128,160},{160,128},{192,224},{224,1... | collective-permute-start | bytes 98312 | tf_op jit(solution)/shard_map/ppermute | solution.py:457
